TPU v7x, 32 devices: a whole 2x2x4 slice. The times are simulated.
32 devices in a mesh: groups: 2 (over y), dp: 2 (over core), tensor: 8 (over z, x).
Axes of the slice: x: 2, y: 2, z: 4, core: 2. Of those that a mesh axis runs over, the one named last changes fastest.
Arguments:
- train_acts: bfloat16 [28672, 16384], P('tensor', ('groups', 'dp')), parts along dimension 1, may hold values from -6 to 6
- train_grads: bfloat16 [8192, 16384], P('tensor', ('groups', 'dp')), parts along dimension 1, may hold values from -6 to 6
- query_acts: bfloat16 [28672, 16384], P('tensor', ('groups', 'dp')), parts along dimension 1, may hold values from -6 to 6
- query_grads: bfloat16 [8192, 16384], P('tensor', ('groups', 'dp')), parts along dimension 1, may hold values from -6 to 6
- basis_in: bfloat16 [64, 28672], P(None, 'tensor'), may hold values from -0.03125 to 0.03125
- basis_out: bfloat16 [64, 8192], P(None, 'tensor'), may hold values from -0.0625 to 0.0625
- train_slots: int32 [16384], P(('groups', 'dp')), parts along dimension 0, may hold values from 0 to 7, as said below
- query_slots: int32 [16384], P(('groups', 'dp')), parts along dimension 0, may hold values from 0 to 7, as said below
Outputs:
- scores: float32 [256, 128], P(('groups', 'dp')), parts along dimension 0
There are 2 independent parts, one for each index of `groups`. A program takes and returns all parts, laid end to end along the dimension named above; an argument that names none is the same for every part. Nothing has to cross between parts.
Inputs may be any that keep to these rules, and one draw needn't show every extreme that they name: `train_slots`: within each aligned block of 512 tokens the slots never fall; the first token of a block has slot 0 and the last has slot 7; some slots may be empty. `query_slots`: same structure as train_slots.
All inputs are finite; a program needn't handle non-finite values.
Results may differ from a plain program's by a relative error of at most 0.0003.
Values sent between devices are 32-bit elements; how exact they have to be, the bound alone decides.
No kernel may reach another device: no remote copies, remote signals or barrier semaphores. Data moves between devices by JAX's collectives and lax.ppermute only.
A program may use at most 192 MiB of HBM per device.

v0:
```python
import jax
import jax.numpy as jnp
from jax import lax
from jax.sharding import PartitionSpec as P

RANK = 64
BLK = 512
SEGS = 8


def example_grads(proj_out, proj_in, slot_ids):
    num_blocks = slot_ids.shape[0] // BLK
    output_block_list = proj_out.reshape(RANK, num_blocks, BLK)
    in_blocks = proj_in.reshape(RANK, num_blocks, BLK)
    onehot = (
        slot_ids.reshape(num_blocks, BLK)[:, :, None]
        == jnp.arange(SEGS, dtype=jnp.int32)[None, None, :]
    ).astype(jnp.float32)
    counts = jnp.maximum(jnp.sum(onehot, axis=1), 1.0)
    weighted_rows = in_blocks[:, :, :, None] * onehot[None]
    summed_total = jnp.einsum(
        "zij,cijd->idzc", output_block_list, weighted_rows, precision=lax.Precision.HIGHEST
    )
    summed_total = summed_total / counts[:, :, None, None]
    return summed_total.reshape(num_blocks * SEGS, RANK * RANK)


def on_device(
    train_acts, train_grads, query_acts, query_grads, basis_in, basis_out, train_slots, query_slots
):
    partial_train_input = jnp.dot(basis_in, train_acts, preferred_element_type=jnp.float32)
    part_tout = jnp.dot(basis_out, train_grads, preferred_element_type=jnp.float32)
    part_qin = jnp.dot(basis_in, query_acts, preferred_element_type=jnp.float32)
    part_qout = jnp.dot(basis_out, query_grads, preferred_element_type=jnp.float32)
    train_in, training_output, query_in, query_out = lax.psum(
        (partial_train_input, part_tout, part_qin, part_qout), "tensor"
    )
    train_ex = example_grads(training_output, train_in, train_slots)
    query_ex = example_grads(query_out, query_in, query_slots)
    return jnp.dot(
        train_ex,
        lax.all_gather(query_ex, "dp", axis=0, tiled=True).T,
        precision=lax.Precision.HIGHEST,
        preferred_element_type=jnp.float32,
    )


def solution(mesh):
    placed = (
        P("tensor", ("groups", "dp")),
        P("tensor", ("groups", "dp")),
        P("tensor", ("groups", "dp")),
        P("tensor", ("groups", "dp")),
        P(None, "tensor"),
        P(None, "tensor"),
        P(("groups", "dp")),
        P(("groups", "dp")),
    )
    return jax.shard_map(
        on_device, mesh=mesh, in_specs=placed, out_specs=P(("groups", "dp"), None), check_vma=False
    )
```

profile of v0, /device:TPU:0, one launch (start us, length us, event | category | flops | bytes accessed | tf_op | source)
XLA Modules:
  0.0 245.9 jit_solution(13019114838287432492)
XLA Ops:
  6.5 0.0 copy-start
  6.5 0.0 copy-start.3
  6.5 0.0 all-reduce.3.cloned.1.call-start
  6.5 0.0 copy-start.2
  6.5 5.2 %fusion.25 = f32[64,4096]{1,0:T(8,128)S(1)} fusion(bf16[64,1024]{1,0:T(8,128)(2,1)} %param.13, bf16[1024,4096]{1,0:T(8,128)(2,1)} %param.11), kind=kOutput, calls=%fused_computation.25 | convolution fusion | flops 536870912 | bytes 9568256 | tf_op jit(solution)/shard_map/dot_general | solution.py:34
  11.7 0.0 copy-done.3
  11.7 0.8 copy-done.2
  12.5 1.6 fusion.23
  14.1 0.0 copy-done
  14.1 12.0 %fusion.22 = f32[64,4096]{1,0:T(8,128)S(1)} fusion(bf16[64,3584]{1,0:T(8,128)(2,1)S(1)} %copy-done, bf16[3584,4096]{1,0:T(8,128)(2,1)} %param.8), kind=kOutput, calls=%fused_computation.22 | convolution fusion | flops 1879048192 | bytes 30867456 | tf_op jit(solution)/shard_map/dot_general | solution.py:31
  26.1 1.6 copy.23
  27.7 12.0 %fusion.24 = f32[64,4096]{1,0:T(8,128)S(1)} fusion(bf16[64,3584]{1,0:T(8,128)(2,1)S(1)} %copy-done, bf16[3584,4096]{1,0:T(8,128)(2,1)} %param.10), kind=kOutput, calls=%fused_computation.24 | convolution fusion | flops 1879048192 | bytes 30867456 | tf_op jit(solution)/shard_map/dot_general | solution.py:33
  39.8 0.0 copy-start.4
  39.8 1.6 copy.24
  41.4 1.5 copy_bitcast_fusion
  42.9 0.0 all-reduce.3.cloned.1.call-update
  42.9 0.2 all-gather.2.cloned.1.call-start
  43.2 0.0 copy-done.4
  43.2 0.1 fusion.20
  43.3 159.9 %all-reduce.3.cloned.1.call-done = (f32[64,8,512]{2,0,1:T(8,128)}, f32[64,8,512]{2,1,0:T(8,128)}, f32[64,8,512]{2,0,1:T(8,128)}, f32[64,8,512]{2,1,0:T(8,128)}) async-done(((f32[64,8,512]{2,0,1:T(8,128)}, f32[64,8,512]{2,1,0:T(8,128)}, f32[64,8,512]{2,0,1:T(8,128)}, f32[64,8,512]{2,1,0:T(8,128)}), (f32[64,8,512]{2,0,1:T(8,128)}, f32[64,8,512]{2,1,0:T(8,128)}, f32[64,8,512]{2,0,1:T(8,128)}, ...) | async-done | bytes 4194320 | tf_op jit(solution)/shard_map/psum | solution.py:35
  203.2 1.8 copy.16
  205.1 0.0 copy-start.5
  205.1 10.0 %divide_bitcast_fusion = f32[8,8,64,64]{2,1,3,0:T(8,128)} fusion(f32[8,8]{1,0:T(8,128)S(1)} %broadcast_maximum_fusion, f32[64,8,512]{2,0,1:T(8,128)} %get-tuple-element.7, f32[8,512,8]{1,2,0:T(8,128)S(1)} %fusion.19, f32[64,8,512]{2,0,1:T(8,128)S(1)} %copy.16), kind=kOutput, calls=%fused_computation.8 | convolution fusion | flops 1612972032 | bytes 3277056 | tf_op jit(solution)/shard_map/zij,cijd->idzc/dot_general | solution.py:21
  215.0 1.9 copy.18
  217.0 1.7 reshape.33
  218.6 0.0 all-gather.2.cloned.1.call-update
  218.6 0.0 copy-done.5
  218.7 0.1 fusion.21
  218.8 1.8 copy.13
  220.6 0.0 copy-start.1
  220.6 10.0 %divide_bitcast_fusion.1 = f32[8,8,64,64]{2,1,3,0:T(8,128)} fusion(f32[8,8]{1,0:T(8,128)S(1)} %broadcast_maximum_fusion.1, f32[64,8,512]{2,0,1:T(8,128)} %get-tuple-element.5, f32[8,512,8]{1,2,0:T(8,128)S(1)} %fusion.18, f32[64,8,512]{2,0,1:T(8,128)S(1)} %copy.13), kind=kOutput, calls=%fused_computation.9 | convolution fusion | flops 1612972032 | bytes 3277056 | tf_op jit(solution)/shard_map/zij,cijd->idzc/dot_general | solution.py:21
  230.6 1.9 copy.15
  232.5 1.7 reshape.31
  234.2 0.0 all-gather.2.cloned.1.call-done
  234.2 4.8 %fusion.26 = f32[64,128]{1,0:T(8,128)} fusion(f32[64,4096]{1,0:T(8,128)} %reshape.31, f32[128,4096]{1,0:T(8,128)} %all-gather.2.cloned.1.call-done), kind=kOutput, calls=%fused_computation.26 | convolution fusion | flops 402653184 | bytes 3178496 | tf_op jit(solution)/shard_map/dot_general | solution.py:40
  239.0 0.0 copy-done.1
  (6 shorter events, 0.0 us)
Async XLA Ops:
  6.5 7.5 %copy-start = (bf16[64,3584]{1,0:T(8,128)(2,1)S(1)}, bf16[64,3584]{1,0:T(8,128)(2,1)}, u32[]{:S(2)}) copy-start(bf16[64,3584]{1,0:T(8,128)(2,1)} %param.12) | copy-start | bytes 1376260
  6.5 5.2 %copy-start.3 = (bf16[64,1024]{1,0:T(8,128)(2,1)S(1)}, bf16[64,1024]{1,0:T(8,128)(2,1)}, u32[]{:S(2)}) copy-start(bf16[64,1024]{1,0:T(8,128)(2,1)} %param.13) | copy-start | bytes 393220
  6.5 196.7 %all-reduce.3.cloned.1.call-start = ((), (), s32[]{:S(2)}) async-start(), calls=%async_computation.1 | async-start | bytes 8388608 | tf_op jit(solution)/shard_map/psum | solution.py:35
  6.5 6.0 %copy-start.2 = (bf16[1024,4096]{1,0:T(8,128)(2,1)S(1)}, bf16[1024,4096]{1,0:T(8,128)(2,1)}, u32[]{:S(2)}) copy-start(bf16[1024,4096]{1,0:T(8,128)(2,1)} %param.9) | copy-start | bytes 25165828
  39.8 3.4 %copy-start.4 = (s32[4096]{0:T(1024)S(1)}, s32[4096]{0:T(1024)}, u32[]{:S(2)}) copy-start(s32[4096]{0:T(1024)} %param.15) | copy-start | bytes 49156
  42.9 191.2 %all-gather.2.cloned.1.call-start = ((), (), s32[]{:S(2)}) async-start(), calls=%async_computation | async-start | bytes 3145728 | tf_op jit(solution)/shard_map/all_gather | solution.py:42
  205.1 13.6 %copy-start.5 = (s32[4096]{0:T(1024)S(1)}, s32[4096]{0:T(1024)}, u32[]{:S(2)}) copy-start(s32[4096]{0:T(1024)} %param.14) | copy-start | bytes 49156
  220.6 18.4 %copy-start.1 = (bf16[64,3584]{1,0:T(8,128)(2,1)S(1)}, bf16[64,3584]{1,0:T(8,128)(2,1)}, u32[]{:S(2)}) copy-start(bf16[64,3584]{1,0:T(8,128)(2,1)} %param.12) | copy-start | bytes 1376260
Sparse Core Ops, SparseCore 0:
  43.1 160.1 all-reduce.2
  218.8 9.4 all-gather.1
where the time goes:
time: 246 us
  waiting for transfers between devices  160 us (65%)
  matrix products  55.5 us (23%)
  local copies, waits for them, and re-layouts  16.4 us (7%)
  between operations  13.5 us (5%)
    psum x1, waiting for transfers between devices, on_device(): lax.psum((partial_train_input, part_tout, part_qin, part_qout), 'tensor')  160 us
    dot_general x2, matrix products, example_grads(): jnp.einsum('zij,cijd->idzc', output_block_list, weighted_rows, precision=...  19.9 us
    dot_general x1, matrix products, on_device(): jnp.dot(basis_in, train_acts, preferred_element_type=jnp.float32)  12 us
    dot_general x1, matrix products, on_device(): part_qin = jnp.dot(basis_in, query_acts, preferred_element_type=jnp.float32)  12 us
    dot_general x1, matrix products, on_device(): jnp.dot(basis_out, query_grads, preferred_element_type=jnp.float32)  5.16 us
  transfers between devices with their start and end apart: 2, of which 1 were waited for; matrix products, arithmetic and copies ran while one was open for 6% of the time, Pallas kernels for 0%

commit v1 on v0

v1 whole, which is shorter than its diff:
```python
import jax
import jax.numpy as jnp
from jax import lax
from jax.experimental import pallas as pl
from jax.experimental.pallas import tpu as pltpu
from jax.sharding import PartitionSpec as P

RANK = 64
BLK = 512
SEGS = 8
HALF = RANK // 2
X, Z1, Z2 = 1, 2, 4
X_FIRST = (0, Z2, Z1, Z1 | Z2, X, X | Z2, X | Z1, X | Z1 | Z2)
Z_FIRST = (0, Z2, X, X | Z2, Z1, Z1 | Z2, Z1 | X, X | Z1 | Z2)
VMEM = 56 * 1024 * 1024


def example_grads(proj_out, proj_in, slot_ids):
    num_blocks = slot_ids.shape[0] // BLK
    output_block_list = proj_out.reshape(RANK, num_blocks, BLK)
    in_blocks = proj_in.reshape(RANK, num_blocks, BLK)
    onehot = (
        slot_ids.reshape(num_blocks, BLK)[:, :, None]
        == jnp.arange(SEGS, dtype=jnp.int32)[None, None, :]
    ).astype(jnp.float32)
    counts = jnp.maximum(jnp.sum(onehot, axis=1), 1.0)
    weighted_rows = in_blocks[:, :, :, None] * onehot[None]
    summed_total = jnp.einsum(
        "zij,cijd->idzc", output_block_list, weighted_rows, precision=lax.Precision.HIGHEST
    )
    summed_total = summed_total / counts[:, :, None, None]
    return summed_total.reshape(num_blocks * SEGS, RANK * RANK)


def any_mesh(
    train_acts, train_grads, query_acts, query_grads, basis_in, basis_out, train_slots, query_slots
):
    sums = lax.psum(
        tuple(
            jnp.dot(basis, data, preferred_element_type=jnp.float32)
            for basis, data in (
                (basis_in, train_acts),
                (basis_out, train_grads),
                (basis_in, query_acts),
                (basis_out, query_grads),
            )
        ),
        "tensor",
    )
    train_ex = example_grads(sums[1], sums[0], train_slots)
    query_ex = example_grads(sums[3], sums[2], query_slots)
    return jnp.dot(
        train_ex,
        lax.all_gather(query_ex, "dp", axis=0, tiled=True).T,
        precision=lax.Precision.HIGHEST,
        preferred_element_type=jnp.float32,
    )


def project(me, jobs):
    count = len(jobs)
    masks = [job[2] for job in jobs]

    def kernel(me_ref, *refs):
        bases, datas = refs[:count], refs[count : 2 * count]
        outs = refs[2 * count : 3 * count]
        held = refs[3 * count : 4 * count]
        slots = refs[4 * count : 5 * count]
        made = refs[5 * count : 6 * count]
        basis_sem, in_sem, out_sem = refs[6 * count :]
        here = me_ref[0]
        steps = []
        for n in range(count):
            first = pltpu.make_async_copy(bases[n], held[n], basis_sem.at[n])
            first.start()
            for i, mask in enumerate(masks[n]):
                at = pl.multiple_of((here ^ mask) * BLK, BLK)
                copy = pltpu.make_async_copy(
                    datas[n].at[:, pl.ds(at, BLK)], slots[n].at[i], in_sem.at[len(steps)]
                )
                copy.start()
                steps.append((n, i, first if i == 0 else None, copy))
        ends = []
        for step, (n, i, first, copy) in enumerate(steps):
            if first is not None:
                first.wait()
            copy.wait()
            made[n][i] = jnp.dot(held[n][...], slots[n][i], preferred_element_type=jnp.float32)
            end = pltpu.make_async_copy(made[n].at[i], outs[n].at[i], out_sem.at[step])
            end.start()
            ends.append(end)
        for end in ends:
            end.wait()

    total = sum(len(m) for m in masks)
    moved = sum(len(m) * job[1].shape[0] * BLK * 2 for job, m in zip(jobs, masks))
    return pl.pallas_call(
        kernel,
        out_shape=[jax.ShapeDtypeStruct((len(m), RANK, BLK), jnp.float32) for m in masks],
        in_specs=[pl.BlockSpec(memory_space=pltpu.SMEM)] + [pl.BlockSpec(memory_space=pl.ANY)] * (2 * count),
        out_specs=[pl.BlockSpec(memory_space=pl.ANY)] * count,
        scratch_shapes=[pltpu.VMEM(job[0].shape, jnp.bfloat16) for job in jobs]
        + [pltpu.VMEM((len(m), job[1].shape[0], BLK), jnp.bfloat16) for job, m in zip(jobs, masks)]
        + [pltpu.VMEM((len(m), RANK, BLK), jnp.float32) for m in masks]
        + [
            pltpu.SemaphoreType.DMA((count,)),
            pltpu.SemaphoreType.DMA((total,)),
            pltpu.SemaphoreType.DMA((total,)),
        ],
        compiler_params=pltpu.CompilerParams(vmem_limit_bytes=VMEM),
        cost_estimate=pl.CostEstimate(flops=moved * RANK, bytes_accessed=moved, transcendentals=0),
    )(me, *[job[0] for job in jobs], *[job[1] for job in jobs])


def two(x):
    high = x.astype(jnp.bfloat16)
    return high, (x - high.astype(jnp.float32)).astype(jnp.bfloat16)


def rows_by_rows(a, b):
    def dot(p, q):
        return lax.dot_general(p, q, (((1,), (1,)), ((), ())), preferred_element_type=jnp.float32)

    return dot(a[0], b[0]) + (dot(a[0], b[1]) + dot(a[1], b[0]))


def examples(place, out_kept, out_got, in_kept, in_got, slots):
    def kernel(place_ref, out_a, out_b, in_a, in_b, slot_ref, ex_ref):
        z, me = place_ref[0], place_ref[1]
        out = out_a[0] + out_b[0]
        inner = in_a[0] + in_b[0]
        seg = lax.broadcasted_iota(jnp.int32, (SEGS, BLK), 0)
        mask = (slot_ref[me] == seg).astype(jnp.float32)
        counts = jnp.maximum(jnp.sum(mask, axis=1, keepdims=True), 1.0)
        none = jnp.zeros_like(inner)
        total = None
        for h, padded in enumerate(((inner, none), (none, inner))):
            rows = out[h * HALF : (h + 1) * HALF][:, None, :] * mask[None]
            part = rows_by_rows(
                two(rows.reshape(HALF * SEGS, BLK)), two(jnp.concatenate(padded, axis=0))
            )
            total = part if total is None else total + part
        ex = total.reshape(4, HALF // 4, SEGS, 2 * RANK) / counts[None, None]
        for g in range(4):
            ex_ref[g ^ z] = ex[g]

    blocks = slots.shape[0] // BLK
    return pl.pallas_call(
        kernel,
        out_shape=jax.ShapeDtypeStruct((4, HALF // 4, SEGS, 2 * RANK), jnp.float32),
        in_specs=[pl.BlockSpec(memory_space=pltpu.SMEM)] + [pl.BlockSpec(memory_space=pltpu.VMEM)] * 5,
        out_specs=pl.BlockSpec(memory_space=pltpu.VMEM),
    )(place, out_kept, out_got, in_kept, in_got, slots.reshape(blocks, 1, BLK))


def partial_scores(place, trains, queries):
    def kernel(place_ref, *refs):
        t_refs, q_refs = refs[:4], refs[4:6]
        out_ref, q_all, t_all = refs[6:]
        z, x, dp = place_ref[0], place_ref[2], place_ref[3]
        for k in range(4):
            t_all[k ^ z] = t_refs[k][...]
        for d in range(2):
            for i in range(8):
                q_all[(d ^ dp) * 8 + ((i % 4) ^ z) * 2 + ((i // 4) ^ x)] = q_refs[d][i]
        a2 = range(HALF // 4)
        train = jnp.concatenate([t_all[:, a].reshape(4 * SEGS, 2 * RANK) for a in a2], axis=1)
        query = jnp.concatenate([q_all[:, a].reshape(16 * SEGS, 2 * RANK) for a in a2], axis=1)
        scores = rows_by_rows(two(train), two(query))
        out_ref[...] = jnp.zeros_like(out_ref)
        for k in range(4):
            out_ref[pl.ds(pl.multiple_of((2 * k + x) * SEGS, SEGS), SEGS)] = scores[k * SEGS : (k + 1) * SEGS]

    return pl.pallas_call(
        kernel,
        out_shape=jax.ShapeDtypeStruct((8 * SEGS, 16 * SEGS), jnp.float32),
        in_specs=[pl.BlockSpec(memory_space=pltpu.SMEM)] + [pl.BlockSpec(memory_space=pltpu.VMEM)] * 6,
        out_specs=pl.BlockSpec(memory_space=pltpu.VMEM),
        scratch_shapes=[
            pltpu.VMEM((16, HALF // 4, SEGS, 2 * RANK), jnp.float32),
            pltpu.VMEM((4, HALF // 4, SEGS, 2 * RANK), jnp.float32),
        ],
    )(place, *trains, *queries)


def swap(value, mask):
    return lax.ppermute(value, "tensor", [(i, i ^ mask) for i in range(8)])


def halve(kept, got, mask):
    n = kept.shape[0] // 2
    sent = swap(kept[n:] + got[n:], mask)
    return kept[:n] + got[:n], sent


def eight(
    train_acts, train_grads, query_acts, query_grads, basis_in, basis_out, train_slots, query_slots
):
    tensor = lax.axis_index("tensor").astype(jnp.int32)
    me = tensor.reshape(1)
    place = jnp.stack([tensor // 2, tensor, tensor % 2, lax.axis_index("dp").astype(jnp.int32)])
    (qo_send,) = project(me, [(basis_out, query_grads, X_FIRST[4:])])
    qo_got = swap(qo_send, X)
    qi_send, qo_keep = project(
        me, [(basis_in, query_acts, X_FIRST[4:]), (basis_out, query_grads, X_FIRST[:4])]
    )
    qi_got = swap(qi_send, X)
    to_send, ti_send = project(
        me, [(basis_out, train_grads, Z_FIRST[4:]), (basis_in, train_acts, X_FIRST[4:])]
    )
    to_got = swap(to_send, Z1)
    ti_got = swap(ti_send, X)
    (qi_keep,) = project(me, [(basis_in, query_acts, X_FIRST[:4])])
    to_keep, ti_keep = project(
        me, [(basis_out, train_grads, Z_FIRST[:4]), (basis_in, train_acts, X_FIRST[:4])]
    )
    qo = halve(*halve(qo_keep, qo_got, Z1), Z2)
    qi = halve(*halve(qi_keep, qi_got, Z1), Z2)
    query = examples(place, *qo, *qi, query_slots)
    query = jnp.stack([query[0]] + [swap(query[k], 2 * k) for k in (1, 2, 3)])
    query = jnp.concatenate([query, swap(query, X)])
    queries = [query, lax.ppermute(query, "dp", [(0, 1), (1, 0)])]
    to = halve(*halve(to_keep, to_got, X), Z2)
    ti = halve(*halve(ti_keep, ti_got, Z1), Z2)
    train = examples(place, *to, *ti, train_slots)
    trains = [train[0]] + [swap(train[k], 2 * k) for k in (1, 2, 3)]
    scores = partial_scores(place, trains, queries)
    for mask in (Z2, Z1, X):
        scores = scores + swap(scores, mask)
    return scores


def solution(mesh):
    placed = (
        P("tensor", ("groups", "dp")),
        P("tensor", ("groups", "dp")),
        P("tensor", ("groups", "dp")),
        P("tensor", ("groups", "dp")),
        P(None, "tensor"),
        P(None, "tensor"),
        P(("groups", "dp")),
        P(("groups", "dp")),
    )

    def on_device(*arrays):
        fits = mesh.shape["tensor"] == 8 and mesh.shape["dp"] == 2 and arrays[6].shape[0] == 8 * BLK
        return (eight if fits and arrays[7].shape[0] == 8 * BLK else any_mesh)(*arrays)

    return jax.shard_map(
        on_device, mesh=mesh, in_specs=placed, out_specs=P(("groups", "dp"), None), check_vma=False
    )
```

time: 246 us -> 128 us (0.52)
  waiting for transfers between devices: 160 us -> 42.7 us
  matrix products: 55.5 us -> 0 us
  Pallas kernels: 0 us -> 48.9 us
  starting transfers between devices: 0.22 us -> 25.2 us
  between operations: 13.5 us -> 0.22 us
  local copies, waits for them, and re-layouts: 16.4 us -> 4.33 us
  other arithmetic: 0.23 us -> 6.09 us
    psum x1 -> x0, waiting for transfers between devices: 160 us -> none  [on_device(): lax.psum((partial_train_input, part_tout, part_qin, part_qout), 'tensor')]
    dot_general x7 -> x0, matrix products: 55.5 us -> none  [the longest x2 19.9 us: example_grads(): jnp.einsum('zij,cijd->idzc', output_block_list, weighted_rows, precision=...]
    pallas_call x0 -> x8, Pallas kernels: none -> 48.9 us  [the longest x5 42.1 us: project(): pl.pallas_call(kernel, out_shape=[jax.ShapeDtypeStruct((len(m), RANK, BLK...]
    ppermute x0 -> x23, waiting for transfers between devices: none -> 42.7 us  [the longest x22 42.6 us: swap(): return lax.ppermute(value, 'tensor', [(i, i ^ mask) for i in range(8)])]
    ppermute x0 -> x23, starting transfers between devices: none -> 25.2 us  [the longest x22 25.1 us: swap(): return lax.ppermute(value, 'tensor', [(i, i ^ mask) for i in range(8)])]
    add x0 -> x11, other arithmetic: none -> 5.49 us  [the longest x4 2.75 us: halve(): sent = swap(kept[n:] + got[n:], mask)]
    reshape x3 -> x0, local copies, waits for them, and re-layouts: 4.83 us -> none  [the longest x2 3.31 us: example_grads(): return summed_total.reshape(num_blocks * SEGS, RANK * RANK)]
    div x2 -> x0, local copies, waits for them, and re-layouts: 3.84 us -> none  [example_grads(): summed_total = summed_total / counts[:, :, None, None]]
  transfers between devices with their start and end apart: 2 -> 23, of which waited for: 1 -> 11; matrix products, arithmetic and copies ran while one was open for 6% -> 5% of each run, Pallas kernels for 0% -> 29%
where the time goes in v1:
time: 128 us; the launch traced here: 127 us
  Pallas kernels  48.9 us (38%)
  waiting for transfers between devices  42.7 us (33%)
  starting transfers between devices  25.2 us (20%)
  other arithmetic  6.09 us (5%)
  local copies, waits for them, and re-layouts  4.33 us (3%)
    ppermute x22, waiting for transfers between devices, swap(): return lax.ppermute(value, 'tensor', [(i, i ^ mask) for i in range(8)])  42.6 us
    pallas_call x5, Pallas kernels, project(): pl.pallas_call(kernel, out_shape=[jax.ShapeDtypeStruct((len(m), RANK, BLK...  42.1 us
    ppermute x22, starting transfers between devices, swap(): return lax.ppermute(value, 'tensor', [(i, i ^ mask) for i in range(8)])  25.1 us
    pallas_call x2, Pallas kernels, examples(): pl.pallas_call(kernel, out_shape=jax.ShapeDtypeStruct((4, HALF // 4, SEGS...  4.7 us
    add x4, other arithmetic, halve(): sent = swap(kept[n:] + got[n:], mask)  2.75 us
  transfers between devices with their start and end apart: 23, of which 11 were waited for; matrix products, arithmetic and copies ran while one was open for 5% of the time, Pallas kernels for 29%

profile of v1, /device:TPU:0, one launch (start us, length us, event | category | flops | bytes accessed | tf_op | source)
XLA Modules:
  0.0 127.4 jit_solution(1073319953073234415)
XLA Ops:
  0.0 9.3 %shard_map.83 = (f32[4,64,512]{2,1,0:T(8,128)}, f32[4,64,512]{2,1,0:T(8,128)}) custom-call(s32[1]{0:T(128)} %bitcast.1.me_ref, bf16[64,1024]{1,0:T(8,128)(2,1)} %refs_0_.8, bf16[64,3584]{1,0:T(8,128)(2,1)} %refs_0_.9, bf16[1024,4096]{1,0:T(8,128)(2,1)} %refs_2_.4, bf16[3584,4096]{1,0:T(8,128)(2,1)} %refs_3_.4), custom_call_target="tpu_custom_call" | custom-call | flops 1207959552 | bytes 18874368 | tf_op jit(solution)/shard_map/pallas_call | solution.py:97
  9.3 3.2 %collective-permute-start = (f32[4,64,512]{2,1,0:T(8,128)}, f32[4,64,512]{2,1,0:T(8,128)S(1)}, u32[]{:S(2)}, u32[]{:S(2)}) collective-permute-start(f32[4,64,512]{2,1,0:T(8,128)} %get-tuple-element.12), channel_id=1, source_target_pairs={{0,2},{1,3},{2,0},{3,1},{4,6},{5,7},{6,4},{7,5},{8,10},{9,11},{10,... | collective-permute-start | bytes 1572872 | tf_op jit(solution)/shard_map/ppermute | solution.py:187
  12.6 1.4 %collective-permute-start.3 = (f32[4,64,512]{2,1,0:T(8,128)}, f32[4,64,512]{2,1,0:T(8,128)S(1)}, u32[]{:S(2)}, u32[]{:S(2)}) collective-permute-start(f32[4,64,512]{2,1,0:T(8,128)} %get-tuple-element.14), channel_id=1, source_target_pairs={{0,1},{1,0},{2,3},{3,2},{4,5},{5,4},{6,7},{7,6},{8,9},{9,8},{10,11... | collective-permute-start | bytes 1572872 | tf_op jit(solution)/shard_map/ppermute | solution.py:187
  14.0 3.8 %shard_map.86 = f32[4,64,512]{2,1,0:T(8,128)} custom-call(s32[1]{0:T(128)} %bitcast.1.me_ref, bf16[64,1024]{1,0:T(8,128)(2,1)} %refs_0_.8, bf16[1024,4096]{1,0:T(8,128)(2,1)} %refs_1_.8), custom_call_target="tpu_custom_call" | custom-call | flops 268435456 | bytes 4194304 | tf_op jit(solution)/shard_map/pallas_call | solution.py:97
  17.8 0.7 collective-permute-start.9
  18.4 11.4 %shard_map.85 = (f32[4,64,512]{2,1,0:T(8,128)}, f32[4,64,512]{2,1,0:T(8,128)}) custom-call(s32[1]{0:T(128)} %bitcast.1.me_ref, bf16[64,3584]{1,0:T(8,128)(2,1)} %refs_0_.9, bf16[64,1024]{1,0:T(8,128)(2,1)} %refs_0_.8, bf16[3584,4096]{1,0:T(8,128)(2,1)} %refs_1_.9, bf16[1024,4096]{1,0:T(8,128)(2,1)} %refs_1_.8), custom_call_target="tpu_custom_call" | custom-call | flops 1207959552 | bytes 18874368 | tf_op jit(solution)/shard_map/pallas_call | solution.py:97
  29.8 1.3 collective-permute-start.12
  31.1 0.6 pad_add_fusion.place_ref
  31.7 9.4 %shard_map.82 = (f32[4,64,512]{2,1,0:T(8,128)}, f32[4,64,512]{2,1,0:T(8,128)}) custom-call(s32[1]{0:T(128)} %bitcast.1.me_ref, bf16[64,1024]{1,0:T(8,128)(2,1)} %refs_0_.8, bf16[64,3584]{1,0:T(8,128)(2,1)} %refs_0_.9, bf16[1024,4096]{1,0:T(8,128)(2,1)} %refs_2_.4, bf16[3584,4096]{1,0:T(8,128)(2,1)} %refs_3_.4), custom_call_target="tpu_custom_call" | custom-call | flops 1207959552 | bytes 18874368 | tf_op jit(solution)/shard_map/pallas_call | solution.py:97
  41.1 8.1 %shard_map.87 = f32[4,64,512]{2,1,0:T(8,128)} custom-call(s32[1]{0:T(128)} %bitcast.1.me_ref, bf16[64,3584]{1,0:T(8,128)(2,1)} %refs_0_.9, bf16[3584,4096]{1,0:T(8,128)(2,1)} %refs_1_.9), custom_call_target="tpu_custom_call" | custom-call | flops 939524096 | bytes 14680064 | tf_op jit(solution)/shard_map/pallas_call | solution.py:97
  49.4 0.9 collective-permute-start.1
  50.5 1.1 slice_add_fusion.1
  51.6 2.0 %collective-permute-start.13 = (f32[2,64,512]{2,1,0:T(8,128)S(1)}, f32[2,64,512]{2,1,0:T(8,128)S(1)}, u32[]{:S(2)}, u32[]{:S(2)}) collective-permute-start(f32[2,64,512]{2,1,0:T(8,128)S(1)} %get-tuple-element.18), channel_id=1, source_target_pairs={{0,2},{1,3},{2,0},{3,1},{4,6},{5,7},{6,4},{7,5},{8,10},{9,11},{10,... | collective-permute-start | bytes 786440 | tf_op jit(solution)/shard_map/ppermute | solution.py:187
  53.7 0.1 collective-permute-start.4
  53.9 7.2 %collective-permute-done.10 = f32[2,64,512]{2,1,0:T(8,128)S(1)} collective-permute-done((f32[2,64,512]{2,1,0:T(8,128)S(1)}, f32[2,64,512]{2,1,0:T(8,128)S(1)}, u32[]{:S(2)}, u32[]{:S(2)}) %collective-permute-start.10) | collective-permute-done | bytes 262176 | tf_op jit(solution)/shard_map/ppermute | solution.py:187
  61.1 0.7 slice_add_fusion.10
  61.8 1.3 collective-permute-start.11
  63.0 6.5 %collective-permute-done.13 = f32[2,64,512]{2,1,0:T(8,128)S(1)} collective-permute-done((f32[2,64,512]{2,1,0:T(8,128)S(1)}, f32[2,64,512]{2,1,0:T(8,128)S(1)}, u32[]{:S(2)}, u32[]{:S(2)}) %collective-permute-start.13) | collective-permute-done | bytes 262176 | tf_op jit(solution)/shard_map/ppermute | solution.py:187
  69.5 0.7 slice_add_fusion.8
  70.2 0.7 slice_add_fusion.14
  70.9 2.9 %collective-permute-start.2 = (f32[1,64,512]{2,1,0:T(8,128)S(1)}, f32[1,64,512]{2,1,0:T(8,128)S(1)}, u32[]{:S(2)}, u32[]{:S(2)}) collective-permute-start(f32[1,64,512]{2,1,0:T(8,128)S(1)} %get-tuple-element.31), channel_id=1, source_target_pairs={{0,4},{1,5},{2,6},{3,7},{4,0},{5,1},{6,2},{7,3},{8,12},{9,13},{10,... | collective-permute-start | bytes 393224 | tf_op jit(solution)/shard_map/ppermute | solution.py:187
  73.8 6.5 %collective-permute-done.14.in_b = f32[1,64,512]{2,1,0:T(8,128)S(1)} collective-permute-done((f32[1,64,512]{2,1,0:T(8,128)S(1)}, f32[1,64,512]{2,1,0:T(8,128)S(1)}, u32[]{:S(2)}, u32[]{:S(2)}) %collective-permute-start.14) | collective-permute-done | bytes 131104 | tf_op jit(solution)/shard_map/ppermute | solution.py:187
  80.4 0.6 copy-done.8
  81.0 2.4 %shard_map.88 = f32[4,8,8,128]{3,2,1,0:T(8,128)} custom-call(s32[4]{0:T(128)} %pad_add_fusion.place_ref, f32[1,64,512]{2,1,0:T(8,128)} %get-tuple-element.28.out_a, f32[1,64,512]{2,1,0:T(8,128)} %copy-done.7, f32[1,64,512]{2,1,0:T(8,128)} %get-tuple-element.26.in_a, f32[1,64,512]{2,1,0:T(8,128)} %copy-done.8, s32[8,1,512]{2,1,0:T(1,128)} %bitcast.29), custom_call_target="tpu_custom_call" | custom-call | tf_op jit(solution)/shard_map/pallas_call | solution.py:148
  83.4 0.8 fusion
  84.3 2.4 %collective-permute-start.16 = (f32[8,8,128]{2,1,0:T(8,128)S(1)}, f32[8,8,128]{2,1,0:T(8,128)S(1)}, u32[]{:S(2)}, u32[]{:S(2)}) collective-permute-start(f32[8,8,128]{2,1,0:T(8,128)S(1)} %get-tuple-element.36), channel_id=1, source_target_pairs={{0,4},{1,5},{2,6},{3,7},{4,0},{5,1},{6,2},{7,3},{8,12},{9,13},{10,... | collective-permute-start | bytes 98312 | tf_op jit(solution)/shard_map/ppermute | solution.py:187
  86.7 2.0 %collective-permute-start.17 = (f32[8,8,128]{2,1,0:T(8,128)S(1)}, f32[8,8,128]{2,1,0:T(8,128)S(1)}, u32[]{:S(2)}, u32[]{:S(2)}) collective-permute-start(f32[8,8,128]{2,1,0:T(8,128)S(1)} %get-tuple-element.35), channel_id=1, source_target_pairs={{0,6},{1,7},{2,4},{3,5},{4,2},{5,3},{6,0},{7,1},{8,14},{9,15},{10,... | collective-permute-start | bytes 98312 | tf_op jit(solution)/shard_map/ppermute | solution.py:187
  88.6 0.7 slice_add_fusion.12
  89.3 0.2 collective-permute-done.16
  89.5 2.9 %collective-permute-done.17 = f32[8,8,128]{2,1,0:T(8,128)S(1)} collective-permute-done((f32[8,8,128]{2,1,0:T(8,128)S(1)}, f32[8,8,128]{2,1,0:T(8,128)S(1)}, u32[]{:S(2)}, u32[]{:S(2)}) %collective-permute-start.17) | collective-permute-done | bytes 32800 | tf_op jit(solution)/shard_map/ppermute | solution.py:187
  92.4 1.3 %collective-permute-start.18 = (f32[4,8,8,128]{3,2,1,0:T(8,128)S(1)}, f32[4,8,8,128]{3,2,1,0:T(8,128)S(1)}, u32[]{:S(2)}, u32[]{:S(2)}) collective-permute-start(f32[4,8,8,128]{3,2,1,0:T(8,128)S(1)} %pad_maximum_fusion), channel_id=1, source_target_pairs={{0,1},{1,0},{2,3},{3,2},{4,5},{5,4},{6,7},{7,6},{8,9},{9,8},{10,11... | collective-permute-start | bytes 393224 | tf_op jit(solution)/shard_map/ppermute | solution.py:187
  93.7 3.7 %collective-permute-done.18 = f32[4,8,8,128]{3,2,1,0:T(8,128)S(1)} collective-permute-done((f32[4,8,8,128]{3,2,1,0:T(8,128)S(1)}, f32[4,8,8,128]{3,2,1,0:T(8,128)S(1)}, u32[]{:S(2)}, u32[]{:S(2)}) %collective-permute-start.18) | collective-permute-done | bytes 131104 | tf_op jit(solution)/shard_map/ppermute | solution.py:187
  97.6 0.6 copy-done.5
  98.3 2.3 %shard_map.84 = f32[4,8,8,128]{3,2,1,0:T(8,128)} custom-call(s32[4]{0:T(128)} %pad_add_fusion.place_ref, f32[1,64,512]{2,1,0:T(8,128)} %get-tuple-element.32.out_a, f32[1,64,512]{2,1,0:T(8,128)} %copy-done.5, f32[1,64,512]{2,1,0:T(8,128)} %get-tuple-element.30.in_a, f32[1,64,512]{2,1,0:T(8,128)} %copy-done.6, s32[8,1,512]{2,1,0:T(1,128)} %bitcast.30), custom_call_target="tpu_custom_call" | custom-call | tf_op jit(solution)/shard_map/pallas_call | solution.py:148
  100.6 1.4 %slice_bitcast_fusion.3 = (f32[8,8,128]{2,1,0:T(8,128)S(1)}, f32[8,8,128]{2,1,0:T(8,128)S(1)}, f32[8,8,128]{2,1,0:T(8,128)S(1)}, f32[8,8,128]{2,1,0:T(8,128)}) fusion(f32[4,8,8,128]{3,2,1,0:T(8,128)} %shard_map.84), kind=kLoop, calls=%fused_computation.20 | loop fusion | bytes 262144 | tf_op jit(solution)/shard_map/squeeze | solution.py:226
  102.1 2.5 %collective-permute-start.7 = (f32[8,8,128]{2,1,0:T(8,128)S(1)}, f32[8,8,128]{2,1,0:T(8,128)S(1)}, u32[]{:S(2)}, u32[]{:S(2)}) collective-permute-start(f32[8,8,128]{2,1,0:T(8,128)S(1)} %get-tuple-element.39), channel_id=1, source_target_pairs={{0,4},{1,5},{2,6},{3,7},{4,0},{5,1},{6,2},{7,3},{8,12},{9,13},{10,... | collective-permute-start | bytes 98312 | tf_op jit(solution)/shard_map/ppermute | solution.py:187
  104.6 1.9 %collective-permute-start.8 = (f32[8,8,128]{2,1,0:T(8,128)S(1)}, f32[8,8,128]{2,1,0:T(8,128)S(1)}, u32[]{:S(2)}, u32[]{:S(2)}) collective-permute-start(f32[8,8,128]{2,1,0:T(8,128)S(1)} %get-tuple-element.38), channel_id=1, source_target_pairs={{0,6},{1,7},{2,4},{3,5},{4,2},{5,3},{6,0},{7,1},{8,14},{9,15},{10,... | collective-permute-start | bytes 98312 | tf_op jit(solution)/shard_map/ppermute | solution.py:187
  106.4 0.5 collective-permute-done.7.refs_2_
  106.9 3.4 %collective-permute-done.8.refs_3_ = f32[8,8,128]{2,1,0:T(8,128)S(1)} collective-permute-done((f32[8,8,128]{2,1,0:T(8,128)S(1)}, f32[8,8,128]{2,1,0:T(8,128)S(1)}, u32[]{:S(2)}, u32[]{:S(2)}) %collective-permute-start.8) | collective-permute-done | bytes 32800 | tf_op jit(solution)/shard_map/ppermute | solution.py:187
  110.3 0.6 copy-done.11
  110.9 0.1 copy-done.4
  111.0 2.1 %shard_map.89 = f32[64,128]{1,0:T(8,128)} custom-call(s32[4]{0:T(128)} %pad_add_fusion.place_ref, f32[8,8,128]{2,1,0:T(8,128)} %get-tuple-element.41.refs_0_, f32[8,8,128]{2,1,0:T(8,128)} %copy-done.9, f32[8,8,128]{2,1,0:T(8,128)} %copy-done.10, f32[8,8,128]{2,1,0:T(8,128)} %copy-done.11, f32[8,8,8,128]{3,2,1,0:T(8,128)} %copy-done.3, f32[8,8,8,128]{3,2,1,0:T(8,128)} %copy-done.4), custom_call_target="tpu_custom_call" | custom-call | tf_op jit(solution)/shard_map/pallas_call | solution.py:174
  113.2 5.0 %collective-permute-done.20 = f32[64,128]{1,0:T(8,128)S(1)} collective-permute-done((f32[64,128]{1,0:T(8,128)}, f32[64,128]{1,0:T(8,128)S(1)}, u32[]{:S(2)}, u32[]{:S(2)}) %collective-permute-start.20) | collective-permute-done | bytes 32800 | tf_op jit(solution)/shard_map/ppermute | solution.py:187
  118.2 0.8 add.79
  118.9 3.9 %collective-permute-done.21 = f32[64,128]{1,0:T(8,128)S(1)} collective-permute-done((f32[64,128]{1,0:T(8,128)S(1)}, f32[64,128]{1,0:T(8,128)S(1)}, u32[]{:S(2)}, u32[]{:S(2)}) %collective-permute-start.21) | collective-permute-done | bytes 32800 | tf_op jit(solution)/shard_map/ppermute | solution.py:187
  122.9 1.1 collective-permute-start.22
  123.9 2.9 %collective-permute-done.22 = f32[64,128]{1,0:T(8,128)S(1)} collective-permute-done((f32[64,128]{1,0:T(8,128)S(1)}, f32[64,128]{1,0:T(8,128)S(1)}, u32[]{:S(2)}, u32[]{:S(2)}) %collective-permute-start.22) | collective-permute-done | bytes 32800 | tf_op jit(solution)/shard_map/ppermute | solution.py:187
  126.8 0.6 add.81
  (49 shorter events, 0.7 us)
Async XLA Ops:
  9.3 39.9 %collective-permute-start = (f32[4,64,512]{2,1,0:T(8,128)}, f32[4,64,512]{2,1,0:T(8,128)S(1)}, u32[]{:S(2)}, u32[]{:S(2)}) collective-permute-start(f32[4,64,512]{2,1,0:T(8,128)} %get-tuple-element.12), channel_id=1, source_target_pairs={{0,2},{1,3},{2,0},{3,1},{4,6},{5,7},{6,4},{7,5},{8,10},{9,11},{10,... | collective-permute-start | bytes 1572872 | tf_op jit(solution)/shard_map/ppermute | solution.py:187
  12.6 41.1 %collective-permute-start.3 = (f32[4,64,512]{2,1,0:T(8,128)}, f32[4,64,512]{2,1,0:T(8,128)S(1)}, u32[]{:S(2)}, u32[]{:S(2)}) collective-permute-start(f32[4,64,512]{2,1,0:T(8,128)} %get-tuple-element.14), channel_id=1, source_target_pairs={{0,1},{1,0},{2,3},{3,2},{4,5},{5,4},{6,7},{7,6},{8,9},{9,8},{10,11... | collective-permute-start | bytes 1572872 | tf_op jit(solution)/shard_map/ppermute | solution.py:187
  17.8 32.5 %collective-permute-start.9 = (f32[4,64,512]{2,1,0:T(8,128)}, f32[4,64,512]{2,1,0:T(8,128)S(1)}, u32[]{:S(2)}, u32[]{:S(2)}) collective-permute-start(f32[4,64,512]{2,1,0:T(8,128)} %shard_map.86), channel_id=1, source_target_pairs={{0,1},{1,0},{2,3},{3,2},{4,5},{5,4},{6,7},{7,6},{8,9},{9,8},{10,11... | collective-permute-start | bytes 1572872 | tf_op jit(solution)/shard_map/ppermute | solution.py:187
  29.8 20.7 %collective-permute-start.12 = (f32[4,64,512]{2,1,0:T(8,128)}, f32[4,64,512]{2,1,0:T(8,128)S(1)}, u32[]{:S(2)}, u32[]{:S(2)}) collective-permute-start(f32[4,64,512]{2,1,0:T(8,128)} %get-tuple-element.16), channel_id=1, source_target_pairs={{0,1},{1,0},{2,3},{3,2},{4,5},{5,4},{6,7},{7,6},{8,9},{9,8},{10,11... | collective-permute-start | bytes 1572872 | tf_op jit(solution)/shard_map/ppermute | solution.py:187
  31.7 18.6 %copy-start = (f32[4,64,512]{2,1,0:T(8,128)S(1)}, f32[4,64,512]{2,1,0:T(8,128)}, u32[]{:S(2)}) copy-start(f32[4,64,512]{2,1,0:T(8,128)} %get-tuple-element.15) | copy-start | bytes 1572868
  41.1 8.2 %copy-start.2 = (f32[4,64,512]{2,1,0:T(8,128)S(1)}, f32[4,64,512]{2,1,0:T(8,128)}, u32[]{:S(2)}) copy-start(f32[4,64,512]{2,1,0:T(8,128)} %get-tuple-element.11) | copy-start | bytes 1572868
  41.1 12.5 %copy-start.1 = (f32[4,64,512]{2,1,0:T(8,128)S(1)}, f32[4,64,512]{2,1,0:T(8,128)}, u32[]{:S(2)}) copy-start(f32[4,64,512]{2,1,0:T(8,128)} %get-tuple-element.13) | copy-start | bytes 1572868
  49.4 20.9 %collective-permute-start.1 = (f32[2,64,512]{2,1,0:T(8,128)S(1)}, f32[2,64,512]{2,1,0:T(8,128)S(1)}, u32[]{:S(2)}, u32[]{:S(2)}) collective-permute-start(f32[2,64,512]{2,1,0:T(8,128)S(1)} %get-tuple-element.24), channel_id=1, source_target_pairs={{0,1},{1,0},{2,3},{3,2},{4,5},{5,4},{6,7},{7,6},{8,9},{9,8},{10,11... | collective-permute-start | bytes 786440 | tf_op jit(solution)/shard_map/ppermute | solution.py:187
  50.4 10.7 %collective-permute-start.10 = (f32[2,64,512]{2,1,0:T(8,128)S(1)}, f32[2,64,512]{2,1,0:T(8,128)S(1)}, u32[]{:S(2)}, u32[]{:S(2)}) collective-permute-start(f32[2,64,512]{2,1,0:T(8,128)S(1)} %get-tuple-element.20), channel_id=1, source_target_pairs={{0,2},{1,3},{2,0},{3,1},{4,6},{5,7},{6,4},{7,5},{8,10},{9,11},{10,... | collective-permute-start | bytes 786440 | tf_op jit(solution)/shard_map/ppermute | solution.py:187
  51.6 17.9 %collective-permute-start.13 = (f32[2,64,512]{2,1,0:T(8,128)S(1)}, f32[2,64,512]{2,1,0:T(8,128)S(1)}, u32[]{:S(2)}, u32[]{:S(2)}) collective-permute-start(f32[2,64,512]{2,1,0:T(8,128)S(1)} %get-tuple-element.18), channel_id=1, source_target_pairs={{0,2},{1,3},{2,0},{3,1},{4,6},{5,7},{6,4},{7,5},{8,10},{9,11},{10,... | collective-permute-start | bytes 786440 | tf_op jit(solution)/shard_map/ppermute | solution.py:187
  53.7 34.9 %collective-permute-start.4 = (f32[2,64,512]{2,1,0:T(8,128)S(1)}, f32[2,64,512]{2,1,0:T(8,128)S(1)}, u32[]{:S(2)}, u32[]{:S(2)}) collective-permute-start(f32[2,64,512]{2,1,0:T(8,128)S(1)} %get-tuple-element.22), channel_id=1, source_target_pairs={{0,2},{1,3},{2,0},{3,1},{4,6},{5,7},{6,4},{7,5},{8,10},{9,11},{10,... | collective-permute-start | bytes 786440 | tf_op jit(solution)/shard_map/ppermute | solution.py:187
  61.8 12.1 %collective-permute-start.11 = (f32[1,64,512]{2,1,0:T(8,128)S(1)}, f32[1,64,512]{2,1,0:T(8,128)S(1)}, u32[]{:S(2)}, u32[]{:S(2)}) collective-permute-start(f32[1,64,512]{2,1,0:T(8,128)S(1)} %get-tuple-element.27), channel_id=1, source_target_pairs={{0,4},{1,5},{2,6},{3,7},{4,0},{5,1},{6,2},{7,3},{8,12},{9,13},{10,... | collective-permute-start | bytes 393224 | tf_op jit(solution)/shard_map/ppermute | solution.py:187
  70.2 10.1 %collective-permute-start.14 = (f32[1,64,512]{2,1,0:T(8,128)S(1)}, f32[1,64,512]{2,1,0:T(8,128)S(1)}, u32[]{:S(2)}, u32[]{:S(2)}) collective-permute-start(f32[1,64,512]{2,1,0:T(8,128)S(1)} %get-tuple-element.25), channel_id=1, source_target_pairs={{0,4},{1,5},{2,6},{3,7},{4,0},{5,1},{6,2},{7,3},{8,12},{9,13},{10,... | collective-permute-start | bytes 393224 | tf_op jit(solution)/shard_map/ppermute | solution.py:187
  70.9 26.6 %collective-permute-start.2 = (f32[1,64,512]{2,1,0:T(8,128)S(1)}, f32[1,64,512]{2,1,0:T(8,128)S(1)}, u32[]{:S(2)}, u32[]{:S(2)}) collective-permute-start(f32[1,64,512]{2,1,0:T(8,128)S(1)} %get-tuple-element.31), channel_id=1, source_target_pairs={{0,4},{1,5},{2,6},{3,7},{4,0},{5,1},{6,2},{7,3},{8,12},{9,13},{10,... | collective-permute-start | bytes 393224 | tf_op jit(solution)/shard_map/ppermute | solution.py:187
  73.8 6.5 %copy-start.7 = (f32[1,64,512]{2,1,0:T(8,128)}, f32[1,64,512]{2,1,0:T(8,128)S(1)}, u32[]{:S(2)}) copy-start(f32[1,64,512]{2,1,0:T(8,128)S(1)} %collective-permute-done.11.out_b) | copy-start | bytes 393220
  80.4 0.6 copy-start.8
  84.2 5.2 %collective-permute-start.15 = (f32[8,8,128]{2,1,0:T(8,128)S(1)}, f32[8,8,128]{2,1,0:T(8,128)S(1)}, u32[]{:S(2)}, u32[]{:S(2)}) collective-permute-start(f32[8,8,128]{2,1,0:T(8,128)S(1)} %get-tuple-element.37), channel_id=1, source_target_pairs={{0,2},{1,3},{2,0},{3,1},{4,6},{5,7},{6,4},{7,5},{8,10},{9,11},{10,... | collective-permute-start | bytes 98312 | tf_op jit(solution)/shard_map/ppermute | solution.py:187
  84.3 5.2 %collective-permute-start.16 = (f32[8,8,128]{2,1,0:T(8,128)S(1)}, f32[8,8,128]{2,1,0:T(8,128)S(1)}, u32[]{:S(2)}, u32[]{:S(2)}) collective-permute-start(f32[8,8,128]{2,1,0:T(8,128)S(1)} %get-tuple-element.36), channel_id=1, source_target_pairs={{0,4},{1,5},{2,6},{3,7},{4,0},{5,1},{6,2},{7,3},{8,12},{9,13},{10,... | collective-permute-start | bytes 98312 | tf_op jit(solution)/shard_map/ppermute | solution.py:187
  86.7 5.7 %collective-permute-start.17 = (f32[8,8,128]{2,1,0:T(8,128)S(1)}, f32[8,8,128]{2,1,0:T(8,128)S(1)}, u32[]{:S(2)}, u32[]{:S(2)}) collective-permute-start(f32[8,8,128]{2,1,0:T(8,128)S(1)} %get-tuple-element.35), channel_id=1, source_target_pairs={{0,6},{1,7},{2,4},{3,5},{4,2},{5,3},{6,0},{7,1},{8,14},{9,15},{10,... | collective-permute-start | bytes 98312 | tf_op jit(solution)/shard_map/ppermute | solution.py:187
  89.3 8.2 %collective-permute-start.5 = (f32[1,64,512]{2,1,0:T(8,128)S(1)}, f32[1,64,512]{2,1,0:T(8,128)S(1)}, u32[]{:S(2)}, u32[]{:S(2)}) collective-permute-start(f32[1,64,512]{2,1,0:T(8,128)S(1)} %get-tuple-element.29), channel_id=1, source_target_pairs={{0,4},{1,5},{2,6},{3,7},{4,0},{5,1},{6,2},{7,3},{8,12},{9,13},{10,... | collective-permute-start | bytes 393224 | tf_op jit(solution)/shard_map/ppermute | solution.py:187
  92.4 5.0 %collective-permute-start.18 = (f32[4,8,8,128]{3,2,1,0:T(8,128)S(1)}, f32[4,8,8,128]{3,2,1,0:T(8,128)S(1)}, u32[]{:S(2)}, u32[]{:S(2)}) collective-permute-start(f32[4,8,8,128]{3,2,1,0:T(8,128)S(1)} %pad_maximum_fusion), channel_id=1, source_target_pairs={{0,1},{1,0},{2,3},{3,2},{4,5},{5,4},{6,7},{7,6},{8,9},{9,8},{10,11... | collective-permute-start | bytes 393224 | tf_op jit(solution)/shard_map/ppermute | solution.py:187
  97.5 12.8 %copy-start.3 = (f32[8,8,8,128]{3,2,1,0:T(8,128)}, f32[8,8,8,128]{3,2,1,0:T(8,128)S(1)}, u32[]{:S(2)}) copy-start(f32[8,8,8,128]{3,2,1,0:T(8,128)S(1)} %constant_dynamic-update-slice_fusion.refs_4_) | copy-start | bytes 786436
  97.5 12.8 %collective-permute-start.19 = (f32[8,8,8,128]{3,2,1,0:T(8,128)S(1)}, f32[8,8,8,128]{3,2,1,0:T(8,128)S(1)}, u32[]{:S(2)}, u32[]{:S(2)}) collective-permute-start(f32[8,8,8,128]{3,2,1,0:T(8,128)S(1)} %constant_dynamic-update-slice_fusion.refs_4_), channel_id=1, source_target_pairs={{0,8},{8,0},{1,9},{9,1},{2,10},{10,2},{3,11},{11,3},{4,12},{12,4},... | collective-permute-start | bytes 786440 | tf_op jit(solution)/shard_map/ppermute | solution.py:222
  97.6 0.7 copy-start.5
  97.6 0.7 copy-start.6
  102.1 4.4 %collective-permute-start.6 = (f32[8,8,128]{2,1,0:T(8,128)S(1)}, f32[8,8,128]{2,1,0:T(8,128)S(1)}, u32[]{:S(2)}, u32[]{:S(2)}) collective-permute-start(f32[8,8,128]{2,1,0:T(8,128)S(1)} %get-tuple-element.40), channel_id=1, source_target_pairs={{0,2},{1,3},{2,0},{3,1},{4,6},{5,7},{6,4},{7,5},{8,10},{9,11},{10,... | collective-permute-start | bytes 98312 | tf_op jit(solution)/shard_map/ppermute | solution.py:187
  102.1 4.9 %collective-permute-start.7 = (f32[8,8,128]{2,1,0:T(8,128)S(1)}, f32[8,8,128]{2,1,0:T(8,128)S(1)}, u32[]{:S(2)}, u32[]{:S(2)}) collective-permute-start(f32[8,8,128]{2,1,0:T(8,128)S(1)} %get-tuple-element.39), channel_id=1, source_target_pairs={{0,4},{1,5},{2,6},{3,7},{4,0},{5,1},{6,2},{7,3},{8,12},{9,13},{10,... | collective-permute-start | bytes 98312 | tf_op jit(solution)/shard_map/ppermute | solution.py:187
  104.6 5.7 %collective-permute-start.8 = (f32[8,8,128]{2,1,0:T(8,128)S(1)}, f32[8,8,128]{2,1,0:T(8,128)S(1)}, u32[]{:S(2)}, u32[]{:S(2)}) collective-permute-start(f32[8,8,128]{2,1,0:T(8,128)S(1)} %get-tuple-element.38), channel_id=1, source_target_pairs={{0,6},{1,7},{2,4},{3,5},{4,2},{5,3},{6,0},{7,1},{8,14},{9,15},{10,... | collective-permute-start | bytes 98312 | tf_op jit(solution)/shard_map/ppermute | solution.py:187
  106.4 3.9 %copy-start.9 = (f32[8,8,128]{2,1,0:T(8,128)}, f32[8,8,128]{2,1,0:T(8,128)S(1)}, u32[]{:S(2)}) copy-start(f32[8,8,128]{2,1,0:T(8,128)S(1)} %collective-permute-done.6.refs_1_) | copy-start | bytes 98308
  106.9 3.4 %copy-start.10 = (f32[8,8,128]{2,1,0:T(8,128)}, f32[8,8,128]{2,1,0:T(8,128)S(1)}, u32[]{:S(2)}) copy-start(f32[8,8,128]{2,1,0:T(8,128)S(1)} %collective-permute-done.7.refs_2_) | copy-start | bytes 98308
  110.3 0.6 copy-start.11
  110.3 0.7 copy-start.4
  113.2 5.0 %collective-permute-start.20 = (f32[64,128]{1,0:T(8,128)}, f32[64,128]{1,0:T(8,128)S(1)}, u32[]{:S(2)}, u32[]{:S(2)}) collective-permute-start(f32[64,128]{1,0:T(8,128)} %shard_map.89), channel_id=1, source_target_pairs={{0,4},{1,5},{2,6},{3,7},{4,0},{5,1},{6,2},{7,3},{8,12},{9,13},{10,... | collective-permute-start | bytes 98312 | tf_op jit(solution)/shard_map/ppermute | solution.py:187
  118.9 3.9 %collective-permute-start.21 = (f32[64,128]{1,0:T(8,128)S(1)}, f32[64,128]{1,0:T(8,128)S(1)}, u32[]{:S(2)}, u32[]{:S(2)}) collective-permute-start(f32[64,128]{1,0:T(8,128)S(1)} %add.79), channel_id=1, source_target_pairs={{0,2},{1,3},{2,0},{3,1},{4,6},{5,7},{6,4},{7,5},{8,10},{9,11},{10,... | collective-permute-start | bytes 98312 | tf_op jit(solution)/shard_map/ppermute | solution.py:187
  122.9 3.9 %collective-permute-start.22 = (f32[64,128]{1,0:T(8,128)S(1)}, f32[64,128]{1,0:T(8,128)S(1)}, u32[]{:S(2)}, u32[]{:S(2)}) collective-permute-start(f32[64,128]{1,0:T(8,128)S(1)} %add.80), channel_id=1, source_target_pairs={{0,1},{1,0},{2,3},{3,2},{4,5},{5,4},{6,7},{7,6},{8,9},{9,8},{10,11... | collective-permute-start | bytes 98312 | tf_op jit(solution)/shard_map/ppermute | solution.py:187

commit v2 on v1

v2 whole, which is shorter than its diff:
```python
import jax
import jax.numpy as jnp
from jax import lax
from jax.experimental import pallas as pl
from jax.experimental.pallas import tpu as pltpu
from jax.sharding import PartitionSpec as P

RANK = 64
BLK = 512
SEGS = 8
HALF = RANK // 2
X, Z1, Z2 = 1, 2, 4
X_FIRST = (0, Z2, Z1, Z1 | Z2, X, X | Z2, X | Z1, X | Z1 | Z2)
Z_FIRST = (0, Z2, X, X | Z2, Z1, Z1 | Z2, Z1 | X, X | Z1 | Z2)
AHEAD = 7 * 1024 * 1024
LIGHT = 1
VMEM = 56 * 1024 * 1024


def example_grads(proj_out, proj_in, slot_ids):
    num_blocks = slot_ids.shape[0] // BLK
    output_block_list = proj_out.reshape(RANK, num_blocks, BLK)
    in_blocks = proj_in.reshape(RANK, num_blocks, BLK)
    onehot = (
        slot_ids.reshape(num_blocks, BLK)[:, :, None]
        == jnp.arange(SEGS, dtype=jnp.int32)[None, None, :]
    ).astype(jnp.float32)
    counts = jnp.maximum(jnp.sum(onehot, axis=1), 1.0)
    weighted_rows = in_blocks[:, :, :, None] * onehot[None]
    summed_total = jnp.einsum(
        "zij,cijd->idzc", output_block_list, weighted_rows, precision=lax.Precision.HIGHEST
    )
    summed_total = summed_total / counts[:, :, None, None]
    return summed_total.reshape(num_blocks * SEGS, RANK * RANK)


def any_mesh(
    train_acts, train_grads, query_acts, query_grads, basis_in, basis_out, train_slots, query_slots
):
    sums = lax.psum(
        tuple(
            jnp.dot(basis, data, preferred_element_type=jnp.float32)
            for basis, data in (
                (basis_in, train_acts),
                (basis_out, train_grads),
                (basis_in, query_acts),
                (basis_out, query_grads),
            )
        ),
        "tensor",
    )
    train_ex = example_grads(sums[1], sums[0], train_slots)
    query_ex = example_grads(sums[3], sums[2], query_slots)
    return jnp.dot(
        train_ex,
        lax.all_gather(query_ex, "dp", axis=0, tiled=True).T,
        precision=lax.Precision.HIGHEST,
        preferred_element_type=jnp.float32,
    )


def project(me, sources, jobs, name):
    count, made_count = len(sources), len(jobs)
    steps = [(n, i, source, mask) for n, (source, masks) in enumerate(jobs) for i, mask in enumerate(masks)]

    ahead = AHEAD // max(data.shape[0] * BLK * 2 for _, data in sources) + 1

    def kernel(me_ref, *refs):
        bases, datas = refs[:count], refs[count : 2 * count]
        refs = refs[2 * count :]
        outs, refs = refs[:made_count], refs[made_count:]
        held, slots = refs[:count], refs[count : 2 * count]
        basis_sem, in_sem = refs[2 * count :]
        here = me_ref[0]
        firsts = [pltpu.make_async_copy(bases[n], held[n], basis_sem.at[n]) for n in range(count)]
        for first in firsts:
            first.start()
        used = [0] * count
        copies = []
        for step, (n, i, source, mask) in enumerate(steps):
            at = pl.multiple_of((here ^ mask) * BLK, BLK)
            copy = pltpu.make_async_copy(
                datas[source].at[:, pl.ds(at, BLK)], slots[source].at[used[source]], in_sem.at[step]
            )
            copies.append((copy, used[source]))
            used[source] += 1
            if step < ahead:
                copy.start()
        for step, (n, i, source, mask) in enumerate(steps):
            copy, slot = copies[step]
            if slot == 0:
                firsts[source].wait()
            copy.wait()
            if step + ahead < len(steps):
                copies[step + ahead][0].start()
            outs[n][i] = jnp.dot(
                held[source][...], slots[source][slot], preferred_element_type=jnp.float32
            )

    slots_of = [sum(len(masks) for source, masks in jobs if source == n) for n in range(count)]
    moved = sum(c * data.shape[0] * BLK * 2 for c, (basis, data) in zip(slots_of, sources))
    return pl.pallas_call(
        kernel,
        out_shape=[pltpu.VMEM((len(masks), RANK, BLK), jnp.float32) for _, masks in jobs],
        in_specs=[pl.BlockSpec(memory_space=pltpu.SMEM)] + [pl.BlockSpec(memory_space=pltpu.HBM)] * (2 * count),
        out_specs=[pl.BlockSpec(memory_space=pltpu.VMEM)] * made_count,
        scratch_shapes=[pltpu.VMEM(basis.shape, jnp.bfloat16) for basis, _ in sources]
        + [pltpu.VMEM((c, data.shape[0], BLK), jnp.bfloat16) for c, (_, data) in zip(slots_of, sources)]
        + [
            pltpu.SemaphoreType.DMA((count,)),
            pltpu.SemaphoreType.DMA((len(steps),)),
        ],
        compiler_params=pltpu.CompilerParams(vmem_limit_bytes=VMEM),
        cost_estimate=pl.CostEstimate(
            flops=moved * RANK // LIGHT, bytes_accessed=moved // LIGHT, transcendentals=0
        ),
        name=name,
    )(me, *[basis for basis, _ in sources], *[data for _, data in sources])


def two(x):
    high = x.astype(jnp.bfloat16)
    return high, (x - high.astype(jnp.float32)).astype(jnp.bfloat16)


def rows_by_rows(a, b):
    def dot(p, q):
        return lax.dot_general(p, q, (((1,), (1,)), ((), ())), preferred_element_type=jnp.float32)

    return dot(a[0], b[0]) + (dot(a[0], b[1]) + dot(a[1], b[0]))


def examples(place, outs, inners, slots):
    def kernel(place_ref, *refs):
        slot_ref, ex_refs, held = refs[8], refs[9:13], refs[13]
        z, me = place_ref[0], place_ref[1]
        out = (refs[0][0] + refs[1][0]) + (refs[2][0] + refs[3][0])
        inner = (refs[4][0] + refs[5][0]) + (refs[6][0] + refs[7][0])
        seg = lax.broadcasted_iota(jnp.int32, (SEGS, BLK), 0)
        mask = (slot_ref[me] == seg).astype(jnp.float32)
        counts = jnp.maximum(jnp.sum(mask, axis=1, keepdims=True), 1.0)
        none = jnp.zeros_like(inner)
        total = None
        for h, padded in enumerate(((inner, none), (none, inner))):
            rows = out[h * HALF : (h + 1) * HALF][:, None, :] * mask[None]
            part = rows_by_rows(
                two(rows.reshape(HALF * SEGS, BLK)), two(jnp.concatenate(padded, axis=0))
            )
            total = part if total is None else total + part
        ex = total.reshape(4, HALF // 4, SEGS, 2 * RANK) / counts[None, None]
        held[...] = ex
        for k in range(4):
            ex_refs[k][...] = held[k ^ z]

    blocks = slots.shape[0] // BLK
    first = pl.BlockSpec((1, RANK, BLK), lambda i: (0, 0, 0))
    return pl.pallas_call(
        kernel,
        grid=(1,),
        out_shape=[jax.ShapeDtypeStruct((HALF // 4, SEGS, 2 * RANK), jnp.float32)] * 4,
        in_specs=[pl.BlockSpec(memory_space=pltpu.SMEM)]
        + [first] * 8
        + [pl.BlockSpec((blocks, 1, BLK), lambda i: (0, 0, 0))],
        out_specs=[pl.BlockSpec((HALF // 4, SEGS, 2 * RANK), lambda i: (0, 0, 0))] * 4,
        scratch_shapes=[pltpu.VMEM((4, HALF // 4, SEGS, 2 * RANK), jnp.float32)],
        name="examples",
    )(place, *outs, *inners, slots.reshape(blocks, 1, BLK))


def partial_scores(place, trains, queries):
    def kernel(place_ref, *refs):
        t_refs, q_refs = refs[:4], refs[4:8]
        out_ref, q_all, t_all = refs[8:]
        z, x, dp = place_ref[0], place_ref[2], place_ref[3]
        for k in range(4):
            t_all[k ^ z] = t_refs[k][...]
        for d in range(4):
            for k in range(4):
                q_all[((d // 2) ^ dp) * 8 + (k ^ z) * 2 + ((d % 2) ^ x)] = q_refs[d][k]
        a2 = range(HALF // 4)
        train = jnp.concatenate([t_all[:, a].reshape(4 * SEGS, 2 * RANK) for a in a2], axis=1)
        query = jnp.concatenate([q_all[:, a].reshape(16 * SEGS, 2 * RANK) for a in a2], axis=1)
        scores = rows_by_rows(two(train), two(query))
        out_ref[...] = jnp.zeros_like(out_ref)
        for k in range(4):
            out_ref[pl.ds(pl.multiple_of((2 * k + x) * SEGS, SEGS), SEGS)] = scores[k * SEGS : (k + 1) * SEGS]

    return pl.pallas_call(
        kernel,
        out_shape=jax.ShapeDtypeStruct((8 * SEGS, 16 * SEGS), jnp.float32),
        in_specs=[pl.BlockSpec(memory_space=pltpu.SMEM)] + [pl.BlockSpec(memory_space=pltpu.VMEM)] * 8,
        out_specs=pl.BlockSpec(memory_space=pltpu.VMEM),
        scratch_shapes=[
            pltpu.VMEM((16, HALF // 4, SEGS, 2 * RANK), jnp.float32),
            pltpu.VMEM((4, HALF // 4, SEGS, 2 * RANK), jnp.float32),
        ],
        name="partial_scores",
    )(place, *trains, *queries)


def swap(value, mask, name):
    with jax.named_scope(name):
        return lax.ppermute(value, "tensor", [(i, i ^ mask) for i in range(8)])


def cross(value, name):
    with jax.named_scope(name):
        return lax.ppermute(value, "dp", [(0, 1), (1, 0)])


def after(value, *others):
    return lax.optimization_barrier((value, *others))[0]


def eight(
    train_acts, train_grads, query_acts, query_grads, basis_in, basis_out, train_slots, query_slots
):
    tensor = lax.axis_index("tensor").astype(jnp.int32)
    me = tensor.reshape(1)
    place = jnp.stack([tensor // 2, tensor, tensor % 2, lax.axis_index("dp").astype(jnp.int32)])

    ins, outs = (basis_in, query_acts), (basis_out, query_grads)
    train_ins, train_outs = (basis_in, train_acts), (basis_out, train_grads)

    qo_send, to_send = project(me, [outs, train_outs], [(0, Z_FIRST[4:]), (1, Z_FIRST[4:])], "first_outs")
    qo1 = swap(qo_send, Z1, "z1_qo")
    me = after(me, qo_send)
    (qi_send,) = project(me, [ins], [(0, X_FIRST[4:])], "first_query_in")
    to_send = after(to_send, qi_send)
    qi1 = swap(qi_send, X, "x_qi")
    to1 = swap(to_send, Z1, "z1_to")
    me = after(me, qi_send)
    qo, qi = project(me, [outs, ins], [(0, Z_FIRST[:4]), (1, X_FIRST[:4])], "last_query")
    qo_send = qo[2:] + qo1[2:]
    qo2 = swap(qo_send, X, "x_qo")
    me = after(me, qo_send)
    (ti_send,) = project(me, [train_ins], [(0, X_FIRST[4:])], "first_train_in")
    ti1 = swap(ti_send, X, "x_ti")
    qi, qi1, _ = lax.optimization_barrier((qi, qi1, ti_send))
    qi_send = qi[2:] + qi1[2:]
    qi2 = swap(qi_send, Z1, "z1_qi")
    qo, qo1, qo2, _ = lax.optimization_barrier((qo, qo1, qo2, qi_send))
    qo_send = qo[1:2] + qo1[1:2] + qo2[1:2]
    qo3 = swap(qo_send, Z2, "z2_qo")
    me = after(me, qo_send)
    to, ti = project(me, [train_outs, train_ins], [(0, Z_FIRST[:4]), (1, X_FIRST[:4])], "last_train")
    to, ti, to1, qi2, qo3 = lax.optimization_barrier((to, ti, to1, qi2, qo3))
    ti_send = ti[2:] + ti1[2:]
    ti2 = swap(ti_send, Z1, "z1_ti")
    qi, qi1, qi2, _ = lax.optimization_barrier((qi, qi1, qi2, ti_send))
    qi_send = qi[1:2] + qi1[1:2] + qi2[1:2]
    qi3 = swap(qi_send, Z2, "z2_qi")
    to, to1, _ = lax.optimization_barrier((to, to1, qi_send))
    to_send = to[2:] + to1[2:]
    to2 = swap(to_send, X, "x_to")
    place = after(place, to_send)
    query = examples(place, (qo, qo1, qo2, qo3), (qi, qi1, qi2, qi3), query_slots)
    query, ti2, to2, _ = lax.optimization_barrier((query, ti2, to2, query[0]))
    ti_send = ti[1:2] + ti1[1:2] + ti2[1:2]
    ti3 = swap(ti_send, Z2, "z2_ti")
    to, to1, to2, _ = lax.optimization_barrier((to, to1, to2, ti_send))
    to_send = to[1:2] + to1[1:2] + to2[1:2]
    to3 = swap(to_send, Z2, "z2_to")
    query = lax.optimization_barrier((*query, to_send))[:4]
    query = [query[0]] + [swap(query[k], 2 * k, "z_query") for k in (1, 2, 3)]
    place, ti3, to3, *query = lax.optimization_barrier((place, ti3, to3, *query))
    train = examples(place, (to, to1, to2, to3), (ti, ti1, ti2, ti3), train_slots)
    query = jnp.stack(query)
    other = swap(query, X, "x_query")
    trains = [train[0]] + [swap(train[k], 2 * k, "z_train") for k in (1, 2, 3)]
    other, *trains = lax.optimization_barrier((other, *trains))
    queries = [query, other, cross(query, "dp_query"), cross(other, "dp_x_query")]
    scores = partial_scores(place, trains, queries)
    for mask in (Z2, Z1, X):
        scores = scores + swap(scores, mask, "scores")
    return scores


def solution(mesh):
    placed = (
        P("tensor", ("groups", "dp")),
        P("tensor", ("groups", "dp")),
        P("tensor", ("groups", "dp")),
        P("tensor", ("groups", "dp")),
        P(None, "tensor"),
        P(None, "tensor"),
        P(("groups", "dp")),
        P(("groups", "dp")),
    )

    def on_device(*arrays):
        fits = mesh.shape["tensor"] == 8 and mesh.shape["dp"] == 2 and arrays[6].shape[0] == 8 * BLK
        return (eight if fits and arrays[7].shape[0] == 8 * BLK else any_mesh)(*arrays)

    return jax.shard_map(
        on_device, mesh=mesh, in_specs=placed, out_specs=P(("groups", "dp"), None), check_vma=False
    )
```

time: 128 us -> 106 us (0.83)
  waiting for transfers between devices: 42.7 us -> 26.7 us
  Pallas kernels: 48.9 us -> 41.8 us
  starting transfers between devices: 25.2 us -> 31.5 us
  local copies, waits for them, and re-layouts: 4.33 us -> 1.37 us
  other arithmetic: 6.09 us -> 3.87 us
    ppermute x22, waiting for transfers between devices: 42.6 us -> 25.4 us  [swap(): return lax.ppermute(value, 'tensor', [(i, i ^ mask) for i in range(8)])]
    pallas_call x7, Pallas kernels: 46.8 us -> 39.6 us  [the longest x5 34.5 us: project(): pl.pallas_call(kernel, out_shape=[pltpu.VMEM((len(masks), RANK, BLK), jnp...]
    ppermute x22, starting transfers between devices: 25.1 us -> 31.4 us  [swap(): return lax.ppermute(value, 'tensor', [(i, i ^ mask) for i in range(8)])]
    add x11, other arithmetic: 5.49 us -> 2.5 us  [the longest x3 1.39 us: eight(): scores = scores + swap(scores, mask, 'scores')]
    squeeze x1 -> x0, local copies, waits for them, and re-layouts: 1.43 us -> none  [eight(): trains = [train[0]] + [swap(train[k], 2 * k) for k in (1, 2, 3)]]
    ppermute x1 -> x2, waiting for transfers between devices: 0.01 us -> 1.32 us  [cross(): return lax.ppermute(value, 'dp', [(0, 1), (1, 0)])]
  transfers between devices with their start and end apart: 23 -> 24, of which waited for: 11 -> 8; matrix products, arithmetic and copies ran while one was open for 5% -> 1% of each run, Pallas kernels for 29% -> 32%
where the time goes in v2:
time: 106 us
  Pallas kernels  41.8 us (39%)
  starting transfers between devices  31.5 us (30%)
  waiting for transfers between devices  26.7 us (25%)
  other arithmetic  3.87 us (4%)
  local copies, waits for them, and re-layouts  1.37 us (1%)
    pallas_call x5, Pallas kernels, project(): pl.pallas_call(kernel, out_shape=[pltpu.VMEM((len(masks), RANK, BLK), jnp...  34.5 us
    ppermute x22, starting transfers between devices, swap(): return lax.ppermute(value, 'tensor', [(i, i ^ mask) for i in range(8)])  31.4 us
    ppermute x22, waiting for transfers between devices, swap(): return lax.ppermute(value, 'tensor', [(i, i ^ mask) for i in range(8)])  25.4 us
    pallas_call x2, Pallas kernels, examples(): pl.pallas_call(kernel, grid=(1,), out_shape=[jax.ShapeDtypeStruct((HALF /...  5.1 us
    pallas_call x1, Pallas kernels, partial_scores(): pl.pallas_call(kernel, out_shape=jax.ShapeDtypeStruct((8 * SEGS, 16 * SEG...  2.2 us
  transfers between devices with their start and end apart: 24, of which 8 were waited for; matrix products, arithmetic and copies ran while one was open for 1% of the time, Pallas kernels for 32%

profile of v2, /device:TPU:0, one launch (start us, length us, event | category | flops | bytes accessed | tf_op | source)
XLA Modules:
  0.0 105.6 jit_solution(6491878241707973928)
XLA Ops:
  0.0 5.5 %first_outs.1 = (f32[4,64,512]{2,1,0:T(8,128)S(1)}, f32[4,64,512]{2,1,0:T(8,128)S(1)}) custom-call(s32[1]{0:T(128)} %bitcast.1.me_ref, bf16[64,1024]{1,0:T(8,128)(2,1)} %refs_0_.9, bf16[64,1024]{1,0:T(8,128)(2,1)} %refs_0_.9, bf16[1024,4096]{1,0:T(8,128)(2,1)} %refs_2_.4, bf16[1024,4096]{1,0:T(8,128)(2,1)} %refs_2_.5), custom_call_target="tpu_custom_call" | custom-call | flops 536870912 | bytes 8388608 | tf_op jit(solution)/shard_map/first_outs/pallas_call | solution.py:102
  5.5 3.0 %collective-permute-start = (f32[4,64,512]{2,1,0:T(8,128)S(1)}, f32[4,64,512]{2,1,0:T(8,128)S(1)}, u32[]{:S(2)}, u32[]{:S(2)}) collective-permute-start(f32[4,64,512]{2,1,0:T(8,128)S(1)} %get-tuple-element.65), channel_id=1, source_target_pairs={{0,2},{1,3},{2,0},{3,1},{4,6},{5,7},{6,4},{7,5},{8,10},{9,11},{10,... | collective-permute-start | bytes 1572872 | tf_op jit(solution)/shard_map/z1_qo/ppermute | solution.py:203
  8.5 6.4 %first_query_in.1 = f32[4,64,512]{2,1,0:T(8,128)S(1)} custom-call(s32[1]{0:T(128)} %bitcast.1.me_ref, bf16[64,3584]{1,0:T(8,128)(2,1)} %refs_1_.9, bf16[3584,4096]{1,0:T(8,128)(2,1)} %refs_3_.4), custom_call_target="tpu_custom_call" | custom-call | flops 939524096 | bytes 14680064 | tf_op jit(solution)/shard_map/first_query_in/pallas_call | solution.py:102
  14.9 1.6 %collective-permute-start.2 = (f32[4,64,512]{2,1,0:T(8,128)S(1)}, f32[4,64,512]{2,1,0:T(8,128)S(1)}, u32[]{:S(2)}, u32[]{:S(2)}) collective-permute-start(f32[4,64,512]{2,1,0:T(8,128)S(1)} %first_query_in.1), channel_id=1, source_target_pairs={{0,1},{1,0},{2,3},{3,2},{4,5},{5,4},{6,7},{7,6},{8,9},{9,8},{10,11... | collective-permute-start | bytes 1572872 | tf_op jit(solution)/shard_map/x_qi/ppermute | solution.py:203
  16.5 0.5 collective-permute-start.3
  17.0 7.9 %last_query.1 = (f32[4,64,512]{2,1,0:T(8,128)S(1)}, f32[4,64,512]{2,1,0:T(8,128)S(1)}) custom-call(s32[1]{0:T(128)} %bitcast.1.me_ref, bf16[64,1024]{1,0:T(8,128)(2,1)} %refs_0_.9, bf16[64,3584]{1,0:T(8,128)(2,1)} %refs_1_.9, bf16[1024,4096]{1,0:T(8,128)(2,1)} %refs_2_.4, bf16[3584,4096]{1,0:T(8,128)(2,1)} %refs_3_.4), custom_call_target="tpu_custom_call" | custom-call | flops 1207959552 | bytes 18874368 | tf_op jit(solution)/shard_map/last_query/pallas_call | solution.py:102
  24.9 0.0 collective-permute-done.refs_1_
  25.0 0.1 collective-permute-start.1
  25.1 6.8 %first_train_in.1 = f32[4,64,512]{2,1,0:T(8,128)S(1)} custom-call(s32[1]{0:T(128)} %bitcast.1.me_ref, bf16[64,3584]{1,0:T(8,128)(2,1)} %refs_1_.9, bf16[3584,4096]{1,0:T(8,128)(2,1)} %refs_3_.5), custom_call_target="tpu_custom_call" | custom-call | flops 939524096 | bytes 14680064 | tf_op jit(solution)/shard_map/first_train_in/pallas_call | solution.py:102
  31.9 1.7 %collective-permute-start.6 = (f32[4,64,512]{2,1,0:T(8,128)S(1)}, f32[4,64,512]{2,1,0:T(8,128)S(1)}, u32[]{:S(2)}, u32[]{:S(2)}) collective-permute-start(f32[4,64,512]{2,1,0:T(8,128)S(1)} %first_train_in.1), channel_id=1, source_target_pairs={{0,1},{1,0},{2,3},{3,2},{4,5},{5,4},{6,7},{7,6},{8,9},{9,8},{10,11... | collective-permute-start | bytes 1572872 | tf_op jit(solution)/shard_map/x_ti/ppermute | solution.py:203
  33.6 1.6 %collective-permute-start.4 = (f32[2,64,512]{2,1,0:T(8,128)S(1)}, f32[2,64,512]{2,1,0:T(8,128)S(1)}, u32[]{:S(2)}, u32[]{:S(2)}) collective-permute-start(f32[2,64,512]{2,1,0:T(8,128)S(1)} %slice_add_fusion.3), channel_id=1, source_target_pairs={{0,2},{1,3},{2,0},{3,1},{4,6},{5,7},{6,4},{7,5},{8,10},{9,11},{10,... | collective-permute-start | bytes 786440 | tf_op jit(solution)/shard_map/z1_qi/ppermute | solution.py:203
  35.2 0.0 collective-permute-done.1.refs_2_
  35.3 2.7 %collective-permute-start.5 = (f32[1,64,512]{2,1,0:T(8,128)S(1)}, f32[1,64,512]{2,1,0:T(8,128)S(1)}, u32[]{:S(2)}, u32[]{:S(2)}) collective-permute-start(f32[1,64,512]{2,1,0:T(8,128)S(1)} %slice_add_fusion.7), channel_id=1, source_target_pairs={{0,4},{1,5},{2,6},{3,7},{4,0},{5,1},{6,2},{7,3},{8,12},{9,13},{10,... | collective-permute-start | bytes 393224 | tf_op jit(solution)/shard_map/z2_qo/ppermute | solution.py:203
  37.9 7.9 %last_train.1 = (f32[4,64,512]{2,1,0:T(8,128)S(1)}, f32[4,64,512]{2,1,0:T(8,128)S(1)}) custom-call(s32[1]{0:T(128)} %bitcast.1.me_ref, bf16[64,1024]{1,0:T(8,128)(2,1)} %refs_0_.9, bf16[64,3584]{1,0:T(8,128)(2,1)} %refs_1_.9, bf16[1024,4096]{1,0:T(8,128)(2,1)} %refs_2_.5, bf16[3584,4096]{1,0:T(8,128)(2,1)} %refs_3_.5), custom_call_target="tpu_custom_call" | custom-call | flops 1207959552 | bytes 18874368 | tf_op jit(solution)/shard_map/last_train/pallas_call | solution.py:102
  45.9 0.0 collective-permute-done.3.refs_1_
  45.9 0.0 collective-permute-done.4.refs_6_
  46.0 0.9 slice_add_fusion
  46.9 0.9 collective-permute-start.9
  47.9 0.7 collective-permute-start.8
  48.6 2.6 %collective-permute-start.7 = (f32[1,64,512]{2,1,0:T(8,128)S(1)}, f32[1,64,512]{2,1,0:T(8,128)S(1)}, u32[]{:S(2)}, u32[]{:S(2)}) collective-permute-start(f32[1,64,512]{2,1,0:T(8,128)S(1)} %slice_add_fusion.6), channel_id=1, source_target_pairs={{0,4},{1,5},{2,6},{3,7},{4,0},{5,1},{6,2},{7,3},{8,12},{9,13},{10,... | collective-permute-start | bytes 393224 | tf_op jit(solution)/shard_map/z2_qi/ppermute | solution.py:203
  51.2 0.6 pad_add_fusion.place_ref
  51.8 3.7 %collective-permute-done.7.refs_7_ = f32[1,64,512]{2,1,0:T(8,128)S(1)} collective-permute-done((f32[1,64,512]{2,1,0:T(8,128)S(1)}, f32[1,64,512]{2,1,0:T(8,128)S(1)}, u32[]{:S(2)}, u32[]{:S(2)}) %collective-permute-start.7) | collective-permute-done | bytes 131104 | tf_op jit(solution)/shard_map/z2_qi/ppermute | solution.py:203
  55.5 0.6 copy-done.14
  56.1 2.5 %examples.2 = (f32[8,8,128]{2,1,0:T(8,128)}, f32[8,8,128]{2,1,0:T(8,128)}, f32[8,8,128]{2,1,0:T(8,128)}, f32[8,8,128]{2,1,0:T(8,128)}) custom-call(s32[4]{0:T(128)} %pad_add_fusion.place_ref, f32[4,64,512]{2,1,0:T(8,128)} %copy-done.2, f32[4,64,512]{2,1,0:T(8,128)} %copy-done.6, f32[2,64,512]{2,1,0:T(8,128)} %copy-done.10, f32[1,64,512]{2,1,0:T(8,128)} %copy-done.13, ...), custom_call_target="tpu_custom_call" | custom-call | tf_op jit(solution)/shard_map/examples/pallas_call | solution.py:157
  58.8 3.0 %collective-permute-start.11 = (f32[1,64,512]{2,1,0:T(8,128)S(1)}, f32[1,64,512]{2,1,0:T(8,128)S(1)}, u32[]{:S(2)}, u32[]{:S(2)}) collective-permute-start(f32[1,64,512]{2,1,0:T(8,128)S(1)} %slice_add_fusion.5), channel_id=1, source_target_pairs={{0,4},{1,5},{2,6},{3,7},{4,0},{5,1},{6,2},{7,3},{8,12},{9,13},{10,... | collective-permute-start | bytes 393224 | tf_op jit(solution)/shard_map/z2_to/ppermute | solution.py:203
  61.8 0.1 collective-permute-start.10
  61.9 4.1 %collective-permute-start.12 = (f32[8,8,128]{2,1,0:T(8,128)}, f32[8,8,128]{2,1,0:T(8,128)S(1)}, u32[]{:S(2)}, u32[]{:S(2)}) collective-permute-start(f32[8,8,128]{2,1,0:T(8,128)} %get-tuple-element.106), channel_id=1, source_target_pairs={{0,2},{1,3},{2,0},{3,1},{4,6},{5,7},{6,4},{7,5},{8,10},{9,11},{10,... | collective-permute-start | bytes 98312 | tf_op jit(solution)/shard_map/z_query/ppermute | solution.py:203
  66.0 0.1 collective-permute-start.13
  66.1 2.3 %collective-permute-start.14 = (f32[8,8,128]{2,1,0:T(8,128)}, f32[8,8,128]{2,1,0:T(8,128)S(1)}, u32[]{:S(2)}, u32[]{:S(2)}) collective-permute-start(f32[8,8,128]{2,1,0:T(8,128)} %get-tuple-element.108), channel_id=1, source_target_pairs={{0,6},{1,7},{2,4},{3,5},{4,2},{5,3},{6,0},{7,1},{8,14},{9,15},{10,... | collective-permute-start | bytes 98312 | tf_op jit(solution)/shard_map/z_query/ppermute | solution.py:203
  68.4 5.5 %collective-permute-done.13 = f32[8,8,128]{2,1,0:T(8,128)S(1)} collective-permute-done((f32[8,8,128]{2,1,0:T(8,128)}, f32[8,8,128]{2,1,0:T(8,128)S(1)}, u32[]{:S(2)}, u32[]{:S(2)}) %collective-permute-start.13) | collective-permute-done | bytes 32800 | tf_op jit(solution)/shard_map/z_query/ppermute | solution.py:203
  73.9 0.8 pad_maximum_fusion.refs_4_
  74.7 0.7 collective-permute-start.15
  75.4 2.6 %examples.3 = (f32[8,8,128]{2,1,0:T(8,128)}, f32[8,8,128]{2,1,0:T(8,128)}, f32[8,8,128]{2,1,0:T(8,128)}, f32[8,8,128]{2,1,0:T(8,128)}) custom-call(s32[4]{0:T(128)} %pad_add_fusion.place_ref, f32[4,64,512]{2,1,0:T(8,128)} %copy-done, f32[4,64,512]{2,1,0:T(8,128)} %copy-done.4, f32[2,64,512]{2,1,0:T(8,128)} %copy-done.8, f32[1,64,512]{2,1,0:T(8,128)} %copy-done.15, ...), custom_call_target="tpu_custom_call" | custom-call | tf_op jit(solution)/shard_map/examples/pallas_call | solution.py:157
  78.0 0.9 collective-permute-start.16
  78.9 2.2 %collective-permute-start.17 = (f32[8,8,128]{2,1,0:T(8,128)}, f32[8,8,128]{2,1,0:T(8,128)S(1)}, u32[]{:S(2)}, u32[]{:S(2)}) collective-permute-start(f32[8,8,128]{2,1,0:T(8,128)} %get-tuple-element.118), channel_id=1, source_target_pairs={{0,4},{1,5},{2,6},{3,7},{4,0},{5,1},{6,2},{7,3},{8,12},{9,13},{10,... | collective-permute-start | bytes 98312 | tf_op jit(solution)/shard_map/z_train/ppermute | solution.py:203
  81.1 1.2 %collective-permute-start.18 = (f32[8,8,128]{2,1,0:T(8,128)}, f32[8,8,128]{2,1,0:T(8,128)S(1)}, u32[]{:S(2)}, u32[]{:S(2)}) collective-permute-start(f32[8,8,128]{2,1,0:T(8,128)} %get-tuple-element.119), channel_id=1, source_target_pairs={{0,6},{1,7},{2,4},{3,5},{4,2},{5,3},{6,0},{7,1},{8,14},{9,15},{10,... | collective-permute-start | bytes 98312 | tf_op jit(solution)/shard_map/z_train/ppermute | solution.py:203
  82.4 2.1 %collective-permute-done.17.refs_2_ = f32[8,8,128]{2,1,0:T(8,128)S(1)} collective-permute-done((f32[8,8,128]{2,1,0:T(8,128)}, f32[8,8,128]{2,1,0:T(8,128)S(1)}, u32[]{:S(2)}, u32[]{:S(2)}) %collective-permute-start.17) | collective-permute-done | bytes 32800 | tf_op jit(solution)/shard_map/z_train/ppermute | solution.py:203
  84.5 2.5 %collective-permute-done.18.refs_3_ = f32[8,8,128]{2,1,0:T(8,128)S(1)} collective-permute-done((f32[8,8,128]{2,1,0:T(8,128)}, f32[8,8,128]{2,1,0:T(8,128)S(1)}, u32[]{:S(2)}, u32[]{:S(2)}) %collective-permute-start.18) | collective-permute-done | bytes 32800 | tf_op jit(solution)/shard_map/z_train/ppermute | solution.py:203
  87.1 0.1 collective-permute-start.20
  87.2 1.3 %collective-permute-done.20.refs_7_ = f32[4,8,8,128]{3,2,1,0:T(8,128)S(1)} collective-permute-done((f32[4,8,8,128]{3,2,1,0:T(8,128)S(1)}, f32[4,8,8,128]{3,2,1,0:T(8,128)S(1)}, u32[]{:S(2)}, u32[]{:S(2)}) %collective-permute-start.20) | collective-permute-done | bytes 131104 | tf_op jit(solution)/shard_map/dp_x_query/ppermute | solution.py:208
  88.5 0.6 copy-done.19
  89.2 2.2 %partial_scores.1 = f32[64,128]{1,0:T(8,128)} custom-call(s32[4]{0:T(128)} %pad_add_fusion.place_ref, f32[8,8,128]{2,1,0:T(8,128)} %get-tuple-element.120.refs_0_, f32[8,8,128]{2,1,0:T(8,128)} %copy-done.20, f32[8,8,128]{2,1,0:T(8,128)} %copy-done.21, f32[8,8,128]{2,1,0:T(8,128)} %copy-done.22, f32[4,8,8,128]{3,2,1,0:T(8,128)} %copy-done.12, ...), custom_call_target="tpu_custom_call" | custom-call | tf_op jit(solution)/shard_map/partial_scores/pallas_call | solution.py:188
  91.4 5.0 %collective-permute-done.21 = f32[64,128]{1,0:T(8,128)S(1)} collective-permute-done((f32[64,128]{1,0:T(8,128)}, f32[64,128]{1,0:T(8,128)S(1)}, u32[]{:S(2)}, u32[]{:S(2)}) %collective-permute-start.21) | collective-permute-done | bytes 32800 | tf_op jit(solution)/shard_map/scores/ppermute | solution.py:203
  96.4 0.8 add.63
  97.2 3.9 %collective-permute-done.22 = f32[64,128]{1,0:T(8,128)S(1)} collective-permute-done((f32[64,128]{1,0:T(8,128)S(1)}, f32[64,128]{1,0:T(8,128)S(1)}, u32[]{:S(2)}, u32[]{:S(2)}) %collective-permute-start.22) | collective-permute-done | bytes 32800 | tf_op jit(solution)/shard_map/scores/ppermute | solution.py:203
  101.1 1.3 %collective-permute-start.23 = (f32[64,128]{1,0:T(8,128)S(1)}, f32[64,128]{1,0:T(8,128)S(1)}, u32[]{:S(2)}, u32[]{:S(2)}) collective-permute-start(f32[64,128]{1,0:T(8,128)S(1)} %add.64), channel_id=1, source_target_pairs={{0,1},{1,0},{2,3},{3,2},{4,5},{5,4},{6,7},{7,6},{8,9},{9,8},{10,11... | collective-permute-start | bytes 98312 | tf_op jit(solution)/shard_map/scores/ppermute | solution.py:203
  102.4 2.6 %collective-permute-done.23 = f32[64,128]{1,0:T(8,128)S(1)} collective-permute-done((f32[64,128]{1,0:T(8,128)S(1)}, f32[64,128]{1,0:T(8,128)S(1)}, u32[]{:S(2)}, u32[]{:S(2)}) %collective-permute-start.23) | collective-permute-done | bytes 32800 | tf_op jit(solution)/shard_map/scores/ppermute | solution.py:203
  105.0 0.6 add.65
  (67 shorter events, 0.4 us)
Async XLA Ops:
  5.5 19.4 %collective-permute-start = (f32[4,64,512]{2,1,0:T(8,128)S(1)}, f32[4,64,512]{2,1,0:T(8,128)S(1)}, u32[]{:S(2)}, u32[]{:S(2)}) collective-permute-start(f32[4,64,512]{2,1,0:T(8,128)S(1)} %get-tuple-element.65), channel_id=1, source_target_pairs={{0,2},{1,3},{2,0},{3,1},{4,6},{5,7},{6,4},{7,5},{8,10},{9,11},{10,... | collective-permute-start | bytes 1572872 | tf_op jit(solution)/shard_map/z1_qo/ppermute | solution.py:203
  14.9 18.6 %collective-permute-start.2 = (f32[4,64,512]{2,1,0:T(8,128)S(1)}, f32[4,64,512]{2,1,0:T(8,128)S(1)}, u32[]{:S(2)}, u32[]{:S(2)}) collective-permute-start(f32[4,64,512]{2,1,0:T(8,128)S(1)} %first_query_in.1), channel_id=1, source_target_pairs={{0,1},{1,0},{2,3},{3,2},{4,5},{5,4},{6,7},{7,6},{8,9},{9,8},{10,11... | collective-permute-start | bytes 1572872 | tf_op jit(solution)/shard_map/x_qi/ppermute | solution.py:203
  16.5 29.4 %collective-permute-start.3 = (f32[4,64,512]{2,1,0:T(8,128)S(1)}, f32[4,64,512]{2,1,0:T(8,128)S(1)}, u32[]{:S(2)}, u32[]{:S(2)}) collective-permute-start(f32[4,64,512]{2,1,0:T(8,128)S(1)} %get-tuple-element.80), channel_id=1, source_target_pairs={{0,2},{1,3},{2,0},{3,1},{4,6},{5,7},{6,4},{7,5},{8,10},{9,11},{10,... | collective-permute-start | bytes 1572872 | tf_op jit(solution)/shard_map/z1_to/ppermute | solution.py:203
  24.9 21.0 %copy-start.2 = (f32[4,64,512]{2,1,0:T(8,128)}, f32[4,64,512]{2,1,0:T(8,128)S(1)}, u32[]{:S(2)}) copy-start(f32[4,64,512]{2,1,0:T(8,128)S(1)} %get-tuple-element.73.refs_0_) | copy-start | bytes 1572868
  24.9 22.0 %copy-start.3 = (f32[4,64,512]{2,1,0:T(8,128)}, f32[4,64,512]{2,1,0:T(8,128)S(1)}, u32[]{:S(2)}) copy-start(f32[4,64,512]{2,1,0:T(8,128)S(1)} %get-tuple-element.85.refs_4_) | copy-start | bytes 1572868
  24.9 20.9 %copy-start.6 = (f32[4,64,512]{2,1,0:T(8,128)}, f32[4,64,512]{2,1,0:T(8,128)S(1)}, u32[]{:S(2)}) copy-start(f32[4,64,512]{2,1,0:T(8,128)S(1)} %collective-permute-done.refs_1_) | copy-start | bytes 1572868
  25.0 10.2 %collective-permute-start.1 = (f32[2,64,512]{2,1,0:T(8,128)S(1)}, f32[2,64,512]{2,1,0:T(8,128)S(1)}, u32[]{:S(2)}, u32[]{:S(2)}) collective-permute-start(f32[2,64,512]{2,1,0:T(8,128)S(1)} %slice_add_fusion.1), channel_id=1, source_target_pairs={{0,1},{1,0},{2,3},{3,2},{4,5},{5,4},{6,7},{7,6},{8,9},{9,8},{10,11... | collective-permute-start | bytes 786440 | tf_op jit(solution)/shard_map/x_qo/ppermute | solution.py:203
  31.9 14.1 %collective-permute-start.6 = (f32[4,64,512]{2,1,0:T(8,128)S(1)}, f32[4,64,512]{2,1,0:T(8,128)S(1)}, u32[]{:S(2)}, u32[]{:S(2)}) collective-permute-start(f32[4,64,512]{2,1,0:T(8,128)S(1)} %first_train_in.1), channel_id=1, source_target_pairs={{0,1},{1,0},{2,3},{3,2},{4,5},{5,4},{6,7},{7,6},{8,9},{9,8},{10,11... | collective-permute-start | bytes 1572872 | tf_op jit(solution)/shard_map/x_ti/ppermute | solution.py:203
  33.6 13.3 %copy-start.7 = (f32[4,64,512]{2,1,0:T(8,128)}, f32[4,64,512]{2,1,0:T(8,128)S(1)}, u32[]{:S(2)}) copy-start(f32[4,64,512]{2,1,0:T(8,128)S(1)} %collective-permute-done.2.refs_5_) | copy-start | bytes 1572868
  33.6 12.3 %collective-permute-start.4 = (f32[2,64,512]{2,1,0:T(8,128)S(1)}, f32[2,64,512]{2,1,0:T(8,128)S(1)}, u32[]{:S(2)}, u32[]{:S(2)}) collective-permute-start(f32[2,64,512]{2,1,0:T(8,128)S(1)} %slice_add_fusion.3), channel_id=1, source_target_pairs={{0,2},{1,3},{2,0},{3,1},{4,6},{5,7},{6,4},{7,5},{8,10},{9,11},{10,... | collective-permute-start | bytes 786440 | tf_op jit(solution)/shard_map/z1_qi/ppermute | solution.py:203
  35.2 20.3 %copy-start.10 = (f32[2,64,512]{2,1,0:T(8,128)}, f32[2,64,512]{2,1,0:T(8,128)S(1)}, u32[]{:S(2)}) copy-start(f32[2,64,512]{2,1,0:T(8,128)S(1)} %collective-permute-done.1.refs_2_) | copy-start | bytes 786436
  35.3 10.7 %collective-permute-start.5 = (f32[1,64,512]{2,1,0:T(8,128)S(1)}, f32[1,64,512]{2,1,0:T(8,128)S(1)}, u32[]{:S(2)}, u32[]{:S(2)}) collective-permute-start(f32[1,64,512]{2,1,0:T(8,128)S(1)} %slice_add_fusion.7), channel_id=1, source_target_pairs={{0,4},{1,5},{2,6},{3,7},{4,0},{5,1},{6,2},{7,3},{8,12},{9,13},{10,... | collective-permute-start | bytes 393224 | tf_op jit(solution)/shard_map/z2_qo/ppermute | solution.py:203
  45.9 29.5 %copy-start = (f32[4,64,512]{2,1,0:T(8,128)}, f32[4,64,512]{2,1,0:T(8,128)S(1)}, u32[]{:S(2)}) copy-start(f32[4,64,512]{2,1,0:T(8,128)S(1)} %get-tuple-element.98.refs_0_) | copy-start | bytes 1572868
  45.9 29.5 %copy-start.1 = (f32[4,64,512]{2,1,0:T(8,128)}, f32[4,64,512]{2,1,0:T(8,128)S(1)}, u32[]{:S(2)}) copy-start(f32[4,64,512]{2,1,0:T(8,128)S(1)} %get-tuple-element.84.refs_4_) | copy-start | bytes 1572868
  45.9 29.5 %copy-start.4 = (f32[4,64,512]{2,1,0:T(8,128)}, f32[4,64,512]{2,1,0:T(8,128)S(1)}, u32[]{:S(2)}) copy-start(f32[4,64,512]{2,1,0:T(8,128)S(1)} %collective-permute-done.3.refs_1_) | copy-start | bytes 1572868
  45.9 1.0 copy-start.11
  45.9 9.5 %copy-start.13 = (f32[1,64,512]{2,1,0:T(8,128)}, f32[1,64,512]{2,1,0:T(8,128)S(1)}, u32[]{:S(2)}) copy-start(f32[1,64,512]{2,1,0:T(8,128)S(1)} %collective-permute-done.5.refs_3_) | copy-start | bytes 393220
  46.0 29.4 %copy-start.5 = (f32[4,64,512]{2,1,0:T(8,128)}, f32[4,64,512]{2,1,0:T(8,128)S(1)}, u32[]{:S(2)}) copy-start(f32[4,64,512]{2,1,0:T(8,128)S(1)} %collective-permute-done.6.refs_5_) | copy-start | bytes 1572868
  46.9 11.7 %collective-permute-start.9 = (f32[2,64,512]{2,1,0:T(8,128)S(1)}, f32[2,64,512]{2,1,0:T(8,128)S(1)}, u32[]{:S(2)}, u32[]{:S(2)}) collective-permute-start(f32[2,64,512]{2,1,0:T(8,128)S(1)} %slice_add_fusion.2), channel_id=1, source_target_pairs={{0,1},{1,0},{2,3},{3,2},{4,5},{5,4},{6,7},{7,6},{8,9},{9,8},{10,11... | collective-permute-start | bytes 786440 | tf_op jit(solution)/shard_map/x_to/ppermute | solution.py:203
  47.9 10.8 %collective-permute-start.8 = (f32[2,64,512]{2,1,0:T(8,128)}, f32[2,64,512]{2,1,0:T(8,128)S(1)}, u32[]{:S(2)}, u32[]{:S(2)}) collective-permute-start(f32[2,64,512]{2,1,0:T(8,128)} %slice_add_fusion), channel_id=1, source_target_pairs={{0,2},{1,3},{2,0},{3,1},{4,6},{5,7},{6,4},{7,5},{8,10},{9,11},{10,... | collective-permute-start | bytes 786440 | tf_op jit(solution)/shard_map/z1_ti/ppermute | solution.py:203
  48.6 6.9 %collective-permute-start.7 = (f32[1,64,512]{2,1,0:T(8,128)S(1)}, f32[1,64,512]{2,1,0:T(8,128)S(1)}, u32[]{:S(2)}, u32[]{:S(2)}) collective-permute-start(f32[1,64,512]{2,1,0:T(8,128)S(1)} %slice_add_fusion.6), channel_id=1, source_target_pairs={{0,4},{1,5},{2,6},{3,7},{4,0},{5,1},{6,2},{7,3},{8,12},{9,13},{10,... | collective-permute-start | bytes 393224 | tf_op jit(solution)/shard_map/z2_qi/ppermute | solution.py:203
  55.5 0.7 copy-start.14
  58.7 16.7 %copy-start.8 = (f32[2,64,512]{2,1,0:T(8,128)}, f32[2,64,512]{2,1,0:T(8,128)S(1)}, u32[]{:S(2)}) copy-start(f32[2,64,512]{2,1,0:T(8,128)S(1)} %collective-permute-done.9.refs_2_) | copy-start | bytes 786436
  58.7 16.7 %copy-start.9 = (f32[2,64,512]{2,1,0:T(8,128)}, f32[2,64,512]{2,1,0:T(8,128)S(1)}, u32[]{:S(2)}) copy-start(f32[2,64,512]{2,1,0:T(8,128)S(1)} %collective-permute-done.8.refs_6_) | copy-start | bytes 786436
  58.8 15.1 %collective-permute-start.11 = (f32[1,64,512]{2,1,0:T(8,128)S(1)}, f32[1,64,512]{2,1,0:T(8,128)S(1)}, u32[]{:S(2)}, u32[]{:S(2)}) collective-permute-start(f32[1,64,512]{2,1,0:T(8,128)S(1)} %slice_add_fusion.5), channel_id=1, source_target_pairs={{0,4},{1,5},{2,6},{3,7},{4,0},{5,1},{6,2},{7,3},{8,12},{9,13},{10,... | collective-permute-start | bytes 393224 | tf_op jit(solution)/shard_map/z2_to/ppermute | solution.py:203
  61.8 12.1 %collective-permute-start.10 = (f32[1,64,512]{2,1,0:T(8,128)S(1)}, f32[1,64,512]{2,1,0:T(8,128)S(1)}, u32[]{:S(2)}, u32[]{:S(2)}) collective-permute-start(f32[1,64,512]{2,1,0:T(8,128)S(1)} %fusion), channel_id=1, source_target_pairs={{0,4},{1,5},{2,6},{3,7},{4,0},{5,1},{6,2},{7,3},{8,12},{9,13},{10,... | collective-permute-start | bytes 393224 | tf_op jit(solution)/shard_map/z2_ti/ppermute | solution.py:203
  61.9 6.5 %collective-permute-start.12 = (f32[8,8,128]{2,1,0:T(8,128)}, f32[8,8,128]{2,1,0:T(8,128)S(1)}, u32[]{:S(2)}, u32[]{:S(2)}) collective-permute-start(f32[8,8,128]{2,1,0:T(8,128)} %get-tuple-element.106), channel_id=1, source_target_pairs={{0,2},{1,3},{2,0},{3,1},{4,6},{5,7},{6,4},{7,5},{8,10},{9,11},{10,... | collective-permute-start | bytes 98312 | tf_op jit(solution)/shard_map/z_query/ppermute | solution.py:203
  66.0 7.8 %collective-permute-start.13 = (f32[8,8,128]{2,1,0:T(8,128)}, f32[8,8,128]{2,1,0:T(8,128)S(1)}, u32[]{:S(2)}, u32[]{:S(2)}) collective-permute-start(f32[8,8,128]{2,1,0:T(8,128)} %get-tuple-element.107), channel_id=1, source_target_pairs={{0,4},{1,5},{2,6},{3,7},{4,0},{5,1},{6,2},{7,3},{8,12},{9,13},{10,... | collective-permute-start | bytes 98312 | tf_op jit(solution)/shard_map/z_query/ppermute | solution.py:203
  66.1 7.8 %collective-permute-start.14 = (f32[8,8,128]{2,1,0:T(8,128)}, f32[8,8,128]{2,1,0:T(8,128)S(1)}, u32[]{:S(2)}, u32[]{:S(2)}) collective-permute-start(f32[8,8,128]{2,1,0:T(8,128)} %get-tuple-element.108), channel_id=1, source_target_pairs={{0,6},{1,7},{2,4},{3,5},{4,2},{5,3},{6,0},{7,1},{8,14},{9,15},{10,... | collective-permute-start | bytes 98312 | tf_op jit(solution)/shard_map/z_query/ppermute | solution.py:203
  73.9 1.6 %copy-start.15 = (f32[1,64,512]{2,1,0:T(8,128)}, f32[1,64,512]{2,1,0:T(8,128)S(1)}, u32[]{:S(2)}) copy-start(f32[1,64,512]{2,1,0:T(8,128)S(1)} %collective-permute-done.11.refs_3_) | copy-start | bytes 393220
  73.9 1.6 %copy-start.16 = (f32[1,64,512]{2,1,0:T(8,128)}, f32[1,64,512]{2,1,0:T(8,128)S(1)}, u32[]{:S(2)}) copy-start(f32[1,64,512]{2,1,0:T(8,128)S(1)} %collective-permute-done.10.refs_7_) | copy-start | bytes 393220
  74.7 13.8 %copy-start.12 = (f32[4,8,8,128]{3,2,1,0:T(8,128)}, f32[4,8,8,128]{3,2,1,0:T(8,128)S(1)}, u32[]{:S(2)}) copy-start(f32[4,8,8,128]{3,2,1,0:T(8,128)S(1)} %pad_maximum_fusion.refs_4_) | copy-start | bytes 393220
  74.7 12.4 %collective-permute-start.15 = (f32[4,8,8,128]{3,2,1,0:T(8,128)S(1)}, f32[4,8,8,128]{3,2,1,0:T(8,128)S(1)}, u32[]{:S(2)}, u32[]{:S(2)}) collective-permute-start(f32[4,8,8,128]{3,2,1,0:T(8,128)S(1)} %pad_maximum_fusion.refs_4_), channel_id=1, source_target_pairs={{0,1},{1,0},{2,3},{3,2},{4,5},{5,4},{6,7},{7,6},{8,9},{9,8},{10,11... | collective-permute-start | bytes 393224 | tf_op jit(solution)/shard_map/x_query/ppermute | solution.py:203
  78.0 4.4 %collective-permute-start.16 = (f32[8,8,128]{2,1,0:T(8,128)}, f32[8,8,128]{2,1,0:T(8,128)S(1)}, u32[]{:S(2)}, u32[]{:S(2)}) collective-permute-start(f32[8,8,128]{2,1,0:T(8,128)} %get-tuple-element.117), channel_id=1, source_target_pairs={{0,2},{1,3},{2,0},{3,1},{4,6},{5,7},{6,4},{7,5},{8,10},{9,11},{10,... | collective-permute-start | bytes 98312 | tf_op jit(solution)/shard_map/z_train/ppermute | solution.py:203
  78.9 5.6 %collective-permute-start.17 = (f32[8,8,128]{2,1,0:T(8,128)}, f32[8,8,128]{2,1,0:T(8,128)S(1)}, u32[]{:S(2)}, u32[]{:S(2)}) collective-permute-start(f32[8,8,128]{2,1,0:T(8,128)} %get-tuple-element.118), channel_id=1, source_target_pairs={{0,4},{1,5},{2,6},{3,7},{4,0},{5,1},{6,2},{7,3},{8,12},{9,13},{10,... | collective-permute-start | bytes 98312 | tf_op jit(solution)/shard_map/z_train/ppermute | solution.py:203
  81.1 5.9 %collective-permute-start.18 = (f32[8,8,128]{2,1,0:T(8,128)}, f32[8,8,128]{2,1,0:T(8,128)S(1)}, u32[]{:S(2)}, u32[]{:S(2)}) collective-permute-start(f32[8,8,128]{2,1,0:T(8,128)} %get-tuple-element.119), channel_id=1, source_target_pairs={{0,6},{1,7},{2,4},{3,5},{4,2},{5,3},{6,0},{7,1},{8,14},{9,15},{10,... | collective-permute-start | bytes 98312 | tf_op jit(solution)/shard_map/z_train/ppermute | solution.py:203
  82.4 4.8 %collective-permute-start.19 = (f32[4,8,8,128]{3,2,1,0:T(8,128)S(1)}, f32[4,8,8,128]{3,2,1,0:T(8,128)S(1)}, u32[]{:S(2)}, u32[]{:S(2)}) collective-permute-start(f32[4,8,8,128]{3,2,1,0:T(8,128)S(1)} %pad_maximum_fusion.refs_4_), channel_id=1, source_target_pairs={{0,8},{8,0},{1,9},{9,1},{2,10},{10,2},{3,11},{11,3},{4,12},{12,4},... | collective-permute-start | bytes 393224 | tf_op jit(solution)/shard_map/dp_query/ppermute | solution.py:208
  82.4 6.1 %copy-start.20 = (f32[8,8,128]{2,1,0:T(8,128)}, f32[8,8,128]{2,1,0:T(8,128)S(1)}, u32[]{:S(2)}) copy-start(f32[8,8,128]{2,1,0:T(8,128)S(1)} %collective-permute-done.16.refs_1_) | copy-start | bytes 98308
  84.5 4.0 %copy-start.21 = (f32[8,8,128]{2,1,0:T(8,128)}, f32[8,8,128]{2,1,0:T(8,128)S(1)}, u32[]{:S(2)}) copy-start(f32[8,8,128]{2,1,0:T(8,128)S(1)} %collective-permute-done.17.refs_2_) | copy-start | bytes 98308
  87.1 1.4 %copy-start.22 = (f32[8,8,128]{2,1,0:T(8,128)}, f32[8,8,128]{2,1,0:T(8,128)S(1)}, u32[]{:S(2)}) copy-start(f32[8,8,128]{2,1,0:T(8,128)S(1)} %collective-permute-done.18.refs_3_) | copy-start | bytes 98308
  87.1 1.4 %copy-start.17 = (f32[4,8,8,128]{3,2,1,0:T(8,128)}, f32[4,8,8,128]{3,2,1,0:T(8,128)S(1)}, u32[]{:S(2)}) copy-start(f32[4,8,8,128]{3,2,1,0:T(8,128)S(1)} %collective-permute-done.15.refs_5_) | copy-start | bytes 393220
  87.1 1.4 %collective-permute-start.20 = (f32[4,8,8,128]{3,2,1,0:T(8,128)S(1)}, f32[4,8,8,128]{3,2,1,0:T(8,128)S(1)}, u32[]{:S(2)}, u32[]{:S(2)}) collective-permute-start(f32[4,8,8,128]{3,2,1,0:T(8,128)S(1)} %collective-permute-done.15.refs_5_), channel_id=1, source_target_pairs={{0,8},{8,0},{1,9},{9,1},{2,10},{10,2},{3,11},{11,3},{4,12},{12,4},... | collective-permute-start | bytes 393224 | tf_op jit(solution)/shard_map/dp_x_query/ppermute | solution.py:208
  87.2 1.4 %copy-start.18 = (f32[4,8,8,128]{3,2,1,0:T(8,128)}, f32[4,8,8,128]{3,2,1,0:T(8,128)S(1)}, u32[]{:S(2)}) copy-start(f32[4,8,8,128]{3,2,1,0:T(8,128)S(1)} %collective-permute-done.19.refs_6_) | copy-start | bytes 393220
  88.5 0.6 copy-start.19
  91.4 5.0 %collective-permute-start.21 = (f32[64,128]{1,0:T(8,128)}, f32[64,128]{1,0:T(8,128)S(1)}, u32[]{:S(2)}, u32[]{:S(2)}) collective-permute-start(f32[64,128]{1,0:T(8,128)} %partial_scores.1), channel_id=1, source_target_pairs={{0,4},{1,5},{2,6},{3,7},{4,0},{5,1},{6,2},{7,3},{8,12},{9,13},{10,... | collective-permute-start | bytes 98312 | tf_op jit(solution)/shard_map/scores/ppermute | solution.py:203
  97.2 3.9 %collective-permute-start.22 = (f32[64,128]{1,0:T(8,128)S(1)}, f32[64,128]{1,0:T(8,128)S(1)}, u32[]{:S(2)}, u32[]{:S(2)}) collective-permute-start(f32[64,128]{1,0:T(8,128)S(1)} %add.63), channel_id=1, source_target_pairs={{0,2},{1,3},{2,0},{3,1},{4,6},{5,7},{6,4},{7,5},{8,10},{9,11},{10,... | collective-permute-start | bytes 98312 | tf_op jit(solution)/shard_map/scores/ppermute | solution.py:203
  101.1 3.9 %collective-permute-start.23 = (f32[64,128]{1,0:T(8,128)S(1)}, f32[64,128]{1,0:T(8,128)S(1)}, u32[]{:S(2)}, u32[]{:S(2)}) collective-permute-start(f32[64,128]{1,0:T(8,128)S(1)} %add.64), channel_id=1, source_target_pairs={{0,1},{1,0},{2,3},{3,2},{4,5},{5,4},{6,7},{7,6},{8,9},{9,8},{10,11... | collective-permute-start | bytes 98312 | tf_op jit(solution)/shard_map/scores/ppermute | solution.py:203

commit v3 on v2

--- a/solution.py
+++ b/solution.py
@@ -14,7 +14,7 @@
 Z_FIRST = (0, Z2, X, X | Z2, Z1, Z1 | Z2, Z1 | X, X | Z1 | Z2)
 AHEAD = 7 * 1024 * 1024
 LIGHT = 1
-VMEM = 56 * 1024 * 1024
+VMEM = 26 * 1024 * 1024
 
 
 def example_grads(proj_out, proj_in, slot_ids):
@@ -115,7 +115,15 @@
             flops=moved * RANK // LIGHT, bytes_accessed=moved // LIGHT, transcendentals=0
         ),
         name=name,
-    )(me, *[basis for basis, _ in sources], *[data for _, data in sources])
+    )(me, *[far(basis) for basis, _ in sources], *[far(data) for _, data in sources])
+
+
+def far(value):
+    return pltpu.with_memory_space_constraint(value, pltpu.HBM)
+
+
+def near(value):
+    return pltpu.with_memory_space_constraint(value, pltpu.VMEM)
 
 
 def two(x):
@@ -132,10 +140,10 @@
 
 def examples(place, outs, inners, slots):
     def kernel(place_ref, *refs):
-        slot_ref, ex_refs, held = refs[8], refs[9:13], refs[13]
+        slot_ref, ex_refs, held = refs[4], refs[5:9], refs[9]
         z, me = place_ref[0], place_ref[1]
-        out = (refs[0][0] + refs[1][0]) + (refs[2][0] + refs[3][0])
-        inner = (refs[4][0] + refs[5][0]) + (refs[6][0] + refs[7][0])
+        out = refs[0][0] + refs[1][0]
+        inner = refs[2][0] + refs[3][0]
         seg = lax.broadcasted_iota(jnp.int32, (SEGS, BLK), 0)
         mask = (slot_ref[me] == seg).astype(jnp.float32)
         counts = jnp.maximum(jnp.sum(mask, axis=1, keepdims=True), 1.0)
@@ -153,18 +161,16 @@
             ex_refs[k][...] = held[k ^ z]
 
     blocks = slots.shape[0] // BLK
-    first = pl.BlockSpec((1, RANK, BLK), lambda i: (0, 0, 0))
+    vmem = pl.BlockSpec(memory_space=pltpu.VMEM)
     return pl.pallas_call(
         kernel,
-        grid=(1,),
-        out_shape=[jax.ShapeDtypeStruct((HALF // 4, SEGS, 2 * RANK), jnp.float32)] * 4,
-        in_specs=[pl.BlockSpec(memory_space=pltpu.SMEM)]
-        + [first] * 8
-        + [pl.BlockSpec((blocks, 1, BLK), lambda i: (0, 0, 0))],
-        out_specs=[pl.BlockSpec((HALF // 4, SEGS, 2 * RANK), lambda i: (0, 0, 0))] * 4,
+        out_shape=[pltpu.VMEM((HALF // 4, SEGS, 2 * RANK), jnp.float32)] * 4,
+        in_specs=[pl.BlockSpec(memory_space=pltpu.SMEM)] + [vmem] * 5,
+        out_specs=[vmem] * 4,
         scratch_shapes=[pltpu.VMEM((4, HALF // 4, SEGS, 2 * RANK), jnp.float32)],
+        cost_estimate=pl.CostEstimate(flops=1, bytes_accessed=1, transcendentals=0),
         name="examples",
-    )(place, *outs, *inners, slots.reshape(blocks, 1, BLK))
+    )(place, *map(near, (*outs, *inners, slots.reshape(blocks, 1, BLK))))
 
 
 def partial_scores(place, trains, queries):
@@ -187,7 +193,7 @@
 
     return pl.pallas_call(
         kernel,
-        out_shape=jax.ShapeDtypeStruct((8 * SEGS, 16 * SEGS), jnp.float32),
+        out_shape=pltpu.VMEM((8 * SEGS, 16 * SEGS), jnp.float32),
         in_specs=[pl.BlockSpec(memory_space=pltpu.SMEM)] + [pl.BlockSpec(memory_space=pltpu.VMEM)] * 8,
         out_specs=pl.BlockSpec(memory_space=pltpu.VMEM),
         scratch_shapes=[
@@ -195,7 +201,7 @@
             pltpu.VMEM((4, HALF // 4, SEGS, 2 * RANK), jnp.float32),
         ],
         name="partial_scores",
-    )(place, *trains, *queries)
+    )(place, *map(near, (*trains, *queries)))
 
 
 def swap(value, mask, name):
@@ -230,44 +236,54 @@
     qi1 = swap(qi_send, X, "x_qi")
     to1 = swap(to_send, Z1, "z1_to")
     me = after(me, qi_send)
-    qo, qi = project(me, [outs, ins], [(0, Z_FIRST[:4]), (1, X_FIRST[:4])], "last_query")
+    qo, ti_send = project(me, [outs, train_ins], [(0, Z_FIRST[:4]), (1, X_FIRST[4:])], "middle_a")
     qo_send = qo[2:] + qo1[2:]
+    ti_send = after(ti_send, qo_send)
     qo2 = swap(qo_send, X, "x_qo")
-    me = after(me, qo_send)
-    (ti_send,) = project(me, [train_ins], [(0, X_FIRST[4:])], "first_train_in")
     ti1 = swap(ti_send, X, "x_ti")
-    qi, qi1, _ = lax.optimization_barrier((qi, qi1, ti_send))
+    me = after(me, qo_send, ti_send)
+    to, qi = project(me, [train_outs, ins], [(0, Z_FIRST[:4]), (1, X_FIRST[:4])], "middle_b")
     qi_send = qi[2:] + qi1[2:]
     qi2 = swap(qi_send, Z1, "z1_qi")
     qo, qo1, qo2, _ = lax.optimization_barrier((qo, qo1, qo2, qi_send))
     qo_send = qo[1:2] + qo1[1:2] + qo2[1:2]
     qo3 = swap(qo_send, Z2, "z2_qo")
-    me = after(me, qo_send)
-    to, ti = project(me, [train_outs, train_ins], [(0, Z_FIRST[:4]), (1, X_FIRST[:4])], "last_train")
-    to, ti, to1, qi2, qo3 = lax.optimization_barrier((to, ti, to1, qi2, qo3))
-    ti_send = ti[2:] + ti1[2:]
+    to, to1, _ = lax.optimization_barrier((to, to1, qo_send))
+    to_send = to[2:] + to1[2:]
+    to2 = swap(to_send, X, "x_to")
+    qo = qo[:1] + qo1[:1] + qo2[:1]
+    me = after(me, to_send, qo)
+    (ti_late,) = project(me, [train_ins], [(0, X_FIRST[2:4])], "last_train_in_a")
+    ti_late, qi2, ti1 = lax.optimization_barrier((ti_late, qi2, ti1))
+    ti_send = ti_late + ti1[2:]
     ti2 = swap(ti_send, Z1, "z1_ti")
     qi, qi1, qi2, _ = lax.optimization_barrier((qi, qi1, qi2, ti_send))
     qi_send = qi[1:2] + qi1[1:2] + qi2[1:2]
     qi3 = swap(qi_send, Z2, "z2_qi")
-    to, to1, _ = lax.optimization_barrier((to, to1, qi_send))
-    to_send = to[2:] + to1[2:]
-    to2 = swap(to_send, X, "x_to")
-    place = after(place, to_send)
-    query = examples(place, (qo, qo1, qo2, qo3), (qi, qi1, qi2, qi3), query_slots)
-    query, ti2, to2, _ = lax.optimization_barrier((query, ti2, to2, query[0]))
+    me = after(me, qi_send)
+    (ti,) = project(me, [train_ins], [(0, X_FIRST[:2])], "last_train_in_b")
+    ti, qo3 = lax.optimization_barrier((ti, qo3))
+    qi, qi1, qi2, _ = lax.optimization_barrier((qi, qi1, qi2, ti))
+    qi = qi[:1] + qi1[:1] + qi2[:1]
+    to, to1, to2, _ = lax.optimization_barrier((to, to1, to2, qi))
+    to_send = to[1:2] + to1[1:2] + to2[1:2]
+    to3 = swap(to_send, Z2, "z2_to")
+    to, to1, to2, ti2, _ = lax.optimization_barrier((to, to1, to2, ti2, to_send))
+    to = to[:1] + to1[:1] + to2[:1]
+    place = after(place, to)
+    query = examples(place, (qo, qo3), (qi, qi3), query_slots)
+    query, ti2, _ = lax.optimization_barrier((query, ti2, query[0]))
     ti_send = ti[1:2] + ti1[1:2] + ti2[1:2]
     ti3 = swap(ti_send, Z2, "z2_ti")
-    to, to1, to2, _ = lax.optimization_barrier((to, to1, to2, ti_send))
-    to_send = to[1:2] + to1[1:2] + to2[1:2]
-    to3 = swap(to_send, Z2, "z2_to")
-    query = lax.optimization_barrier((*query, to_send))[:4]
-    query = [query[0]] + [swap(query[k], 2 * k, "z_query") for k in (1, 2, 3)]
+    ti, ti1, ti2, _ = lax.optimization_barrier((ti, ti1, ti2, ti_send))
+    ti = ti[:1] + ti1[:1] + ti2[:1]
+    query = lax.optimization_barrier((*query, ti_send))[:4]
+    query = [query[0]] + [swap(query[k], 2 * k, "z_query") for k in (3, 2, 1)][::-1]
     place, ti3, to3, *query = lax.optimization_barrier((place, ti3, to3, *query))
-    train = examples(place, (to, to1, to2, to3), (ti, ti1, ti2, ti3), train_slots)
+    train = examples(place, (to, to3), (ti, ti3), train_slots)
     query = jnp.stack(query)
     other = swap(query, X, "x_query")
-    trains = [train[0]] + [swap(train[k], 2 * k, "z_train") for k in (1, 2, 3)]
+    trains = [train[0]] + [swap(train[k], 2 * k, "z_train") for k in (3, 2, 1)][::-1]
     other, *trains = lax.optimization_barrier((other, *trains))
     queries = [query, other, cross(query, "dp_query"), cross(other, "dp_x_query")]
     scores = partial_scores(place, trains, queries)

time: 106 us -> 96 us (0.906)
  starting transfers between devices: 31.5 us -> 29 us
  Pallas kernels: 41.8 us -> 39.4 us
  other arithmetic: 3.87 us -> 1.71 us
  waiting for transfers between devices: 26.7 us -> 24.8 us
    pallas_call x3, Pallas kernels: 7.3 us -> 3.57 us  [the longest x2 2.53 us: examples(): pl.pallas_call(kernel, out_shape=[pltpu.VMEM((HALF // 4, SEGS, 2 * RANK),...]
    ppermute x22, starting transfers between devices: 31.4 us -> 29 us  [swap(): return lax.ppermute(value, 'tensor', [(i, i ^ mask) for i in range(8)])]
    ppermute x22, waiting for transfers between devices: 25.4 us -> 23.5 us  [swap(): return lax.ppermute(value, 'tensor', [(i, i ^ mask) for i in range(8)])]
    pallas_call x5 -> x6, Pallas kernels: 34.5 us -> 35.9 us  [project(): pl.pallas_call(kernel, out_shape=[pltpu.VMEM((len(masks), RANK, BLK), jnp...]
  transfers between devices with their start and end apart: 24 -> 24, of which waited for: 8 -> 11; matrix products, arithmetic and copies ran while one was open for 1% -> 1% of each run, Pallas kernels for 32% -> 34%
where the time goes in v3:
time: 96 us; the launch traced here: 95.8 us
  Pallas kernels  39.4 us (41%)
  starting transfers between devices  29 us (30%)
  waiting for transfers between devices  24.8 us (26%)
  other arithmetic  1.71 us (2%)
    pallas_call x6, Pallas kernels, project(): pl.pallas_call(kernel, out_shape=[pltpu.VMEM((len(masks), RANK, BLK), jnp...  35.9 us
    ppermute x22, starting transfers between devices, swap(): return lax.ppermute(value, 'tensor', [(i, i ^ mask) for i in range(8)])  29 us
    ppermute x22, waiting for transfers between devices, swap(): return lax.ppermute(value, 'tensor', [(i, i ^ mask) for i in range(8)])  23.5 us
    pallas_call x2, Pallas kernels, examples(): pl.pallas_call(kernel, out_shape=[pltpu.VMEM((HALF // 4, SEGS, 2 * RANK),...  2.53 us
  transfers between devices with their start and end apart: 24, of which 11 were waited for; matrix products, arithmetic and copies ran while one was open for 1% of the time, Pallas kernels for 34%

profile of v3, /device:TPU:0, one launch (start us, length us, event | category | flops | bytes accessed | tf_op | source)
XLA Modules:
  0.0 95.8 jit_solution(294502903116872803)
XLA Ops:
  0.0 5.5 %first_outs.1 = (f32[4,64,512]{2,1,0:T(8,128)S(1)}, f32[4,64,512]{2,1,0:T(8,128)S(1)}) custom-call(s32[1]{0:T(128)} %bitcast.1.me_ref, bf16[64,1024]{1,0:T(8,128)(2,1)} %refs_0_.9, bf16[64,1024]{1,0:T(8,128)(2,1)} %refs_0_.9, bf16[1024,4096]{1,0:T(8,128)(2,1)} %refs_2_.4, bf16[1024,4096]{1,0:T(8,128)(2,1)} %refs_2_.5), custom_call_target="tpu_custom_call" | custom-call | flops 536870912 | bytes 8388608 | tf_op jit(solution)/shard_map/first_outs/pallas_call | solution.py:102
  5.5 3.0 %collective-permute-start = (f32[4,64,512]{2,1,0:T(8,128)S(1)}, f32[4,64,512]{2,1,0:T(8,128)S(1)}, u32[]{:S(2)}, u32[]{:S(2)}) collective-permute-start(f32[4,64,512]{2,1,0:T(8,128)S(1)} %get-tuple-element.74), channel_id=1, source_target_pairs={{0,2},{1,3},{2,0},{3,1},{4,6},{5,7},{6,4},{7,5},{8,10},{9,11},{10,... | collective-permute-start | bytes 1572872 | tf_op jit(solution)/shard_map/z1_qo/ppermute | solution.py:209
  8.5 6.4 %first_query_in.1 = f32[4,64,512]{2,1,0:T(8,128)S(1)} custom-call(s32[1]{0:T(128)} %bitcast.1.me_ref, bf16[64,3584]{1,0:T(8,128)(2,1)} %refs_0_.11, bf16[3584,4096]{1,0:T(8,128)(2,1)} %refs_3_.5), custom_call_target="tpu_custom_call" | custom-call | flops 939524096 | bytes 14680064 | tf_op jit(solution)/shard_map/first_query_in/pallas_call | solution.py:102
  14.9 1.6 %collective-permute-start.3 = (f32[4,64,512]{2,1,0:T(8,128)S(1)}, f32[4,64,512]{2,1,0:T(8,128)S(1)}, u32[]{:S(2)}, u32[]{:S(2)}) collective-permute-start(f32[4,64,512]{2,1,0:T(8,128)S(1)} %first_query_in.1), channel_id=1, source_target_pairs={{0,1},{1,0},{2,3},{3,2},{4,5},{5,4},{6,7},{7,6},{8,9},{9,8},{10,11... | collective-permute-start | bytes 1572872 | tf_op jit(solution)/shard_map/x_qi/ppermute | solution.py:209
  16.5 0.5 collective-permute-start.1
  17.0 0.7 pad_add_fusion.place_ref
  17.6 7.9 %middle_a.1 = (f32[4,64,512]{2,1,0:T(8,128)S(1)}, f32[4,64,512]{2,1,0:T(8,128)S(1)}) custom-call(s32[1]{0:T(128)} %bitcast.1.me_ref, bf16[64,1024]{1,0:T(8,128)(2,1)} %refs_0_.9, bf16[64,3584]{1,0:T(8,128)(2,1)} %refs_0_.11, bf16[1024,4096]{1,0:T(8,128)(2,1)} %refs_2_.4, bf16[3584,4096]{1,0:T(8,128)(2,1)} %refs_1_.11), custom_call_target="tpu_custom_call" | custom-call | flops 1207959552 | bytes 18874368 | tf_op jit(solution)/shard_map/middle_a/pallas_call | solution.py:102
  25.5 0.0 collective-permute-done
  25.6 0.1 collective-permute-start.2
  25.7 0.6 copy-done.2
  26.3 1.4 %collective-permute-start.6 = (f32[4,64,512]{2,1,0:T(8,128)S(1)}, f32[4,64,512]{2,1,0:T(8,128)S(1)}, u32[]{:S(2)}, u32[]{:S(2)}) collective-permute-start(f32[4,64,512]{2,1,0:T(8,128)S(1)} %get-tuple-element.79), channel_id=1, source_target_pairs={{0,1},{1,0},{2,3},{3,2},{4,5},{5,4},{6,7},{7,6},{8,9},{9,8},{10,11... | collective-permute-start | bytes 1572872 | tf_op jit(solution)/shard_map/x_ti/ppermute | solution.py:209
  27.7 7.9 %middle_b.1 = (f32[4,64,512]{2,1,0:T(8,128)S(1)}, f32[4,64,512]{2,1,0:T(8,128)S(1)}) custom-call(s32[1]{0:T(128)} %bitcast.1.me_ref, bf16[64,1024]{1,0:T(8,128)(2,1)} %refs_0_.9, bf16[64,3584]{1,0:T(8,128)(2,1)} %refs_0_.11, bf16[1024,4096]{1,0:T(8,128)(2,1)} %refs_2_.5, bf16[3584,4096]{1,0:T(8,128)(2,1)} %refs_3_.5), custom_call_target="tpu_custom_call" | custom-call | flops 1207959552 | bytes 18874368 | tf_op jit(solution)/shard_map/middle_b/pallas_call | solution.py:102
  35.6 0.0 collective-permute-done.3
  35.7 1.6 %collective-permute-start.5 = (f32[2,64,512]{2,1,0:T(8,128)S(1)}, f32[2,64,512]{2,1,0:T(8,128)S(1)}, u32[]{:S(2)}, u32[]{:S(2)}) collective-permute-start(f32[2,64,512]{2,1,0:T(8,128)S(1)} %slice_add_fusion), channel_id=1, source_target_pairs={{0,2},{1,3},{2,0},{3,1},{4,6},{5,7},{6,4},{7,5},{8,10},{9,11},{10,... | collective-permute-start | bytes 786440 | tf_op jit(solution)/shard_map/z1_qi/ppermute | solution.py:209
  37.3 0.1 slice_add_fusion.10
  37.4 2.7 %collective-permute-start.7 = (f32[1,64,512]{2,1,0:T(8,128)S(1)}, f32[1,64,512]{2,1,0:T(8,128)S(1)}, u32[]{:S(2)}, u32[]{:S(2)}) collective-permute-start(f32[1,64,512]{2,1,0:T(8,128)S(1)} %get-tuple-element.144), channel_id=1, source_target_pairs={{0,4},{1,5},{2,6},{3,7},{4,0},{5,1},{6,2},{7,3},{8,12},{9,13},{10,... | collective-permute-start | bytes 393224 | tf_op jit(solution)/shard_map/z2_qo/ppermute | solution.py:209
  40.1 0.7 collective-permute-start.4
  40.8 4.1 %last_train_in_a.1 = f32[2,64,512]{2,1,0:T(8,128)S(1)} custom-call(s32[1]{0:T(128)} %bitcast.1.me_ref, bf16[64,3584]{1,0:T(8,128)(2,1)} %refs_0_.11, bf16[3584,4096]{1,0:T(8,128)(2,1)} %refs_1_.11), custom_call_target="tpu_custom_call" | custom-call | flops 469762048 | bytes 7340032 | tf_op jit(solution)/shard_map/last_train_in_a/pallas_call | solution.py:102
  44.9 0.3 collective-permute-done.5
  45.2 1.0 %collective-permute-done.6 = f32[4,64,512]{2,1,0:T(8,128)S(1)} collective-permute-done((f32[4,64,512]{2,1,0:T(8,128)S(1)}, f32[4,64,512]{2,1,0:T(8,128)S(1)}, u32[]{:S(2)}, u32[]{:S(2)}) %collective-permute-start.6) | collective-permute-done | bytes 524320 | tf_op jit(solution)/shard_map/x_ti/ppermute | solution.py:209
  46.3 2.7 %collective-permute-start.9 = (f32[1,64,512]{2,1,0:T(8,128)S(1)}, f32[1,64,512]{2,1,0:T(8,128)S(1)}, u32[]{:S(2)}, u32[]{:S(2)}) collective-permute-start(f32[1,64,512]{2,1,0:T(8,128)S(1)} %slice_add_fusion.9), channel_id=1, source_target_pairs={{0,4},{1,5},{2,6},{3,7},{4,0},{5,1},{6,2},{7,3},{8,12},{9,13},{10,... | collective-permute-start | bytes 393224 | tf_op jit(solution)/shard_map/z2_qi/ppermute | solution.py:209
  49.0 1.5 %collective-permute-start.8 = (f32[2,64,512]{2,1,0:T(8,128)S(1)}, f32[2,64,512]{2,1,0:T(8,128)S(1)}, u32[]{:S(2)}, u32[]{:S(2)}) collective-permute-start(f32[2,64,512]{2,1,0:T(8,128)S(1)} %slice_add_fusion.2), channel_id=1, source_target_pairs={{0,2},{1,3},{2,0},{3,1},{4,6},{5,7},{6,4},{7,5},{8,10},{9,11},{10,... | collective-permute-start | bytes 786440 | tf_op jit(solution)/shard_map/z1_ti/ppermute | solution.py:209
  50.5 4.1 %last_train_in_b.1 = f32[2,64,512]{2,1,0:T(8,128)S(1)} custom-call(s32[1]{0:T(128)} %bitcast.1.me_ref, bf16[64,3584]{1,0:T(8,128)(2,1)} %refs_0_.11, bf16[3584,4096]{1,0:T(8,128)(2,1)} %refs_1_.11), custom_call_target="tpu_custom_call" | custom-call | flops 469762048 | bytes 7340032 | tf_op jit(solution)/shard_map/last_train_in_b/pallas_call | solution.py:102
  54.6 0.4 collective-permute-start.11
  55.0 3.4 %collective-permute-done.8 = f32[2,64,512]{2,1,0:T(8,128)S(1)} collective-permute-done((f32[2,64,512]{2,1,0:T(8,128)S(1)}, f32[2,64,512]{2,1,0:T(8,128)S(1)}, u32[]{:S(2)}, u32[]{:S(2)}) %collective-permute-start.8) | collective-permute-done | bytes 262176 | tf_op jit(solution)/shard_map/z1_ti/ppermute | solution.py:209
  58.5 1.3 %examples.2 = (f32[8,8,128]{2,1,0:T(8,128)S(1)}, f32[8,8,128]{2,1,0:T(8,128)S(1)}, f32[8,8,128]{2,1,0:T(8,128)S(1)}, f32[8,8,128]{2,1,0:T(8,128)S(1)}) custom-call(s32[4]{0:T(128)} %pad_add_fusion.place_ref, f32[1,64,512]{2,1,0:T(8,128)S(1)} %get-tuple-element.143.refs_0_, f32[1,64,512]{2,1,0:T(8,128)S(1)} %collective-permute-done.7.refs_1_, ...), custom_call_target="tpu_custom_call" | custom-call | flops 1 | bytes 1 | tf_op jit(solution)/shard_map/examples/pallas_call | solution.py:165
  59.8 0.5 collective-permute-start.10
  60.3 3.3 %collective-permute-start.12 = (f32[8,8,128]{2,1,0:T(8,128)S(1)}, f32[8,8,128]{2,1,0:T(8,128)S(1)}, u32[]{:S(2)}, u32[]{:S(2)}) collective-permute-start(f32[8,8,128]{2,1,0:T(8,128)S(1)} %get-tuple-element.121), channel_id=1, source_target_pairs={{0,2},{1,3},{2,0},{3,1},{4,6},{5,7},{6,4},{7,5},{8,10},{9,11},{10,... | collective-permute-start | bytes 98312 | tf_op jit(solution)/shard_map/z_query/ppermute | solution.py:209
  63.6 0.2 collective-permute-start.13
  63.8 2.1 %collective-permute-start.14 = (f32[8,8,128]{2,1,0:T(8,128)S(1)}, f32[8,8,128]{2,1,0:T(8,128)S(1)}, u32[]{:S(2)}, u32[]{:S(2)}) collective-permute-start(f32[8,8,128]{2,1,0:T(8,128)S(1)} %get-tuple-element.123), channel_id=1, source_target_pairs={{0,6},{1,7},{2,4},{3,5},{4,2},{5,3},{6,0},{7,1},{8,14},{9,15},{10,... | collective-permute-start | bytes 98312 | tf_op jit(solution)/shard_map/z_query/ppermute | solution.py:209
  66.0 0.8 collective-permute-done.11.refs_1_
  66.8 3.3 %collective-permute-done.13 = f32[8,8,128]{2,1,0:T(8,128)S(1)} collective-permute-done((f32[8,8,128]{2,1,0:T(8,128)S(1)}, f32[8,8,128]{2,1,0:T(8,128)S(1)}, u32[]{:S(2)}, u32[]{:S(2)}) %collective-permute-start.13) | collective-permute-done | bytes 32800 | tf_op jit(solution)/shard_map/z_query/ppermute | solution.py:209
  70.1 0.9 collective-permute-start.15
  71.0 1.3 %examples.3 = (f32[8,8,128]{2,1,0:T(8,128)S(1)}, f32[8,8,128]{2,1,0:T(8,128)S(1)}, f32[8,8,128]{2,1,0:T(8,128)S(1)}, f32[8,8,128]{2,1,0:T(8,128)S(1)}) custom-call(s32[4]{0:T(128)} %pad_add_fusion.place_ref, f32[1,64,512]{2,1,0:T(8,128)S(1)} %slice_add_fusion.6.refs_0_, f32[1,64,512]{2,1,0:T(8,128)S(1)} %collective-permute-done.11.refs_1_, ...), custom_call_target="tpu_custom_call" | custom-call | flops 1 | bytes 1 | tf_op jit(solution)/shard_map/examples/pallas_call | solution.py:165
  72.3 0.3 collective-permute-start.16
  72.6 1.8 %collective-permute-start.17 = (f32[8,8,128]{2,1,0:T(8,128)S(1)}, f32[8,8,128]{2,1,0:T(8,128)S(1)}, u32[]{:S(2)}, u32[]{:S(2)}) collective-permute-start(f32[8,8,128]{2,1,0:T(8,128)S(1)} %get-tuple-element.136), channel_id=1, source_target_pairs={{0,4},{1,5},{2,6},{3,7},{4,0},{5,1},{6,2},{7,3},{8,12},{9,13},{10,... | collective-permute-start | bytes 98312 | tf_op jit(solution)/shard_map/z_train/ppermute | solution.py:209
  74.4 2.4 %collective-permute-start.18 = (f32[8,8,128]{2,1,0:T(8,128)S(1)}, f32[8,8,128]{2,1,0:T(8,128)S(1)}, u32[]{:S(2)}, u32[]{:S(2)}) collective-permute-start(f32[8,8,128]{2,1,0:T(8,128)S(1)} %get-tuple-element.137), channel_id=1, source_target_pairs={{0,6},{1,7},{2,4},{3,5},{4,2},{5,3},{6,0},{7,1},{8,14},{9,15},{10,... | collective-permute-start | bytes 98312 | tf_op jit(solution)/shard_map/z_train/ppermute | solution.py:209
  76.8 1.0 %collective-permute-done.17.refs_2_ = f32[8,8,128]{2,1,0:T(8,128)S(1)} collective-permute-done((f32[8,8,128]{2,1,0:T(8,128)S(1)}, f32[8,8,128]{2,1,0:T(8,128)S(1)}, u32[]{:S(2)}, u32[]{:S(2)}) %collective-permute-start.17) | collective-permute-done | bytes 32800 | tf_op jit(solution)/shard_map/z_train/ppermute | solution.py:209
  77.8 2.4 %collective-permute-done.18.refs_3_ = f32[8,8,128]{2,1,0:T(8,128)S(1)} collective-permute-done((f32[8,8,128]{2,1,0:T(8,128)S(1)}, f32[8,8,128]{2,1,0:T(8,128)S(1)}, u32[]{:S(2)}, u32[]{:S(2)}) %collective-permute-start.18) | collective-permute-done | bytes 32800 | tf_op jit(solution)/shard_map/z_train/ppermute | solution.py:209
  80.1 1.3 %collective-permute-done.20.refs_7_ = f32[4,8,8,128]{3,2,1,0:T(8,128)S(1)} collective-permute-done((f32[4,8,8,128]{3,2,1,0:T(8,128)S(1)}, f32[4,8,8,128]{3,2,1,0:T(8,128)S(1)}, u32[]{:S(2)}, u32[]{:S(2)}) %collective-permute-start.20) | collective-permute-done | bytes 131104 | tf_op jit(solution)/shard_map/dp_x_query/ppermute | solution.py:214
  81.5 1.0 %partial_scores.1 = f32[64,128]{1,0:T(8,128)S(1)} custom-call(s32[4]{0:T(128)} %pad_add_fusion.place_ref, f32[8,8,128]{2,1,0:T(8,128)S(1)} %get-tuple-element.138.refs_0_, f32[8,8,128]{2,1,0:T(8,128)S(1)} %collective-permute-done.16.refs_1_, f32[8,8,128]{2,1,0:T(8,128)S(1)} %collective-permute-done.17.refs_2_, ...), custom_call_target="tpu_custom_call" | custom-call | tf_op jit(solution)/shard_map/partial_scores/pallas_call | solution.py:194
  82.5 0.0 collective-permute-start.21
  82.6 4.8 %collective-permute-done.21 = f32[64,128]{1,0:T(8,128)S(1)} collective-permute-done((f32[64,128]{1,0:T(8,128)S(1)}, f32[64,128]{1,0:T(8,128)S(1)}, u32[]{:S(2)}, u32[]{:S(2)}) %collective-permute-start.21) | collective-permute-done | bytes 32800 | tf_op jit(solution)/shard_map/scores/ppermute | solution.py:209
  87.4 0.0 collective-permute-start.22
  87.4 3.9 %collective-permute-done.22 = f32[64,128]{1,0:T(8,128)S(1)} collective-permute-done((f32[64,128]{1,0:T(8,128)S(1)}, f32[64,128]{1,0:T(8,128)S(1)}, u32[]{:S(2)}, u32[]{:S(2)}) %collective-permute-start.22) | collective-permute-done | bytes 32800 | tf_op jit(solution)/shard_map/scores/ppermute | solution.py:209
  91.3 1.3 %collective-permute-start.23 = (f32[64,128]{1,0:T(8,128)S(1)}, f32[64,128]{1,0:T(8,128)S(1)}, u32[]{:S(2)}, u32[]{:S(2)}) collective-permute-start(f32[64,128]{1,0:T(8,128)S(1)} %add.96), channel_id=1, source_target_pairs={{0,1},{1,0},{2,3},{3,2},{4,5},{5,4},{6,7},{7,6},{8,9},{9,8},{10,11... | collective-permute-start | bytes 98312 | tf_op jit(solution)/shard_map/scores/ppermute | solution.py:209
  92.6 2.6 %collective-permute-done.23 = f32[64,128]{1,0:T(8,128)S(1)} collective-permute-done((f32[64,128]{1,0:T(8,128)S(1)}, f32[64,128]{1,0:T(8,128)S(1)}, u32[]{:S(2)}, u32[]{:S(2)}) %collective-permute-start.23) | collective-permute-done | bytes 32800 | tf_op jit(solution)/shard_map/scores/ppermute | solution.py:209
  95.2 0.6 add.97
  (33 shorter events, 0.4 us)
Async XLA Ops:
  5.5 20.1 %collective-permute-start = (f32[4,64,512]{2,1,0:T(8,128)S(1)}, f32[4,64,512]{2,1,0:T(8,128)S(1)}, u32[]{:S(2)}, u32[]{:S(2)}) collective-permute-start(f32[4,64,512]{2,1,0:T(8,128)S(1)} %get-tuple-element.74), channel_id=1, source_target_pairs={{0,2},{1,3},{2,0},{3,1},{4,6},{5,7},{6,4},{7,5},{8,10},{9,11},{10,... | collective-permute-start | bytes 1572872 | tf_op jit(solution)/shard_map/z1_qo/ppermute | solution.py:209
  14.9 20.7 %collective-permute-start.3 = (f32[4,64,512]{2,1,0:T(8,128)S(1)}, f32[4,64,512]{2,1,0:T(8,128)S(1)}, u32[]{:S(2)}, u32[]{:S(2)}) collective-permute-start(f32[4,64,512]{2,1,0:T(8,128)S(1)} %first_query_in.1), channel_id=1, source_target_pairs={{0,1},{1,0},{2,3},{3,2},{4,5},{5,4},{6,7},{7,6},{8,9},{9,8},{10,11... | collective-permute-start | bytes 1572872 | tf_op jit(solution)/shard_map/x_qi/ppermute | solution.py:209
  16.5 23.5 %collective-permute-start.1 = (f32[4,64,512]{2,1,0:T(8,128)S(1)}, f32[4,64,512]{2,1,0:T(8,128)S(1)}, u32[]{:S(2)}, u32[]{:S(2)}) collective-permute-start(f32[4,64,512]{2,1,0:T(8,128)S(1)} %get-tuple-element.83), channel_id=1, source_target_pairs={{0,2},{1,3},{2,0},{3,1},{4,6},{5,7},{6,4},{7,5},{8,10},{9,11},{10,... | collective-permute-start | bytes 1572872 | tf_op jit(solution)/shard_map/z1_to/ppermute | solution.py:209
  25.5 0.8 copy-start.2
  25.6 11.7 %collective-permute-start.2 = (f32[2,64,512]{2,1,0:T(8,128)S(1)}, f32[2,64,512]{2,1,0:T(8,128)S(1)}, u32[]{:S(2)}, u32[]{:S(2)}) collective-permute-start(f32[2,64,512]{2,1,0:T(8,128)S(1)} %slice_add_fusion.1), channel_id=1, source_target_pairs={{0,1},{1,0},{2,3},{3,2},{4,5},{5,4},{6,7},{7,6},{8,9},{9,8},{10,11... | collective-permute-start | bytes 786440 | tf_op jit(solution)/shard_map/x_qo/ppermute | solution.py:209
  26.3 11.0 %copy-start.3 = (f32[4,64,512]{2,1,0:T(8,128)S(1)}, f32[4,64,512]{2,1,0:T(8,128)}, u32[]{:S(2)}) copy-start(f32[4,64,512]{2,1,0:T(8,128)} %copy-done.2) | copy-start | bytes 1572868
  26.3 19.9 %collective-permute-start.6 = (f32[4,64,512]{2,1,0:T(8,128)S(1)}, f32[4,64,512]{2,1,0:T(8,128)S(1)}, u32[]{:S(2)}, u32[]{:S(2)}) collective-permute-start(f32[4,64,512]{2,1,0:T(8,128)S(1)} %get-tuple-element.79), channel_id=1, source_target_pairs={{0,1},{1,0},{2,3},{3,2},{4,5},{5,4},{6,7},{7,6},{8,9},{9,8},{10,11... | collective-permute-start | bytes 1572872 | tf_op jit(solution)/shard_map/x_ti/ppermute | solution.py:209
  35.7 9.5 %collective-permute-start.5 = (f32[2,64,512]{2,1,0:T(8,128)S(1)}, f32[2,64,512]{2,1,0:T(8,128)S(1)}, u32[]{:S(2)}, u32[]{:S(2)}) collective-permute-start(f32[2,64,512]{2,1,0:T(8,128)S(1)} %slice_add_fusion), channel_id=1, source_target_pairs={{0,2},{1,3},{2,0},{3,1},{4,6},{5,7},{6,4},{7,5},{8,10},{9,11},{10,... | collective-permute-start | bytes 786440 | tf_op jit(solution)/shard_map/z1_qi/ppermute | solution.py:209
  37.4 17.2 %collective-permute-start.7 = (f32[1,64,512]{2,1,0:T(8,128)S(1)}, f32[1,64,512]{2,1,0:T(8,128)S(1)}, u32[]{:S(2)}, u32[]{:S(2)}) collective-permute-start(f32[1,64,512]{2,1,0:T(8,128)S(1)} %get-tuple-element.144), channel_id=1, source_target_pairs={{0,4},{1,5},{2,6},{3,7},{4,0},{5,1},{6,2},{7,3},{8,12},{9,13},{10,... | collective-permute-start | bytes 393224 | tf_op jit(solution)/shard_map/z2_qo/ppermute | solution.py:209
  40.1 14.5 %collective-permute-start.4 = (f32[2,64,512]{2,1,0:T(8,128)S(1)}, f32[2,64,512]{2,1,0:T(8,128)S(1)}, u32[]{:S(2)}, u32[]{:S(2)}) collective-permute-start(f32[2,64,512]{2,1,0:T(8,128)S(1)} %slice_add_fusion.3), channel_id=1, source_target_pairs={{0,1},{1,0},{2,3},{3,2},{4,5},{5,4},{6,7},{7,6},{8,9},{9,8},{10,11... | collective-permute-start | bytes 786440 | tf_op jit(solution)/shard_map/x_to/ppermute | solution.py:209
  40.8 17.7 %copy-start = (s32[4096]{0:T(1024)S(1)}, s32[4096]{0:T(1024)}, u32[]{:S(2)}) copy-start(s32[4096]{0:T(1024)} %param.15) | copy-start | bytes 49156
  40.8 30.2 %copy-start.1 = (s32[4096]{0:T(1024)S(1)}, s32[4096]{0:T(1024)}, u32[]{:S(2)}) copy-start(s32[4096]{0:T(1024)} %param.14) | copy-start | bytes 49156
  46.3 12.2 %collective-permute-start.9 = (f32[1,64,512]{2,1,0:T(8,128)S(1)}, f32[1,64,512]{2,1,0:T(8,128)S(1)}, u32[]{:S(2)}, u32[]{:S(2)}) collective-permute-start(f32[1,64,512]{2,1,0:T(8,128)S(1)} %slice_add_fusion.9), channel_id=1, source_target_pairs={{0,4},{1,5},{2,6},{3,7},{4,0},{5,1},{6,2},{7,3},{8,12},{9,13},{10,... | collective-permute-start | bytes 393224 | tf_op jit(solution)/shard_map/z2_qi/ppermute | solution.py:209
  49.0 9.5 %collective-permute-start.8 = (f32[2,64,512]{2,1,0:T(8,128)S(1)}, f32[2,64,512]{2,1,0:T(8,128)S(1)}, u32[]{:S(2)}, u32[]{:S(2)}) collective-permute-start(f32[2,64,512]{2,1,0:T(8,128)S(1)} %slice_add_fusion.2), channel_id=1, source_target_pairs={{0,2},{1,3},{2,0},{3,1},{4,6},{5,7},{6,4},{7,5},{8,10},{9,11},{10,... | collective-permute-start | bytes 786440 | tf_op jit(solution)/shard_map/z1_ti/ppermute | solution.py:209
  54.6 12.1 %collective-permute-start.11 = (f32[1,64,512]{2,1,0:T(8,128)S(1)}, f32[1,64,512]{2,1,0:T(8,128)S(1)}, u32[]{:S(2)}, u32[]{:S(2)}) collective-permute-start(f32[1,64,512]{2,1,0:T(8,128)S(1)} %slice_add_fusion.7), channel_id=1, source_target_pairs={{0,4},{1,5},{2,6},{3,7},{4,0},{5,1},{6,2},{7,3},{8,12},{9,13},{10,... | collective-permute-start | bytes 393224 | tf_op jit(solution)/shard_map/z2_to/ppermute | solution.py:209
  59.8 10.2 %collective-permute-start.10 = (f32[1,64,512]{2,1,0:T(8,128)S(1)}, f32[1,64,512]{2,1,0:T(8,128)S(1)}, u32[]{:S(2)}, u32[]{:S(2)}) collective-permute-start(f32[1,64,512]{2,1,0:T(8,128)S(1)} %slice_add_fusion.5), channel_id=1, source_target_pairs={{0,4},{1,5},{2,6},{3,7},{4,0},{5,1},{6,2},{7,3},{8,12},{9,13},{10,... | collective-permute-start | bytes 393224 | tf_op jit(solution)/shard_map/z2_ti/ppermute | solution.py:209
  60.3 6.5 %collective-permute-start.12 = (f32[8,8,128]{2,1,0:T(8,128)S(1)}, f32[8,8,128]{2,1,0:T(8,128)S(1)}, u32[]{:S(2)}, u32[]{:S(2)}) collective-permute-start(f32[8,8,128]{2,1,0:T(8,128)S(1)} %get-tuple-element.121), channel_id=1, source_target_pairs={{0,2},{1,3},{2,0},{3,1},{4,6},{5,7},{6,4},{7,5},{8,10},{9,11},{10,... | collective-permute-start | bytes 98312 | tf_op jit(solution)/shard_map/z_query/ppermute | solution.py:209
  63.6 6.4 %collective-permute-start.13 = (f32[8,8,128]{2,1,0:T(8,128)S(1)}, f32[8,8,128]{2,1,0:T(8,128)S(1)}, u32[]{:S(2)}, u32[]{:S(2)}) collective-permute-start(f32[8,8,128]{2,1,0:T(8,128)S(1)} %get-tuple-element.122), channel_id=1, source_target_pairs={{0,4},{1,5},{2,6},{3,7},{4,0},{5,1},{6,2},{7,3},{8,12},{9,13},{10,... | collective-permute-start | bytes 98312 | tf_op jit(solution)/shard_map/z_query/ppermute | solution.py:209
  63.8 6.2 %collective-permute-start.14 = (f32[8,8,128]{2,1,0:T(8,128)S(1)}, f32[8,8,128]{2,1,0:T(8,128)S(1)}, u32[]{:S(2)}, u32[]{:S(2)}) collective-permute-start(f32[8,8,128]{2,1,0:T(8,128)S(1)} %get-tuple-element.123), channel_id=1, source_target_pairs={{0,6},{1,7},{2,4},{3,5},{4,2},{5,3},{6,0},{7,1},{8,14},{9,15},{10,... | collective-permute-start | bytes 98312 | tf_op jit(solution)/shard_map/z_query/ppermute | solution.py:209
  70.1 10.1 %collective-permute-start.15 = (f32[4,8,8,128]{3,2,1,0:T(8,128)S(1)}, f32[4,8,8,128]{3,2,1,0:T(8,128)S(1)}, u32[]{:S(2)}, u32[]{:S(2)}) collective-permute-start(f32[4,8,8,128]{3,2,1,0:T(8,128)S(1)} %pad_maximum_fusion.refs_4_), channel_id=1, source_target_pairs={{0,1},{1,0},{2,3},{3,2},{4,5},{5,4},{6,7},{7,6},{8,9},{9,8},{10,11... | collective-permute-start | bytes 393224 | tf_op jit(solution)/shard_map/x_query/ppermute | solution.py:209
  72.3 4.5 %collective-permute-start.16 = (f32[8,8,128]{2,1,0:T(8,128)S(1)}, f32[8,8,128]{2,1,0:T(8,128)S(1)}, u32[]{:S(2)}, u32[]{:S(2)}) collective-permute-start(f32[8,8,128]{2,1,0:T(8,128)S(1)} %get-tuple-element.135), channel_id=1, source_target_pairs={{0,2},{1,3},{2,0},{3,1},{4,6},{5,7},{6,4},{7,5},{8,10},{9,11},{10,... | collective-permute-start | bytes 98312 | tf_op jit(solution)/shard_map/z_train/ppermute | solution.py:209
  72.6 5.2 %collective-permute-start.17 = (f32[8,8,128]{2,1,0:T(8,128)S(1)}, f32[8,8,128]{2,1,0:T(8,128)S(1)}, u32[]{:S(2)}, u32[]{:S(2)}) collective-permute-start(f32[8,8,128]{2,1,0:T(8,128)S(1)} %get-tuple-element.136), channel_id=1, source_target_pairs={{0,4},{1,5},{2,6},{3,7},{4,0},{5,1},{6,2},{7,3},{8,12},{9,13},{10,... | collective-permute-start | bytes 98312 | tf_op jit(solution)/shard_map/z_train/ppermute | solution.py:209
  74.4 5.7 %collective-permute-start.18 = (f32[8,8,128]{2,1,0:T(8,128)S(1)}, f32[8,8,128]{2,1,0:T(8,128)S(1)}, u32[]{:S(2)}, u32[]{:S(2)}) collective-permute-start(f32[8,8,128]{2,1,0:T(8,128)S(1)} %get-tuple-element.137), channel_id=1, source_target_pairs={{0,6},{1,7},{2,4},{3,5},{4,2},{5,3},{6,0},{7,1},{8,14},{9,15},{10,... | collective-permute-start | bytes 98312 | tf_op jit(solution)/shard_map/z_train/ppermute | solution.py:209
  76.8 3.4 %collective-permute-start.19 = (f32[4,8,8,128]{3,2,1,0:T(8,128)S(1)}, f32[4,8,8,128]{3,2,1,0:T(8,128)S(1)}, u32[]{:S(2)}, u32[]{:S(2)}) collective-permute-start(f32[4,8,8,128]{3,2,1,0:T(8,128)S(1)} %pad_maximum_fusion.refs_4_), channel_id=1, source_target_pairs={{0,8},{8,0},{1,9},{9,1},{2,10},{10,2},{3,11},{11,3},{4,12},{12,4},... | collective-permute-start | bytes 393224 | tf_op jit(solution)/shard_map/dp_query/ppermute | solution.py:214
  80.1 1.3 %collective-permute-start.20 = (f32[4,8,8,128]{3,2,1,0:T(8,128)S(1)}, f32[4,8,8,128]{3,2,1,0:T(8,128)S(1)}, u32[]{:S(2)}, u32[]{:S(2)}) collective-permute-start(f32[4,8,8,128]{3,2,1,0:T(8,128)S(1)} %collective-permute-done.15.refs_5_), channel_id=1, source_target_pairs={{0,8},{8,0},{1,9},{9,1},{2,10},{10,2},{3,11},{11,3},{4,12},{12,4},... | collective-permute-start | bytes 393224 | tf_op jit(solution)/shard_map/dp_x_query/ppermute | solution.py:214
  82.5 4.9 %collective-permute-start.21 = (f32[64,128]{1,0:T(8,128)S(1)}, f32[64,128]{1,0:T(8,128)S(1)}, u32[]{:S(2)}, u32[]{:S(2)}) collective-permute-start(f32[64,128]{1,0:T(8,128)S(1)} %partial_scores.1), channel_id=1, source_target_pairs={{0,4},{1,5},{2,6},{3,7},{4,0},{5,1},{6,2},{7,3},{8,12},{9,13},{10,... | collective-permute-start | bytes 98312 | tf_op jit(solution)/shard_map/scores/ppermute | solution.py:209
  87.4 3.9 %collective-permute-start.22 = (f32[64,128]{1,0:T(8,128)S(1)}, f32[64,128]{1,0:T(8,128)S(1)}, u32[]{:S(2)}, u32[]{:S(2)}) collective-permute-start(f32[64,128]{1,0:T(8,128)S(1)} %add.95), channel_id=1, source_target_pairs={{0,2},{1,3},{2,0},{3,1},{4,6},{5,7},{6,4},{7,5},{8,10},{9,11},{10,... | collective-permute-start | bytes 98312 | tf_op jit(solution)/shard_map/scores/ppermute | solution.py:209
  91.3 3.9 %collective-permute-start.23 = (f32[64,128]{1,0:T(8,128)S(1)}, f32[64,128]{1,0:T(8,128)S(1)}, u32[]{:S(2)}, u32[]{:S(2)}) collective-permute-start(f32[64,128]{1,0:T(8,128)S(1)} %add.96), channel_id=1, source_target_pairs={{0,1},{1,0},{2,3},{3,2},{4,5},{5,4},{6,7},{7,6},{8,9},{9,8},{10,11... | collective-permute-start | bytes 98312 | tf_op jit(solution)/shard_map/scores/ppermute | solution.py:209

commit v4 on v3

--- a/solution.py
+++ b/solution.py
@@ -175,14 +175,14 @@
 
 def partial_scores(place, trains, queries):
     def kernel(place_ref, *refs):
-        t_refs, q_refs = refs[:4], refs[4:8]
-        out_ref, q_all, t_all = refs[8:]
+        t_refs, q_refs = refs[:4], refs[4:6]
+        out_ref, q_all, t_all = refs[6:]
         z, x, dp = place_ref[0], place_ref[2], place_ref[3]
         for k in range(4):
             t_all[k ^ z] = t_refs[k][...]
-        for d in range(4):
-            for k in range(4):
-                q_all[((d // 2) ^ dp) * 8 + (k ^ z) * 2 + ((d % 2) ^ x)] = q_refs[d][k]
+        for d in range(2):
+            for i in range(8):
+                q_all[((i // 4) ^ dp) * 8 + ((i % 4) ^ z) * 2 + (d ^ x)] = q_refs[d][i]
         a2 = range(HALF // 4)
         train = jnp.concatenate([t_all[:, a].reshape(4 * SEGS, 2 * RANK) for a in a2], axis=1)
         query = jnp.concatenate([q_all[:, a].reshape(16 * SEGS, 2 * RANK) for a in a2], axis=1)
@@ -194,7 +194,7 @@
     return pl.pallas_call(
         kernel,
         out_shape=pltpu.VMEM((8 * SEGS, 16 * SEGS), jnp.float32),
-        in_specs=[pl.BlockSpec(memory_space=pltpu.SMEM)] + [pl.BlockSpec(memory_space=pltpu.VMEM)] * 8,
+        in_specs=[pl.BlockSpec(memory_space=pltpu.SMEM)] + [pl.BlockSpec(memory_space=pltpu.VMEM)] * 6,
         out_specs=pl.BlockSpec(memory_space=pltpu.VMEM),
         scratch_shapes=[
             pltpu.VMEM((16, HALF // 4, SEGS, 2 * RANK), jnp.float32),
@@ -282,10 +282,10 @@
     place, ti3, to3, *query = lax.optimization_barrier((place, ti3, to3, *query))
     train = examples(place, (to, to3), (ti, ti3), train_slots)
     query = jnp.stack(query)
+    query = jnp.concatenate([query, after(cross(query, "dp_query"), train[0])])
     other = swap(query, X, "x_query")
     trains = [train[0]] + [swap(train[k], 2 * k, "z_train") for k in (3, 2, 1)][::-1]
-    other, *trains = lax.optimization_barrier((other, *trains))
-    queries = [query, other, cross(query, "dp_query"), cross(other, "dp_x_query")]
+    queries = [query, other]
     scores = partial_scores(place, trains, queries)
     for mask in (Z2, Z1, X):
         scores = scores + swap(scores, mask, "scores")

time: 96 us -> 94.8 us (0.987)
  waiting for transfers between devices: 24.8 us -> 22.5 us
  starting transfers between devices: 29 us -> 30.1 us
    ppermute x2 -> x1, waiting for transfers between devices: 1.34 us -> 0.01 us  [cross(): return lax.ppermute(value, 'dp', [(0, 1), (1, 0)])]
    ppermute x22, starting transfers between devices: 29 us -> 30 us  [swap(): return lax.ppermute(value, 'tensor', [(i, i ^ mask) for i in range(8)])]
    ppermute x22, waiting for transfers between devices: 23.5 us -> 22.5 us  [swap(): return lax.ppermute(value, 'tensor', [(i, i ^ mask) for i in range(8)])]
  transfers between devices with their start and end apart: 24 -> 23, of which waited for: 11 -> 11; matrix products, arithmetic and copies ran while one was open for 1% -> 1% of each run, Pallas kernels for 34% -> 35%
where the time goes in v4:
time: 94.8 us; the launch traced here: 94.6 us
  Pallas kernels  39.4 us (42%)
  starting transfers between devices  30.1 us (32%)
  waiting for transfers between devices  22.5 us (24%)
  other arithmetic  1.67 us (2%)
    pallas_call x6, Pallas kernels, project(): pl.pallas_call(kernel, out_shape=[pltpu.VMEM((len(masks), RANK, BLK), jnp...  35.9 us
    ppermute x22, starting transfers between devices, swap(): return lax.ppermute(value, 'tensor', [(i, i ^ mask) for i in range(8)])  30 us
    ppermute x22, waiting for transfers between devices, swap(): return lax.ppermute(value, 'tensor', [(i, i ^ mask) for i in range(8)])  22.5 us
    pallas_call x2, Pallas kernels, examples(): pl.pallas_call(kernel, out_shape=[pltpu.VMEM((HALF // 4, SEGS, 2 * RANK),...  2.54 us
  transfers between devices with their start and end apart: 23, of which 11 were waited for; matrix products, arithmetic and copies ran while one was open for 1% of the time, Pallas kernels for 35%

profile of v4, /device:TPU:0, one launch (start us, length us, event | category | flops | bytes accessed | tf_op | source)
XLA Modules:
  0.0 94.6 jit_solution(18026458088079670073)
XLA Ops:
  0.0 5.5 %first_outs.1 = (f32[4,64,512]{2,1,0:T(8,128)S(1)}, f32[4,64,512]{2,1,0:T(8,128)S(1)}) custom-call(s32[1]{0:T(128)} %bitcast.1.me_ref, bf16[64,1024]{1,0:T(8,128)(2,1)} %refs_0_.9, bf16[64,1024]{1,0:T(8,128)(2,1)} %refs_0_.9, bf16[1024,4096]{1,0:T(8,128)(2,1)} %refs_2_.4, bf16[1024,4096]{1,0:T(8,128)(2,1)} %refs_2_.5), custom_call_target="tpu_custom_call" | custom-call | flops 536870912 | bytes 8388608 | tf_op jit(solution)/shard_map/first_outs/pallas_call | solution.py:102
  5.5 3.0 %collective-permute-start = (f32[4,64,512]{2,1,0:T(8,128)S(1)}, f32[4,64,512]{2,1,0:T(8,128)S(1)}, u32[]{:S(2)}, u32[]{:S(2)}) collective-permute-start(f32[4,64,512]{2,1,0:T(8,128)S(1)} %get-tuple-element.70), channel_id=1, source_target_pairs={{0,2},{1,3},{2,0},{3,1},{4,6},{5,7},{6,4},{7,5},{8,10},{9,11},{10,... | collective-permute-start | bytes 1572872 | tf_op jit(solution)/shard_map/z1_qo/ppermute | solution.py:209
  8.5 6.4 %first_query_in.1 = f32[4,64,512]{2,1,0:T(8,128)S(1)} custom-call(s32[1]{0:T(128)} %bitcast.1.me_ref, bf16[64,3584]{1,0:T(8,128)(2,1)} %refs_0_.11, bf16[3584,4096]{1,0:T(8,128)(2,1)} %refs_3_.5), custom_call_target="tpu_custom_call" | custom-call | flops 939524096 | bytes 14680064 | tf_op jit(solution)/shard_map/first_query_in/pallas_call | solution.py:102
  14.9 1.6 %collective-permute-start.3 = (f32[4,64,512]{2,1,0:T(8,128)S(1)}, f32[4,64,512]{2,1,0:T(8,128)S(1)}, u32[]{:S(2)}, u32[]{:S(2)}) collective-permute-start(f32[4,64,512]{2,1,0:T(8,128)S(1)} %first_query_in.1), channel_id=1, source_target_pairs={{0,1},{1,0},{2,3},{3,2},{4,5},{5,4},{6,7},{7,6},{8,9},{9,8},{10,11... | collective-permute-start | bytes 1572872 | tf_op jit(solution)/shard_map/x_qi/ppermute | solution.py:209
  16.5 0.5 collective-permute-start.1
  17.0 0.6 pad_add_fusion.place_ref
  17.6 7.9 %middle_a.1 = (f32[4,64,512]{2,1,0:T(8,128)S(1)}, f32[4,64,512]{2,1,0:T(8,128)S(1)}) custom-call(s32[1]{0:T(128)} %bitcast.1.me_ref, bf16[64,1024]{1,0:T(8,128)(2,1)} %refs_0_.9, bf16[64,3584]{1,0:T(8,128)(2,1)} %refs_0_.11, bf16[1024,4096]{1,0:T(8,128)(2,1)} %refs_2_.4, bf16[3584,4096]{1,0:T(8,128)(2,1)} %refs_1_.11), custom_call_target="tpu_custom_call" | custom-call | flops 1207959552 | bytes 18874368 | tf_op jit(solution)/shard_map/middle_a/pallas_call | solution.py:102
  25.6 0.1 collective-permute-start.2
  25.7 0.6 copy-done.2
  26.3 1.3 %collective-permute-start.6 = (f32[4,64,512]{2,1,0:T(8,128)S(1)}, f32[4,64,512]{2,1,0:T(8,128)S(1)}, u32[]{:S(2)}, u32[]{:S(2)}) collective-permute-start(f32[4,64,512]{2,1,0:T(8,128)S(1)} %get-tuple-element.75), channel_id=1, source_target_pairs={{0,1},{1,0},{2,3},{3,2},{4,5},{5,4},{6,7},{7,6},{8,9},{9,8},{10,11... | collective-permute-start | bytes 1572872 | tf_op jit(solution)/shard_map/x_ti/ppermute | solution.py:209
  27.7 7.9 %middle_b.1 = (f32[4,64,512]{2,1,0:T(8,128)S(1)}, f32[4,64,512]{2,1,0:T(8,128)S(1)}) custom-call(s32[1]{0:T(128)} %bitcast.1.me_ref, bf16[64,1024]{1,0:T(8,128)(2,1)} %refs_0_.9, bf16[64,3584]{1,0:T(8,128)(2,1)} %refs_0_.11, bf16[1024,4096]{1,0:T(8,128)(2,1)} %refs_2_.5, bf16[3584,4096]{1,0:T(8,128)(2,1)} %refs_3_.5), custom_call_target="tpu_custom_call" | custom-call | flops 1207959552 | bytes 18874368 | tf_op jit(solution)/shard_map/middle_b/pallas_call | solution.py:102
  35.6 1.6 %collective-permute-start.5 = (f32[2,64,512]{2,1,0:T(8,128)S(1)}, f32[2,64,512]{2,1,0:T(8,128)S(1)}, u32[]{:S(2)}, u32[]{:S(2)}) collective-permute-start(f32[2,64,512]{2,1,0:T(8,128)S(1)} %slice_add_fusion), channel_id=1, source_target_pairs={{0,2},{1,3},{2,0},{3,1},{4,6},{5,7},{6,4},{7,5},{8,10},{9,11},{10,... | collective-permute-start | bytes 786440 | tf_op jit(solution)/shard_map/z1_qi/ppermute | solution.py:209
  37.3 0.1 slice_add_fusion.10
  37.3 2.7 %collective-permute-start.7 = (f32[1,64,512]{2,1,0:T(8,128)S(1)}, f32[1,64,512]{2,1,0:T(8,128)S(1)}, u32[]{:S(2)}, u32[]{:S(2)}) collective-permute-start(f32[1,64,512]{2,1,0:T(8,128)S(1)} %get-tuple-element.136), channel_id=1, source_target_pairs={{0,4},{1,5},{2,6},{3,7},{4,0},{5,1},{6,2},{7,3},{8,12},{9,13},{10,... | collective-permute-start | bytes 393224 | tf_op jit(solution)/shard_map/z2_qo/ppermute | solution.py:209
  40.1 0.8 collective-permute-start.4
  40.8 4.1 %last_train_in_a.1 = f32[2,64,512]{2,1,0:T(8,128)S(1)} custom-call(s32[1]{0:T(128)} %bitcast.1.me_ref, bf16[64,3584]{1,0:T(8,128)(2,1)} %refs_0_.11, bf16[3584,4096]{1,0:T(8,128)(2,1)} %refs_1_.11), custom_call_target="tpu_custom_call" | custom-call | flops 469762048 | bytes 7340032 | tf_op jit(solution)/shard_map/last_train_in_a/pallas_call | solution.py:102
  44.9 0.2 collective-permute-done.5
  45.2 1.1 %collective-permute-done.6 = f32[4,64,512]{2,1,0:T(8,128)S(1)} collective-permute-done((f32[4,64,512]{2,1,0:T(8,128)S(1)}, f32[4,64,512]{2,1,0:T(8,128)S(1)}, u32[]{:S(2)}, u32[]{:S(2)}) %collective-permute-start.6) | collective-permute-done | bytes 524320 | tf_op jit(solution)/shard_map/x_ti/ppermute | solution.py:209
  46.4 2.7 %collective-permute-start.9 = (f32[1,64,512]{2,1,0:T(8,128)S(1)}, f32[1,64,512]{2,1,0:T(8,128)S(1)}, u32[]{:S(2)}, u32[]{:S(2)}) collective-permute-start(f32[1,64,512]{2,1,0:T(8,128)S(1)} %slice_add_fusion.9), channel_id=1, source_target_pairs={{0,4},{1,5},{2,6},{3,7},{4,0},{5,1},{6,2},{7,3},{8,12},{9,13},{10,... | collective-permute-start | bytes 393224 | tf_op jit(solution)/shard_map/z2_qi/ppermute | solution.py:209
  49.0 1.4 %collective-permute-start.8 = (f32[2,64,512]{2,1,0:T(8,128)S(1)}, f32[2,64,512]{2,1,0:T(8,128)S(1)}, u32[]{:S(2)}, u32[]{:S(2)}) collective-permute-start(f32[2,64,512]{2,1,0:T(8,128)S(1)} %slice_add_fusion.2), channel_id=1, source_target_pairs={{0,2},{1,3},{2,0},{3,1},{4,6},{5,7},{6,4},{7,5},{8,10},{9,11},{10,... | collective-permute-start | bytes 786440 | tf_op jit(solution)/shard_map/z1_ti/ppermute | solution.py:209
  50.4 4.1 %last_train_in_b.1 = f32[2,64,512]{2,1,0:T(8,128)S(1)} custom-call(s32[1]{0:T(128)} %bitcast.1.me_ref, bf16[64,3584]{1,0:T(8,128)(2,1)} %refs_0_.11, bf16[3584,4096]{1,0:T(8,128)(2,1)} %refs_1_.11), custom_call_target="tpu_custom_call" | custom-call | flops 469762048 | bytes 7340032 | tf_op jit(solution)/shard_map/last_train_in_b/pallas_call | solution.py:102
  54.6 0.4 collective-permute-start.11
  55.0 3.4 %collective-permute-done.8 = f32[2,64,512]{2,1,0:T(8,128)S(1)} collective-permute-done((f32[2,64,512]{2,1,0:T(8,128)S(1)}, f32[2,64,512]{2,1,0:T(8,128)S(1)}, u32[]{:S(2)}, u32[]{:S(2)}) %collective-permute-start.8) | collective-permute-done | bytes 262176 | tf_op jit(solution)/shard_map/z1_ti/ppermute | solution.py:209
  58.5 1.3 %examples.2 = (f32[8,8,128]{2,1,0:T(8,128)S(1)}, f32[8,8,128]{2,1,0:T(8,128)S(1)}, f32[8,8,128]{2,1,0:T(8,128)S(1)}, f32[8,8,128]{2,1,0:T(8,128)S(1)}) custom-call(s32[4]{0:T(128)} %pad_add_fusion.place_ref, f32[1,64,512]{2,1,0:T(8,128)S(1)} %get-tuple-element.135.refs_0_, f32[1,64,512]{2,1,0:T(8,128)S(1)} %collective-permute-done.7.refs_1_, ...), custom_call_target="tpu_custom_call" | custom-call | flops 1 | bytes 1 | tf_op jit(solution)/shard_map/examples/pallas_call | solution.py:165
  59.8 0.5 collective-permute-start.10
  60.2 3.3 %collective-permute-start.12 = (f32[8,8,128]{2,1,0:T(8,128)S(1)}, f32[8,8,128]{2,1,0:T(8,128)S(1)}, u32[]{:S(2)}, u32[]{:S(2)}) collective-permute-start(f32[8,8,128]{2,1,0:T(8,128)S(1)} %get-tuple-element.117), channel_id=1, source_target_pairs={{0,2},{1,3},{2,0},{3,1},{4,6},{5,7},{6,4},{7,5},{8,10},{9,11},{10,... | collective-permute-start | bytes 98312 | tf_op jit(solution)/shard_map/z_query/ppermute | solution.py:209
  63.6 0.3 collective-permute-start.13
  63.8 2.1 %collective-permute-start.14 = (f32[8,8,128]{2,1,0:T(8,128)S(1)}, f32[8,8,128]{2,1,0:T(8,128)S(1)}, u32[]{:S(2)}, u32[]{:S(2)}) collective-permute-start(f32[8,8,128]{2,1,0:T(8,128)S(1)} %get-tuple-element.119), channel_id=1, source_target_pairs={{0,6},{1,7},{2,4},{3,5},{4,2},{5,3},{6,0},{7,1},{8,14},{9,15},{10,... | collective-permute-start | bytes 98312 | tf_op jit(solution)/shard_map/z_query/ppermute | solution.py:209
  65.9 0.8 collective-permute-done.11.refs_1_
  66.7 3.3 %collective-permute-done.13 = f32[8,8,128]{2,1,0:T(8,128)S(1)} collective-permute-done((f32[8,8,128]{2,1,0:T(8,128)S(1)}, f32[8,8,128]{2,1,0:T(8,128)S(1)}, u32[]{:S(2)}, u32[]{:S(2)}) %collective-permute-start.13) | collective-permute-done | bytes 32800 | tf_op jit(solution)/shard_map/z_query/ppermute | solution.py:209
  70.0 0.1 collective-permute-start.18
  70.2 1.3 %examples.3 = (f32[8,8,128]{2,1,0:T(8,128)S(1)}, f32[8,8,128]{2,1,0:T(8,128)S(1)}, f32[8,8,128]{2,1,0:T(8,128)S(1)}, f32[8,8,128]{2,1,0:T(8,128)S(1)}) custom-call(s32[4]{0:T(128)} %pad_add_fusion.place_ref, f32[1,64,512]{2,1,0:T(8,128)S(1)} %slice_add_fusion.6.refs_0_, f32[1,64,512]{2,1,0:T(8,128)S(1)} %collective-permute-done.11.refs_1_, ...), custom_call_target="tpu_custom_call" | custom-call | flops 1 | bytes 1 | tf_op jit(solution)/shard_map/examples/pallas_call | solution.py:165
  71.5 0.0 collective-permute-done.18
  71.5 0.9 %collective-permute-start.19 = (f32[8,8,8,128]{3,2,1,0:T(8,128)S(1)}, f32[8,8,8,128]{3,2,1,0:T(8,128)S(1)}, u32[]{:S(2)}, u32[]{:S(2)}) collective-permute-start(f32[8,8,8,128]{3,2,1,0:T(8,128)S(1)} %constant_dynamic-update-slice_fusion.refs_4_), channel_id=1, source_target_pairs={{0,1},{1,0},{2,3},{3,2},{4,5},{5,4},{6,7},{7,6},{8,9},{9,8},{10,11... | collective-permute-start | bytes 786440 | tf_op jit(solution)/shard_map/x_query/ppermute | solution.py:209
  72.4 0.2 collective-permute-start.15
  72.7 1.8 %collective-permute-start.16 = (f32[8,8,128]{2,1,0:T(8,128)S(1)}, f32[8,8,128]{2,1,0:T(8,128)S(1)}, u32[]{:S(2)}, u32[]{:S(2)}) collective-permute-start(f32[8,8,128]{2,1,0:T(8,128)S(1)} %get-tuple-element.128), channel_id=1, source_target_pairs={{0,4},{1,5},{2,6},{3,7},{4,0},{5,1},{6,2},{7,3},{8,12},{9,13},{10,... | collective-permute-start | bytes 98312 | tf_op jit(solution)/shard_map/z_train/ppermute | solution.py:209
  74.5 2.3 %collective-permute-start.17 = (f32[8,8,128]{2,1,0:T(8,128)S(1)}, f32[8,8,128]{2,1,0:T(8,128)S(1)}, u32[]{:S(2)}, u32[]{:S(2)}) collective-permute-start(f32[8,8,128]{2,1,0:T(8,128)S(1)} %get-tuple-element.129), channel_id=1, source_target_pairs={{0,6},{1,7},{2,4},{3,5},{4,2},{5,3},{6,0},{7,1},{8,14},{9,15},{10,... | collective-permute-start | bytes 98312 | tf_op jit(solution)/shard_map/z_train/ppermute | solution.py:209
  76.8 1.3 %collective-permute-done.16.refs_2_ = f32[8,8,128]{2,1,0:T(8,128)S(1)} collective-permute-done((f32[8,8,128]{2,1,0:T(8,128)S(1)}, f32[8,8,128]{2,1,0:T(8,128)S(1)}, u32[]{:S(2)}, u32[]{:S(2)}) %collective-permute-start.16) | collective-permute-done | bytes 32800 | tf_op jit(solution)/shard_map/z_train/ppermute | solution.py:209
  78.1 2.1 %collective-permute-done.17.refs_3_ = f32[8,8,128]{2,1,0:T(8,128)S(1)} collective-permute-done((f32[8,8,128]{2,1,0:T(8,128)S(1)}, f32[8,8,128]{2,1,0:T(8,128)S(1)}, u32[]{:S(2)}, u32[]{:S(2)}) %collective-permute-start.17) | collective-permute-done | bytes 32800 | tf_op jit(solution)/shard_map/z_train/ppermute | solution.py:209
  80.2 0.1 collective-permute-done.19.refs_5_
  80.2 1.0 %partial_scores.1 = f32[64,128]{1,0:T(8,128)S(1)} custom-call(s32[4]{0:T(128)} %pad_add_fusion.place_ref, f32[8,8,128]{2,1,0:T(8,128)S(1)} %get-tuple-element.126.refs_0_, f32[8,8,128]{2,1,0:T(8,128)S(1)} %collective-permute-done.15.refs_1_, f32[8,8,128]{2,1,0:T(8,128)S(1)} %collective-permute-done.16.refs_2_, ...), custom_call_target="tpu_custom_call" | custom-call | tf_op jit(solution)/shard_map/partial_scores/pallas_call | solution.py:194
  81.3 0.4 collective-permute-start.20
  81.7 4.5 %collective-permute-done.20 = f32[64,128]{1,0:T(8,128)S(1)} collective-permute-done((f32[64,128]{1,0:T(8,128)S(1)}, f32[64,128]{1,0:T(8,128)S(1)}, u32[]{:S(2)}, u32[]{:S(2)}) %collective-permute-start.20) | collective-permute-done | bytes 32800 | tf_op jit(solution)/shard_map/scores/ppermute | solution.py:209
  86.2 0.9 collective-permute-start.21
  87.1 3.0 %collective-permute-done.21 = f32[64,128]{1,0:T(8,128)S(1)} collective-permute-done((f32[64,128]{1,0:T(8,128)S(1)}, f32[64,128]{1,0:T(8,128)S(1)}, u32[]{:S(2)}, u32[]{:S(2)}) %collective-permute-start.21) | collective-permute-done | bytes 32800 | tf_op jit(solution)/shard_map/scores/ppermute | solution.py:209
  90.1 1.2 %collective-permute-start.22 = (f32[64,128]{1,0:T(8,128)S(1)}, f32[64,128]{1,0:T(8,128)S(1)}, u32[]{:S(2)}, u32[]{:S(2)}) collective-permute-start(f32[64,128]{1,0:T(8,128)S(1)} %add.96), channel_id=1, source_target_pairs={{0,1},{1,0},{2,3},{3,2},{4,5},{5,4},{6,7},{7,6},{8,9},{9,8},{10,11... | collective-permute-start | bytes 98312 | tf_op jit(solution)/shard_map/scores/ppermute | solution.py:209
  91.3 2.7 %collective-permute-done.22 = f32[64,128]{1,0:T(8,128)S(1)} collective-permute-done((f32[64,128]{1,0:T(8,128)S(1)}, f32[64,128]{1,0:T(8,128)S(1)}, u32[]{:S(2)}, u32[]{:S(2)}) %collective-permute-start.22) | collective-permute-done | bytes 32800 | tf_op jit(solution)/shard_map/scores/ppermute | solution.py:209
  94.0 0.6 add.97
  (36 shorter events, 0.4 us)
Async XLA Ops:
  5.5 20.0 %collective-permute-start = (f32[4,64,512]{2,1,0:T(8,128)S(1)}, f32[4,64,512]{2,1,0:T(8,128)S(1)}, u32[]{:S(2)}, u32[]{:S(2)}) collective-permute-start(f32[4,64,512]{2,1,0:T(8,128)S(1)} %get-tuple-element.70), channel_id=1, source_target_pairs={{0,2},{1,3},{2,0},{3,1},{4,6},{5,7},{6,4},{7,5},{8,10},{9,11},{10,... | collective-permute-start | bytes 1572872 | tf_op jit(solution)/shard_map/z1_qo/ppermute | solution.py:209
  14.9 20.7 %collective-permute-start.3 = (f32[4,64,512]{2,1,0:T(8,128)S(1)}, f32[4,64,512]{2,1,0:T(8,128)S(1)}, u32[]{:S(2)}, u32[]{:S(2)}) collective-permute-start(f32[4,64,512]{2,1,0:T(8,128)S(1)} %first_query_in.1), channel_id=1, source_target_pairs={{0,1},{1,0},{2,3},{3,2},{4,5},{5,4},{6,7},{7,6},{8,9},{9,8},{10,11... | collective-permute-start | bytes 1572872 | tf_op jit(solution)/shard_map/x_qi/ppermute | solution.py:209
  16.5 23.5 %collective-permute-start.1 = (f32[4,64,512]{2,1,0:T(8,128)S(1)}, f32[4,64,512]{2,1,0:T(8,128)S(1)}, u32[]{:S(2)}, u32[]{:S(2)}) collective-permute-start(f32[4,64,512]{2,1,0:T(8,128)S(1)} %get-tuple-element.79), channel_id=1, source_target_pairs={{0,2},{1,3},{2,0},{3,1},{4,6},{5,7},{6,4},{7,5},{8,10},{9,11},{10,... | collective-permute-start | bytes 1572872 | tf_op jit(solution)/shard_map/z1_to/ppermute | solution.py:209
  25.5 0.8 copy-start.2
  25.6 11.7 %collective-permute-start.2 = (f32[2,64,512]{2,1,0:T(8,128)S(1)}, f32[2,64,512]{2,1,0:T(8,128)S(1)}, u32[]{:S(2)}, u32[]{:S(2)}) collective-permute-start(f32[2,64,512]{2,1,0:T(8,128)S(1)} %slice_add_fusion.1), channel_id=1, source_target_pairs={{0,1},{1,0},{2,3},{3,2},{4,5},{5,4},{6,7},{7,6},{8,9},{9,8},{10,11... | collective-permute-start | bytes 786440 | tf_op jit(solution)/shard_map/x_qo/ppermute | solution.py:209
  26.3 10.9 %copy-start.3 = (f32[4,64,512]{2,1,0:T(8,128)S(1)}, f32[4,64,512]{2,1,0:T(8,128)}, u32[]{:S(2)}) copy-start(f32[4,64,512]{2,1,0:T(8,128)} %copy-done.2) | copy-start | bytes 1572868
  26.3 19.9 %collective-permute-start.6 = (f32[4,64,512]{2,1,0:T(8,128)S(1)}, f32[4,64,512]{2,1,0:T(8,128)S(1)}, u32[]{:S(2)}, u32[]{:S(2)}) collective-permute-start(f32[4,64,512]{2,1,0:T(8,128)S(1)} %get-tuple-element.75), channel_id=1, source_target_pairs={{0,1},{1,0},{2,3},{3,2},{4,5},{5,4},{6,7},{7,6},{8,9},{9,8},{10,11... | collective-permute-start | bytes 1572872 | tf_op jit(solution)/shard_map/x_ti/ppermute | solution.py:209
  35.6 9.5 %collective-permute-start.5 = (f32[2,64,512]{2,1,0:T(8,128)S(1)}, f32[2,64,512]{2,1,0:T(8,128)S(1)}, u32[]{:S(2)}, u32[]{:S(2)}) collective-permute-start(f32[2,64,512]{2,1,0:T(8,128)S(1)} %slice_add_fusion), channel_id=1, source_target_pairs={{0,2},{1,3},{2,0},{3,1},{4,6},{5,7},{6,4},{7,5},{8,10},{9,11},{10,... | collective-permute-start | bytes 786440 | tf_op jit(solution)/shard_map/z1_qi/ppermute | solution.py:209
  37.3 17.2 %collective-permute-start.7 = (f32[1,64,512]{2,1,0:T(8,128)S(1)}, f32[1,64,512]{2,1,0:T(8,128)S(1)}, u32[]{:S(2)}, u32[]{:S(2)}) collective-permute-start(f32[1,64,512]{2,1,0:T(8,128)S(1)} %get-tuple-element.136), channel_id=1, source_target_pairs={{0,4},{1,5},{2,6},{3,7},{4,0},{5,1},{6,2},{7,3},{8,12},{9,13},{10,... | collective-permute-start | bytes 393224 | tf_op jit(solution)/shard_map/z2_qo/ppermute | solution.py:209
  40.1 14.5 %collective-permute-start.4 = (f32[2,64,512]{2,1,0:T(8,128)S(1)}, f32[2,64,512]{2,1,0:T(8,128)S(1)}, u32[]{:S(2)}, u32[]{:S(2)}) collective-permute-start(f32[2,64,512]{2,1,0:T(8,128)S(1)} %slice_add_fusion.3), channel_id=1, source_target_pairs={{0,1},{1,0},{2,3},{3,2},{4,5},{5,4},{6,7},{7,6},{8,9},{9,8},{10,11... | collective-permute-start | bytes 786440 | tf_op jit(solution)/shard_map/x_to/ppermute | solution.py:209
  40.8 17.7 %copy-start = (s32[4096]{0:T(1024)S(1)}, s32[4096]{0:T(1024)}, u32[]{:S(2)}) copy-start(s32[4096]{0:T(1024)} %param.15) | copy-start | bytes 49156
  40.8 29.4 %copy-start.1 = (s32[4096]{0:T(1024)S(1)}, s32[4096]{0:T(1024)}, u32[]{:S(2)}) copy-start(s32[4096]{0:T(1024)} %param.14) | copy-start | bytes 49156
  46.4 12.1 %collective-permute-start.9 = (f32[1,64,512]{2,1,0:T(8,128)S(1)}, f32[1,64,512]{2,1,0:T(8,128)S(1)}, u32[]{:S(2)}, u32[]{:S(2)}) collective-permute-start(f32[1,64,512]{2,1,0:T(8,128)S(1)} %slice_add_fusion.9), channel_id=1, source_target_pairs={{0,4},{1,5},{2,6},{3,7},{4,0},{5,1},{6,2},{7,3},{8,12},{9,13},{10,... | collective-permute-start | bytes 393224 | tf_op jit(solution)/shard_map/z2_qi/ppermute | solution.py:209
  49.0 9.4 %collective-permute-start.8 = (f32[2,64,512]{2,1,0:T(8,128)S(1)}, f32[2,64,512]{2,1,0:T(8,128)S(1)}, u32[]{:S(2)}, u32[]{:S(2)}) collective-permute-start(f32[2,64,512]{2,1,0:T(8,128)S(1)} %slice_add_fusion.2), channel_id=1, source_target_pairs={{0,2},{1,3},{2,0},{3,1},{4,6},{5,7},{6,4},{7,5},{8,10},{9,11},{10,... | collective-permute-start | bytes 786440 | tf_op jit(solution)/shard_map/z1_ti/ppermute | solution.py:209
  54.6 12.1 %collective-permute-start.11 = (f32[1,64,512]{2,1,0:T(8,128)S(1)}, f32[1,64,512]{2,1,0:T(8,128)S(1)}, u32[]{:S(2)}, u32[]{:S(2)}) collective-permute-start(f32[1,64,512]{2,1,0:T(8,128)S(1)} %slice_add_fusion.7), channel_id=1, source_target_pairs={{0,4},{1,5},{2,6},{3,7},{4,0},{5,1},{6,2},{7,3},{8,12},{9,13},{10,... | collective-permute-start | bytes 393224 | tf_op jit(solution)/shard_map/z2_to/ppermute | solution.py:209
  59.8 10.2 %collective-permute-start.10 = (f32[1,64,512]{2,1,0:T(8,128)S(1)}, f32[1,64,512]{2,1,0:T(8,128)S(1)}, u32[]{:S(2)}, u32[]{:S(2)}) collective-permute-start(f32[1,64,512]{2,1,0:T(8,128)S(1)} %slice_add_fusion.5), channel_id=1, source_target_pairs={{0,4},{1,5},{2,6},{3,7},{4,0},{5,1},{6,2},{7,3},{8,12},{9,13},{10,... | collective-permute-start | bytes 393224 | tf_op jit(solution)/shard_map/z2_ti/ppermute | solution.py:209
  60.2 6.5 %collective-permute-start.12 = (f32[8,8,128]{2,1,0:T(8,128)S(1)}, f32[8,8,128]{2,1,0:T(8,128)S(1)}, u32[]{:S(2)}, u32[]{:S(2)}) collective-permute-start(f32[8,8,128]{2,1,0:T(8,128)S(1)} %get-tuple-element.117), channel_id=1, source_target_pairs={{0,2},{1,3},{2,0},{3,1},{4,6},{5,7},{6,4},{7,5},{8,10},{9,11},{10,... | collective-permute-start | bytes 98312 | tf_op jit(solution)/shard_map/z_query/ppermute | solution.py:209
  63.6 6.5 %collective-permute-start.13 = (f32[8,8,128]{2,1,0:T(8,128)S(1)}, f32[8,8,128]{2,1,0:T(8,128)S(1)}, u32[]{:S(2)}, u32[]{:S(2)}) collective-permute-start(f32[8,8,128]{2,1,0:T(8,128)S(1)} %get-tuple-element.118), channel_id=1, source_target_pairs={{0,4},{1,5},{2,6},{3,7},{4,0},{5,1},{6,2},{7,3},{8,12},{9,13},{10,... | collective-permute-start | bytes 98312 | tf_op jit(solution)/shard_map/z_query/ppermute | solution.py:209
  63.8 6.2 %collective-permute-start.14 = (f32[8,8,128]{2,1,0:T(8,128)S(1)}, f32[8,8,128]{2,1,0:T(8,128)S(1)}, u32[]{:S(2)}, u32[]{:S(2)}) collective-permute-start(f32[8,8,128]{2,1,0:T(8,128)S(1)} %get-tuple-element.119), channel_id=1, source_target_pairs={{0,6},{1,7},{2,4},{3,5},{4,2},{5,3},{6,0},{7,1},{8,14},{9,15},{10,... | collective-permute-start | bytes 98312 | tf_op jit(solution)/shard_map/z_query/ppermute | solution.py:209
  70.0 1.4 %collective-permute-start.18 = (f32[4,8,8,128]{3,2,1,0:T(8,128)S(1)}, f32[4,8,8,128]{3,2,1,0:T(8,128)S(1)}, u32[]{:S(2)}, u32[]{:S(2)}) collective-permute-start(f32[4,8,8,128]{3,2,1,0:T(8,128)S(1)} %pad_maximum_fusion), channel_id=1, source_target_pairs={{0,8},{8,0},{1,9},{9,1},{2,10},{10,2},{3,11},{11,3},{4,12},{12,4},... | collective-permute-start | bytes 393224 | tf_op jit(solution)/shard_map/dp_query/ppermute | solution.py:214
  71.5 8.8 %collective-permute-start.19 = (f32[8,8,8,128]{3,2,1,0:T(8,128)S(1)}, f32[8,8,8,128]{3,2,1,0:T(8,128)S(1)}, u32[]{:S(2)}, u32[]{:S(2)}) collective-permute-start(f32[8,8,8,128]{3,2,1,0:T(8,128)S(1)} %constant_dynamic-update-slice_fusion.refs_4_), channel_id=1, source_target_pairs={{0,1},{1,0},{2,3},{3,2},{4,5},{5,4},{6,7},{7,6},{8,9},{9,8},{10,11... | collective-permute-start | bytes 786440 | tf_op jit(solution)/shard_map/x_query/ppermute | solution.py:209
  72.4 4.4 %collective-permute-start.15 = (f32[8,8,128]{2,1,0:T(8,128)S(1)}, f32[8,8,128]{2,1,0:T(8,128)S(1)}, u32[]{:S(2)}, u32[]{:S(2)}) collective-permute-start(f32[8,8,128]{2,1,0:T(8,128)S(1)} %get-tuple-element.127), channel_id=1, source_target_pairs={{0,2},{1,3},{2,0},{3,1},{4,6},{5,7},{6,4},{7,5},{8,10},{9,11},{10,... | collective-permute-start | bytes 98312 | tf_op jit(solution)/shard_map/z_train/ppermute | solution.py:209
  72.7 5.4 %collective-permute-start.16 = (f32[8,8,128]{2,1,0:T(8,128)S(1)}, f32[8,8,128]{2,1,0:T(8,128)S(1)}, u32[]{:S(2)}, u32[]{:S(2)}) collective-permute-start(f32[8,8,128]{2,1,0:T(8,128)S(1)} %get-tuple-element.128), channel_id=1, source_target_pairs={{0,4},{1,5},{2,6},{3,7},{4,0},{5,1},{6,2},{7,3},{8,12},{9,13},{10,... | collective-permute-start | bytes 98312 | tf_op jit(solution)/shard_map/z_train/ppermute | solution.py:209
  74.5 5.7 %collective-permute-start.17 = (f32[8,8,128]{2,1,0:T(8,128)S(1)}, f32[8,8,128]{2,1,0:T(8,128)S(1)}, u32[]{:S(2)}, u32[]{:S(2)}) collective-permute-start(f32[8,8,128]{2,1,0:T(8,128)S(1)} %get-tuple-element.129), channel_id=1, source_target_pairs={{0,6},{1,7},{2,4},{3,5},{4,2},{5,3},{6,0},{7,1},{8,14},{9,15},{10,... | collective-permute-start | bytes 98312 | tf_op jit(solution)/shard_map/z_train/ppermute | solution.py:209
  81.3 4.9 %collective-permute-start.20 = (f32[64,128]{1,0:T(8,128)S(1)}, f32[64,128]{1,0:T(8,128)S(1)}, u32[]{:S(2)}, u32[]{:S(2)}) collective-permute-start(f32[64,128]{1,0:T(8,128)S(1)} %partial_scores.1), channel_id=1, source_target_pairs={{0,4},{1,5},{2,6},{3,7},{4,0},{5,1},{6,2},{7,3},{8,12},{9,13},{10,... | collective-permute-start | bytes 98312 | tf_op jit(solution)/shard_map/scores/ppermute | solution.py:209
  86.2 3.9 %collective-permute-start.21 = (f32[64,128]{1,0:T(8,128)S(1)}, f32[64,128]{1,0:T(8,128)S(1)}, u32[]{:S(2)}, u32[]{:S(2)}) collective-permute-start(f32[64,128]{1,0:T(8,128)S(1)} %add.95), channel_id=1, source_target_pairs={{0,2},{1,3},{2,0},{3,1},{4,6},{5,7},{6,4},{7,5},{8,10},{9,11},{10,... | collective-permute-start | bytes 98312 | tf_op jit(solution)/shard_map/scores/ppermute | solution.py:209
  90.1 3.9 %collective-permute-start.22 = (f32[64,128]{1,0:T(8,128)S(1)}, f32[64,128]{1,0:T(8,128)S(1)}, u32[]{:S(2)}, u32[]{:S(2)}) collective-permute-start(f32[64,128]{1,0:T(8,128)S(1)} %add.96), channel_id=1, source_target_pairs={{0,1},{1,0},{2,3},{3,2},{4,5},{5,4},{6,7},{7,6},{8,9},{9,8},{10,11... | collective-permute-start | bytes 98312 | tf_op jit(solution)/shard_map/scores/ppermute | solution.py:209

commit v5 on v4

--- a/solution.py
+++ b/solution.py
@@ -169,6 +169,7 @@
         out_specs=[vmem] * 4,
         scratch_shapes=[pltpu.VMEM((4, HALF // 4, SEGS, 2 * RANK), jnp.float32)],
         cost_estimate=pl.CostEstimate(flops=1, bytes_accessed=1, transcendentals=0),
+        compiler_params=pltpu.CompilerParams(vmem_limit_bytes=8 * 1024 * 1024),
         name="examples",
     )(place, *map(near, (*outs, *inners, slots.reshape(blocks, 1, BLK))))
 
@@ -200,6 +201,7 @@
             pltpu.VMEM((16, HALF // 4, SEGS, 2 * RANK), jnp.float32),
             pltpu.VMEM((4, HALF // 4, SEGS, 2 * RANK), jnp.float32),
         ],
+        compiler_params=pltpu.CompilerParams(vmem_limit_bytes=8 * 1024 * 1024),
         name="partial_scores",
     )(place, *map(near, (*trains, *queries)))
 
@@ -228,11 +230,12 @@
     ins, outs = (basis_in, query_acts), (basis_out, query_grads)
     train_ins, train_outs = (basis_in, train_acts), (basis_out, train_grads)
 
-    qo_send, to_send = project(me, [outs, train_outs], [(0, Z_FIRST[4:]), (1, Z_FIRST[4:])], "first_outs")
+    (qo_send,) = project(me, [outs], [(0, Z_FIRST[4:])], "first_query_out")
     qo1 = swap(qo_send, Z1, "z1_qo")
     me = after(me, qo_send)
-    (qi_send,) = project(me, [ins], [(0, X_FIRST[4:])], "first_query_in")
-    to_send = after(to_send, qi_send)
+    to_send, qi_send = project(
+        me, [train_outs, ins], [(0, Z_FIRST[4:]), (1, X_FIRST[4:])], "first_query_in"
+    )
     qi1 = swap(qi_send, X, "x_qi")
     to1 = swap(to_send, Z1, "z1_to")
     me = after(me, qi_send)
@@ -254,13 +257,13 @@
     qo = qo[:1] + qo1[:1] + qo2[:1]
     me = after(me, to_send, qo)
     (ti_late,) = project(me, [train_ins], [(0, X_FIRST[2:4])], "last_train_in_a")
-    ti_late, qi2, ti1 = lax.optimization_barrier((ti_late, qi2, ti1))
+    ti_late, qi2 = lax.optimization_barrier((ti_late, qi2))
+    qi_send = qi[1:2] + qi1[1:2] + qi2[1:2]
+    qi3 = swap(qi_send, Z2, "z2_qi")
+    ti_late, ti1, _ = lax.optimization_barrier((ti_late, ti1, qi_send))
     ti_send = ti_late + ti1[2:]
     ti2 = swap(ti_send, Z1, "z1_ti")
-    qi, qi1, qi2, _ = lax.optimization_barrier((qi, qi1, qi2, ti_send))
-    qi_send = qi[1:2] + qi1[1:2] + qi2[1:2]
-    qi3 = swap(qi_send, Z2, "z2_qi")
-    me = after(me, qi_send)
+    me = after(me, ti_send)
     (ti,) = project(me, [train_ins], [(0, X_FIRST[:2])], "last_train_in_b")
     ti, qo3 = lax.optimization_barrier((ti, qo3))
     qi, qi1, qi2, _ = lax.optimization_barrier((qi, qi1, qi2, ti))

time: 94.8 us -> 93.5 us (0.986)
  starting transfers between devices: 30.1 us -> 32.7 us
  waiting for transfers between devices: 22.5 us -> 21 us
  Pallas kernels: 39.4 us -> 38.2 us
    ppermute x22, starting transfers between devices: 30 us -> 32.6 us  [swap(): return lax.ppermute(value, 'tensor', [(i, i ^ mask) for i in range(8)])]
    ppermute x22, waiting for transfers between devices: 22.5 us -> 20.9 us  [swap(): return lax.ppermute(value, 'tensor', [(i, i ^ mask) for i in range(8)])]
  transfers between devices with their start and end apart: 23 -> 23, of which waited for: 11 -> 10; matrix products, arithmetic and copies ran while one was open for 1% -> 1% of each run, Pallas kernels for 35% -> 37%
where the time goes in v5:
time: 93.5 us; the launch traced here: 93.4 us
  Pallas kernels  38.2 us (41%)
  starting transfers between devices  32.7 us (35%)
  waiting for transfers between devices  21 us (22%)
  other arithmetic  1.14 us (1%)
    pallas_call x6, Pallas kernels, project(): pl.pallas_call(kernel, out_shape=[pltpu.VMEM((len(masks), RANK, BLK), jnp...  35 us
    ppermute x22, starting transfers between devices, swap(): return lax.ppermute(value, 'tensor', [(i, i ^ mask) for i in range(8)])  32.6 us
    ppermute x22, waiting for transfers between devices, swap(): return lax.ppermute(value, 'tensor', [(i, i ^ mask) for i in range(8)])  20.9 us
    pallas_call x2, Pallas kernels, examples(): pl.pallas_call(kernel, out_shape=[pltpu.VMEM((HALF // 4, SEGS, 2 * RANK),...  2.3 us
  transfers between devices with their start and end apart: 23, of which 10 were waited for; matrix products, arithmetic and copies ran while one was open for 1% of the time, Pallas kernels for 37%

profile of v5, /device:TPU:0, one launch (start us, length us, event | category | flops | bytes accessed | tf_op | source)
XLA Modules:
  0.0 93.4 jit_solution(2055364816540660577)
XLA Ops:
  0.0 3.1 %first_query_out.1 = f32[4,64,512]{2,1,0:T(8,128)S(1)} custom-call(s32[1]{0:T(128)} %bitcast.1.me_ref, bf16[64,1024]{1,0:T(8,128)(2,1)} %refs_0_.9, bf16[1024,4096]{1,0:T(8,128)(2,1)} %refs_2_.4), custom_call_target="tpu_custom_call" | custom-call | flops 268435456 | bytes 4194304 | tf_op jit(solution)/shard_map/first_query_out/pallas_call | solution.py:102
  3.1 3.1 %collective-permute-start = (f32[4,64,512]{2,1,0:T(8,128)S(1)}, f32[4,64,512]{2,1,0:T(8,128)S(1)}, u32[]{:S(2)}, u32[]{:S(2)}) collective-permute-start(f32[4,64,512]{2,1,0:T(8,128)S(1)} %first_query_out.1), channel_id=1, source_target_pairs={{0,2},{1,3},{2,0},{3,1},{4,6},{5,7},{6,4},{7,5},{8,10},{9,11},{10,... | collective-permute-start | bytes 1572872 | tf_op jit(solution)/shard_map/z1_qo/ppermute | solution.py:211
  6.2 7.9 %first_query_in.1 = (f32[4,64,512]{2,1,0:T(8,128)S(1)}, f32[4,64,512]{2,1,0:T(8,128)S(1)}) custom-call(s32[1]{0:T(128)} %bitcast.1.me_ref, bf16[64,1024]{1,0:T(8,128)(2,1)} %refs_0_.9, bf16[64,3584]{1,0:T(8,128)(2,1)} %refs_0_.11, bf16[1024,4096]{1,0:T(8,128)(2,1)} %refs_2_.5, bf16[3584,4096]{1,0:T(8,128)(2,1)} %refs_3_.5), custom_call_target="tpu_custom_call" | custom-call | flops 1207959552 | bytes 18874368 | tf_op jit(solution)/shard_map/first_query_in/pallas_call | solution.py:102
  14.1 0.1 collective-permute-start.1
  14.2 1.9 %collective-permute-start.3 = (f32[4,64,512]{2,1,0:T(8,128)S(1)}, f32[4,64,512]{2,1,0:T(8,128)S(1)}, u32[]{:S(2)}, u32[]{:S(2)}) collective-permute-start(f32[4,64,512]{2,1,0:T(8,128)S(1)} %get-tuple-element.68), channel_id=1, source_target_pairs={{0,1},{1,0},{2,3},{3,2},{4,5},{5,4},{6,7},{7,6},{8,9},{9,8},{10,11... | collective-permute-start | bytes 1572872 | tf_op jit(solution)/shard_map/x_qi/ppermute | solution.py:211
  16.1 0.1 pad_add_fusion.place_ref
  16.2 7.9 %middle_a.1 = (f32[4,64,512]{2,1,0:T(8,128)S(1)}, f32[4,64,512]{2,1,0:T(8,128)S(1)}) custom-call(s32[1]{0:T(128)} %bitcast.1.me_ref, bf16[64,1024]{1,0:T(8,128)(2,1)} %refs_0_.9, bf16[64,3584]{1,0:T(8,128)(2,1)} %refs_0_.11, bf16[1024,4096]{1,0:T(8,128)(2,1)} %refs_2_.4, bf16[3584,4096]{1,0:T(8,128)(2,1)} %refs_1_.11), custom_call_target="tpu_custom_call" | custom-call | flops 1207959552 | bytes 18874368 | tf_op jit(solution)/shard_map/middle_a/pallas_call | solution.py:102
  24.2 0.2 collective-permute-start.2
  24.4 1.9 %collective-permute-start.6 = (f32[4,64,512]{2,1,0:T(8,128)S(1)}, f32[4,64,512]{2,1,0:T(8,128)S(1)}, u32[]{:S(2)}, u32[]{:S(2)}) collective-permute-start(f32[4,64,512]{2,1,0:T(8,128)S(1)} %get-tuple-element.72), channel_id=1, source_target_pairs={{0,1},{1,0},{2,3},{3,2},{4,5},{5,4},{6,7},{7,6},{8,9},{9,8},{10,11... | collective-permute-start | bytes 1572872 | tf_op jit(solution)/shard_map/x_ti/ppermute | solution.py:211
  26.3 7.9 %middle_b.1 = (f32[4,64,512]{2,1,0:T(8,128)S(1)}, f32[4,64,512]{2,1,0:T(8,128)S(1)}) custom-call(s32[1]{0:T(128)} %bitcast.1.me_ref, bf16[64,1024]{1,0:T(8,128)(2,1)} %refs_0_.9, bf16[64,3584]{1,0:T(8,128)(2,1)} %refs_0_.11, bf16[1024,4096]{1,0:T(8,128)(2,1)} %refs_2_.5, bf16[3584,4096]{1,0:T(8,128)(2,1)} %refs_3_.5), custom_call_target="tpu_custom_call" | custom-call | flops 1207959552 | bytes 18874368 | tf_op jit(solution)/shard_map/middle_b/pallas_call | solution.py:102
  34.2 0.0 collective-permute-done.3
  34.2 1.6 %collective-permute-start.5 = (f32[2,64,512]{2,1,0:T(8,128)S(1)}, f32[2,64,512]{2,1,0:T(8,128)S(1)}, u32[]{:S(2)}, u32[]{:S(2)}) collective-permute-start(f32[2,64,512]{2,1,0:T(8,128)S(1)} %slice_add_fusion), channel_id=1, source_target_pairs={{0,2},{1,3},{2,0},{3,1},{4,6},{5,7},{6,4},{7,5},{8,10},{9,11},{10,... | collective-permute-start | bytes 786440 | tf_op jit(solution)/shard_map/z1_qi/ppermute | solution.py:211
  35.9 0.1 slice_add_fusion.10
  36.0 2.7 %collective-permute-start.7 = (f32[1,64,512]{2,1,0:T(8,128)S(1)}, f32[1,64,512]{2,1,0:T(8,128)S(1)}, u32[]{:S(2)}, u32[]{:S(2)}) collective-permute-start(f32[1,64,512]{2,1,0:T(8,128)S(1)} %get-tuple-element.130), channel_id=1, source_target_pairs={{0,4},{1,5},{2,6},{3,7},{4,0},{5,1},{6,2},{7,3},{8,12},{9,13},{10,... | collective-permute-start | bytes 393224 | tf_op jit(solution)/shard_map/z2_qo/ppermute | solution.py:211
  38.7 0.8 collective-permute-start.4
  39.5 4.1 %last_train_in_a.1 = f32[2,64,512]{2,1,0:T(8,128)S(1)} custom-call(s32[1]{0:T(128)} %bitcast.1.me_ref, bf16[64,3584]{1,0:T(8,128)(2,1)} %refs_0_.11, bf16[3584,4096]{1,0:T(8,128)(2,1)} %refs_1_.11), custom_call_target="tpu_custom_call" | custom-call | flops 469762048 | bytes 7340032 | tf_op jit(solution)/shard_map/last_train_in_a/pallas_call | solution.py:102
  43.5 0.2 collective-permute-done.5
  43.8 1.7 %collective-permute-start.9 = (f32[1,64,512]{2,1,0:T(8,128)S(1)}, f32[1,64,512]{2,1,0:T(8,128)S(1)}, u32[]{:S(2)}, u32[]{:S(2)}) collective-permute-start(f32[1,64,512]{2,1,0:T(8,128)S(1)} %fusion), channel_id=1, source_target_pairs={{0,4},{1,5},{2,6},{3,7},{4,0},{5,1},{6,2},{7,3},{8,12},{9,13},{10,... | collective-permute-start | bytes 393224 | tf_op jit(solution)/shard_map/z2_qi/ppermute | solution.py:211
  45.5 0.4 collective-permute-done.6
  46.0 2.1 %collective-permute-start.8 = (f32[2,64,512]{2,1,0:T(8,128)S(1)}, f32[2,64,512]{2,1,0:T(8,128)S(1)}, u32[]{:S(2)}, u32[]{:S(2)}) collective-permute-start(f32[2,64,512]{2,1,0:T(8,128)S(1)} %slice_add_fusion.2), channel_id=1, source_target_pairs={{0,2},{1,3},{2,0},{3,1},{4,6},{5,7},{6,4},{7,5},{8,10},{9,11},{10,... | collective-permute-start | bytes 786440 | tf_op jit(solution)/shard_map/z1_ti/ppermute | solution.py:211
  48.1 4.1 %last_train_in_b.1 = f32[2,64,512]{2,1,0:T(8,128)S(1)} custom-call(s32[1]{0:T(128)} %bitcast.1.me_ref, bf16[64,3584]{1,0:T(8,128)(2,1)} %refs_0_.11, bf16[3584,4096]{1,0:T(8,128)(2,1)} %refs_1_.11), custom_call_target="tpu_custom_call" | custom-call | flops 469762048 | bytes 7340032 | tf_op jit(solution)/shard_map/last_train_in_b/pallas_call | solution.py:102
  52.3 0.0 collective-permute-done.4
  52.3 2.6 %collective-permute-start.11 = (f32[1,64,512]{2,1,0:T(8,128)S(1)}, f32[1,64,512]{2,1,0:T(8,128)S(1)}, u32[]{:S(2)}, u32[]{:S(2)}) collective-permute-start(f32[1,64,512]{2,1,0:T(8,128)S(1)} %slice_add_fusion.8), channel_id=1, source_target_pairs={{0,4},{1,5},{2,6},{3,7},{4,0},{5,1},{6,2},{7,3},{8,12},{9,13},{10,... | collective-permute-start | bytes 393224 | tf_op jit(solution)/shard_map/z2_to/ppermute | solution.py:211
  54.9 0.1 collective-permute-done.8
  55.0 1.1 %examples.2 = (f32[8,8,128]{2,1,0:T(8,128)S(1)}, f32[8,8,128]{2,1,0:T(8,128)S(1)}, f32[8,8,128]{2,1,0:T(8,128)S(1)}, f32[8,8,128]{2,1,0:T(8,128)S(1)}) custom-call(s32[4]{0:T(128)S(1)} %pad_add_fusion.place_ref, f32[1,64,512]{2,1,0:T(8,128)S(1)} %get-tuple-element.129.refs_0_, f32[1,64,512]{2,1,0:T(8,128)S(1)} %collective-permute-done.7.refs_1_, ...), custom_call_target="tpu_custom_call" | custom-call | flops 1 | bytes 1 | tf_op jit(solution)/shard_map/examples/pallas_call | solution.py:165
  56.2 2.6 %collective-permute-start.10 = (f32[1,64,512]{2,1,0:T(8,128)S(1)}, f32[1,64,512]{2,1,0:T(8,128)S(1)}, u32[]{:S(2)}, u32[]{:S(2)}) collective-permute-start(f32[1,64,512]{2,1,0:T(8,128)S(1)} %slice_add_fusion.6), channel_id=1, source_target_pairs={{0,4},{1,5},{2,6},{3,7},{4,0},{5,1},{6,2},{7,3},{8,12},{9,13},{10,... | collective-permute-start | bytes 393224 | tf_op jit(solution)/shard_map/z2_ti/ppermute | solution.py:211
  58.8 2.1 %collective-permute-start.12 = (f32[8,8,128]{2,1,0:T(8,128)S(1)}, f32[8,8,128]{2,1,0:T(8,128)S(1)}, u32[]{:S(2)}, u32[]{:S(2)}) collective-permute-start(f32[8,8,128]{2,1,0:T(8,128)S(1)} %get-tuple-element.111), channel_id=1, source_target_pairs={{0,2},{1,3},{2,0},{3,1},{4,6},{5,7},{6,4},{7,5},{8,10},{9,11},{10,... | collective-permute-start | bytes 98312 | tf_op jit(solution)/shard_map/z_query/ppermute | solution.py:211
  61.0 0.7 collective-permute-start.13
  61.7 1.6 %collective-permute-start.14 = (f32[8,8,128]{2,1,0:T(8,128)S(1)}, f32[8,8,128]{2,1,0:T(8,128)S(1)}, u32[]{:S(2)}, u32[]{:S(2)}) collective-permute-start(f32[8,8,128]{2,1,0:T(8,128)S(1)} %get-tuple-element.113), channel_id=1, source_target_pairs={{0,6},{1,7},{2,4},{3,5},{4,2},{5,3},{6,0},{7,1},{8,14},{9,15},{10,... | collective-permute-start | bytes 98312 | tf_op jit(solution)/shard_map/z_query/ppermute | solution.py:211
  63.4 0.0 collective-permute-done.12
  63.4 4.3 %collective-permute-done.13 = f32[8,8,128]{2,1,0:T(8,128)S(1)} collective-permute-done((f32[8,8,128]{2,1,0:T(8,128)S(1)}, f32[8,8,128]{2,1,0:T(8,128)S(1)}, u32[]{:S(2)}, u32[]{:S(2)}) %collective-permute-start.13) | collective-permute-done | bytes 32800 | tf_op jit(solution)/shard_map/z_query/ppermute | solution.py:211
  67.8 0.1 collective-permute-start.18
  67.9 1.2 %examples.3 = (f32[8,8,128]{2,1,0:T(8,128)S(1)}, f32[8,8,128]{2,1,0:T(8,128)S(1)}, f32[8,8,128]{2,1,0:T(8,128)S(1)}, f32[8,8,128]{2,1,0:T(8,128)S(1)}) custom-call(s32[4]{0:T(128)S(1)} %pad_add_fusion.place_ref, f32[1,64,512]{2,1,0:T(8,128)S(1)} %slice_add_fusion.7.refs_0_, f32[1,64,512]{2,1,0:T(8,128)S(1)} %collective-permute-done.11.refs_1_, ...), custom_call_target="tpu_custom_call" | custom-call | flops 1 | bytes 1 | tf_op jit(solution)/shard_map/examples/pallas_call | solution.py:165
  69.1 0.1 collective-permute-done.18
  69.2 0.8 collective-permute-start.19
  70.0 0.9 collective-permute-start.15
  70.9 2.5 %collective-permute-start.16 = (f32[8,8,128]{2,1,0:T(8,128)S(1)}, f32[8,8,128]{2,1,0:T(8,128)S(1)}, u32[]{:S(2)}, u32[]{:S(2)}) collective-permute-start(f32[8,8,128]{2,1,0:T(8,128)S(1)} %get-tuple-element.122), channel_id=1, source_target_pairs={{0,4},{1,5},{2,6},{3,7},{4,0},{5,1},{6,2},{7,3},{8,12},{9,13},{10,... | collective-permute-start | bytes 98312 | tf_op jit(solution)/shard_map/z_train/ppermute | solution.py:211
  73.4 0.9 %collective-permute-start.17 = (f32[8,8,128]{2,1,0:T(8,128)S(1)}, f32[8,8,128]{2,1,0:T(8,128)S(1)}, u32[]{:S(2)}, u32[]{:S(2)}) collective-permute-start(f32[8,8,128]{2,1,0:T(8,128)S(1)} %get-tuple-element.123), channel_id=1, source_target_pairs={{0,6},{1,7},{2,4},{3,5},{4,2},{5,3},{6,0},{7,1},{8,14},{9,15},{10,... | collective-permute-start | bytes 98312 | tf_op jit(solution)/shard_map/z_train/ppermute | solution.py:211
  74.4 1.3 %collective-permute-done.16.refs_2_ = f32[8,8,128]{2,1,0:T(8,128)S(1)} collective-permute-done((f32[8,8,128]{2,1,0:T(8,128)S(1)}, f32[8,8,128]{2,1,0:T(8,128)S(1)}, u32[]{:S(2)}, u32[]{:S(2)}) %collective-permute-start.16) | collective-permute-done | bytes 32800 | tf_op jit(solution)/shard_map/z_train/ppermute | solution.py:211
  75.7 3.4 %collective-permute-done.17.refs_3_ = f32[8,8,128]{2,1,0:T(8,128)S(1)} collective-permute-done((f32[8,8,128]{2,1,0:T(8,128)S(1)}, f32[8,8,128]{2,1,0:T(8,128)S(1)}, u32[]{:S(2)}, u32[]{:S(2)}) %collective-permute-start.17) | collective-permute-done | bytes 32800 | tf_op jit(solution)/shard_map/z_train/ppermute | solution.py:211
  79.1 0.0 collective-permute-done.19.refs_5_
  79.1 0.9 partial_scores.1
  80.0 0.7 collective-permute-start.20
  80.7 4.2 %collective-permute-done.20 = f32[64,128]{1,0:T(8,128)S(1)} collective-permute-done((f32[64,128]{1,0:T(8,128)S(1)}, f32[64,128]{1,0:T(8,128)S(1)}, u32[]{:S(2)}, u32[]{:S(2)}) %collective-permute-start.20) | collective-permute-done | bytes 32800 | tf_op jit(solution)/shard_map/scores/ppermute | solution.py:211
  84.9 3.9 %collective-permute-done.21 = f32[64,128]{1,0:T(8,128)S(1)} collective-permute-done((f32[64,128]{1,0:T(8,128)S(1)}, f32[64,128]{1,0:T(8,128)S(1)}, u32[]{:S(2)}, u32[]{:S(2)}) %collective-permute-start.21) | collective-permute-done | bytes 32800 | tf_op jit(solution)/shard_map/scores/ppermute | solution.py:211
  88.8 0.9 %collective-permute-start.22 = (f32[64,128]{1,0:T(8,128)S(1)}, f32[64,128]{1,0:T(8,128)S(1)}, u32[]{:S(2)}, u32[]{:S(2)}) collective-permute-start(f32[64,128]{1,0:T(8,128)S(1)} %add.96), channel_id=1, source_target_pairs={{0,1},{1,0},{2,3},{3,2},{4,5},{5,4},{6,7},{7,6},{8,9},{9,8},{10,11... | collective-permute-start | bytes 98312 | tf_op jit(solution)/shard_map/scores/ppermute | solution.py:211
  89.8 3.0 %collective-permute-done.22 = f32[64,128]{1,0:T(8,128)S(1)} collective-permute-done((f32[64,128]{1,0:T(8,128)S(1)}, f32[64,128]{1,0:T(8,128)S(1)}, u32[]{:S(2)}, u32[]{:S(2)}) %collective-permute-start.22) | collective-permute-done | bytes 32800 | tf_op jit(solution)/shard_map/scores/ppermute | solution.py:211
  92.7 0.6 add.97
  (32 shorter events, 0.4 us)
Async XLA Ops:
  3.1 21.0 %collective-permute-start = (f32[4,64,512]{2,1,0:T(8,128)S(1)}, f32[4,64,512]{2,1,0:T(8,128)S(1)}, u32[]{:S(2)}, u32[]{:S(2)}) collective-permute-start(f32[4,64,512]{2,1,0:T(8,128)S(1)} %first_query_out.1), channel_id=1, source_target_pairs={{0,2},{1,3},{2,0},{3,1},{4,6},{5,7},{6,4},{7,5},{8,10},{9,11},{10,... | collective-permute-start | bytes 1572872 | tf_op jit(solution)/shard_map/z1_qo/ppermute | solution.py:211
  14.1 24.5 %collective-permute-start.1 = (f32[4,64,512]{2,1,0:T(8,128)S(1)}, f32[4,64,512]{2,1,0:T(8,128)S(1)}, u32[]{:S(2)}, u32[]{:S(2)}) collective-permute-start(f32[4,64,512]{2,1,0:T(8,128)S(1)} %get-tuple-element.75), channel_id=1, source_target_pairs={{0,2},{1,3},{2,0},{3,1},{4,6},{5,7},{6,4},{7,5},{8,10},{9,11},{10,... | collective-permute-start | bytes 1572872 | tf_op jit(solution)/shard_map/z1_to/ppermute | solution.py:211
  14.2 20.0 %collective-permute-start.3 = (f32[4,64,512]{2,1,0:T(8,128)S(1)}, f32[4,64,512]{2,1,0:T(8,128)S(1)}, u32[]{:S(2)}, u32[]{:S(2)}) collective-permute-start(f32[4,64,512]{2,1,0:T(8,128)S(1)} %get-tuple-element.68), channel_id=1, source_target_pairs={{0,1},{1,0},{2,3},{3,2},{4,5},{5,4},{6,7},{7,6},{8,9},{9,8},{10,11... | collective-permute-start | bytes 1572872 | tf_op jit(solution)/shard_map/x_qi/ppermute | solution.py:211
  24.2 11.7 %collective-permute-start.2 = (f32[2,64,512]{2,1,0:T(8,128)S(1)}, f32[2,64,512]{2,1,0:T(8,128)S(1)}, u32[]{:S(2)}, u32[]{:S(2)}) collective-permute-start(f32[2,64,512]{2,1,0:T(8,128)S(1)} %slice_add_fusion.1), channel_id=1, source_target_pairs={{0,1},{1,0},{2,3},{3,2},{4,5},{5,4},{6,7},{7,6},{8,9},{9,8},{10,11... | collective-permute-start | bytes 786440 | tf_op jit(solution)/shard_map/x_qo/ppermute | solution.py:211
  24.4 21.6 %collective-permute-start.6 = (f32[4,64,512]{2,1,0:T(8,128)S(1)}, f32[4,64,512]{2,1,0:T(8,128)S(1)}, u32[]{:S(2)}, u32[]{:S(2)}) collective-permute-start(f32[4,64,512]{2,1,0:T(8,128)S(1)} %get-tuple-element.72), channel_id=1, source_target_pairs={{0,1},{1,0},{2,3},{3,2},{4,5},{5,4},{6,7},{7,6},{8,9},{9,8},{10,11... | collective-permute-start | bytes 1572872 | tf_op jit(solution)/shard_map/x_ti/ppermute | solution.py:211
  34.2 9.5 %collective-permute-start.5 = (f32[2,64,512]{2,1,0:T(8,128)S(1)}, f32[2,64,512]{2,1,0:T(8,128)S(1)}, u32[]{:S(2)}, u32[]{:S(2)}) collective-permute-start(f32[2,64,512]{2,1,0:T(8,128)S(1)} %slice_add_fusion), channel_id=1, source_target_pairs={{0,2},{1,3},{2,0},{3,1},{4,6},{5,7},{6,4},{7,5},{8,10},{9,11},{10,... | collective-permute-start | bytes 786440 | tf_op jit(solution)/shard_map/z1_qi/ppermute | solution.py:211
  36.0 16.3 %collective-permute-start.7 = (f32[1,64,512]{2,1,0:T(8,128)S(1)}, f32[1,64,512]{2,1,0:T(8,128)S(1)}, u32[]{:S(2)}, u32[]{:S(2)}) collective-permute-start(f32[1,64,512]{2,1,0:T(8,128)S(1)} %get-tuple-element.130), channel_id=1, source_target_pairs={{0,4},{1,5},{2,6},{3,7},{4,0},{5,1},{6,2},{7,3},{8,12},{9,13},{10,... | collective-permute-start | bytes 393224 | tf_op jit(solution)/shard_map/z2_qo/ppermute | solution.py:211
  38.7 13.6 %collective-permute-start.4 = (f32[2,64,512]{2,1,0:T(8,128)S(1)}, f32[2,64,512]{2,1,0:T(8,128)S(1)}, u32[]{:S(2)}, u32[]{:S(2)}) collective-permute-start(f32[2,64,512]{2,1,0:T(8,128)S(1)} %slice_add_fusion.3), channel_id=1, source_target_pairs={{0,1},{1,0},{2,3},{3,2},{4,5},{5,4},{6,7},{7,6},{8,9},{9,8},{10,11... | collective-permute-start | bytes 786440 | tf_op jit(solution)/shard_map/x_to/ppermute | solution.py:211
  39.4 15.6 %copy-start = (s32[4096]{0:T(1024)S(1)}, s32[4096]{0:T(1024)}, u32[]{:S(2)}) copy-start(s32[4096]{0:T(1024)} %param.15) | copy-start | bytes 49156
  39.5 28.4 %copy-start.1 = (s32[4096]{0:T(1024)S(1)}, s32[4096]{0:T(1024)}, u32[]{:S(2)}) copy-start(s32[4096]{0:T(1024)} %param.14) | copy-start | bytes 49156
  43.8 11.2 %collective-permute-start.9 = (f32[1,64,512]{2,1,0:T(8,128)S(1)}, f32[1,64,512]{2,1,0:T(8,128)S(1)}, u32[]{:S(2)}, u32[]{:S(2)}) collective-permute-start(f32[1,64,512]{2,1,0:T(8,128)S(1)} %fusion), channel_id=1, source_target_pairs={{0,4},{1,5},{2,6},{3,7},{4,0},{5,1},{6,2},{7,3},{8,12},{9,13},{10,... | collective-permute-start | bytes 393224 | tf_op jit(solution)/shard_map/z2_qi/ppermute | solution.py:211
  46.0 8.9 %collective-permute-start.8 = (f32[2,64,512]{2,1,0:T(8,128)S(1)}, f32[2,64,512]{2,1,0:T(8,128)S(1)}, u32[]{:S(2)}, u32[]{:S(2)}) collective-permute-start(f32[2,64,512]{2,1,0:T(8,128)S(1)} %slice_add_fusion.2), channel_id=1, source_target_pairs={{0,2},{1,3},{2,0},{3,1},{4,6},{5,7},{6,4},{7,5},{8,10},{9,11},{10,... | collective-permute-start | bytes 786440 | tf_op jit(solution)/shard_map/z1_ti/ppermute | solution.py:211
  52.3 11.0 %collective-permute-start.11 = (f32[1,64,512]{2,1,0:T(8,128)S(1)}, f32[1,64,512]{2,1,0:T(8,128)S(1)}, u32[]{:S(2)}, u32[]{:S(2)}) collective-permute-start(f32[1,64,512]{2,1,0:T(8,128)S(1)} %slice_add_fusion.8), channel_id=1, source_target_pairs={{0,4},{1,5},{2,6},{3,7},{4,0},{5,1},{6,2},{7,3},{8,12},{9,13},{10,... | collective-permute-start | bytes 393224 | tf_op jit(solution)/shard_map/z2_to/ppermute | solution.py:211
  56.2 11.5 %collective-permute-start.10 = (f32[1,64,512]{2,1,0:T(8,128)S(1)}, f32[1,64,512]{2,1,0:T(8,128)S(1)}, u32[]{:S(2)}, u32[]{:S(2)}) collective-permute-start(f32[1,64,512]{2,1,0:T(8,128)S(1)} %slice_add_fusion.6), channel_id=1, source_target_pairs={{0,4},{1,5},{2,6},{3,7},{4,0},{5,1},{6,2},{7,3},{8,12},{9,13},{10,... | collective-permute-start | bytes 393224 | tf_op jit(solution)/shard_map/z2_ti/ppermute | solution.py:211
  58.8 4.6 %collective-permute-start.12 = (f32[8,8,128]{2,1,0:T(8,128)S(1)}, f32[8,8,128]{2,1,0:T(8,128)S(1)}, u32[]{:S(2)}, u32[]{:S(2)}) collective-permute-start(f32[8,8,128]{2,1,0:T(8,128)S(1)} %get-tuple-element.111), channel_id=1, source_target_pairs={{0,2},{1,3},{2,0},{3,1},{4,6},{5,7},{6,4},{7,5},{8,10},{9,11},{10,... | collective-permute-start | bytes 98312 | tf_op jit(solution)/shard_map/z_query/ppermute | solution.py:211
  61.0 6.8 %collective-permute-start.13 = (f32[8,8,128]{2,1,0:T(8,128)S(1)}, f32[8,8,128]{2,1,0:T(8,128)S(1)}, u32[]{:S(2)}, u32[]{:S(2)}) collective-permute-start(f32[8,8,128]{2,1,0:T(8,128)S(1)} %get-tuple-element.112), channel_id=1, source_target_pairs={{0,4},{1,5},{2,6},{3,7},{4,0},{5,1},{6,2},{7,3},{8,12},{9,13},{10,... | collective-permute-start | bytes 98312 | tf_op jit(solution)/shard_map/z_query/ppermute | solution.py:211
  61.7 6.1 %collective-permute-start.14 = (f32[8,8,128]{2,1,0:T(8,128)S(1)}, f32[8,8,128]{2,1,0:T(8,128)S(1)}, u32[]{:S(2)}, u32[]{:S(2)}) collective-permute-start(f32[8,8,128]{2,1,0:T(8,128)S(1)} %get-tuple-element.113), channel_id=1, source_target_pairs={{0,6},{1,7},{2,4},{3,5},{4,2},{5,3},{6,0},{7,1},{8,14},{9,15},{10,... | collective-permute-start | bytes 98312 | tf_op jit(solution)/shard_map/z_query/ppermute | solution.py:211
  67.8 1.4 %collective-permute-start.18 = (f32[4,8,8,128]{3,2,1,0:T(8,128)S(1)}, f32[4,8,8,128]{3,2,1,0:T(8,128)S(1)}, u32[]{:S(2)}, u32[]{:S(2)}) collective-permute-start(f32[4,8,8,128]{3,2,1,0:T(8,128)S(1)} %pad_maximum_fusion), channel_id=1, source_target_pairs={{0,8},{8,0},{1,9},{9,1},{2,10},{10,2},{3,11},{11,3},{4,12},{12,4},... | collective-permute-start | bytes 393224 | tf_op jit(solution)/shard_map/dp_query/ppermute | solution.py:216
  69.2 9.9 %collective-permute-start.19 = (f32[8,8,8,128]{3,2,1,0:T(8,128)S(1)}, f32[8,8,8,128]{3,2,1,0:T(8,128)S(1)}, u32[]{:S(2)}, u32[]{:S(2)}) collective-permute-start(f32[8,8,8,128]{3,2,1,0:T(8,128)S(1)} %constant_dynamic-update-slice_fusion.refs_4_), channel_id=1, source_target_pairs={{0,1},{1,0},{2,3},{3,2},{4,5},{5,4},{6,7},{7,6},{8,9},{9,8},{10,11... | collective-permute-start | bytes 786440 | tf_op jit(solution)/shard_map/x_query/ppermute | solution.py:211
  70.0 4.4 %collective-permute-start.15 = (f32[8,8,128]{2,1,0:T(8,128)S(1)}, f32[8,8,128]{2,1,0:T(8,128)S(1)}, u32[]{:S(2)}, u32[]{:S(2)}) collective-permute-start(f32[8,8,128]{2,1,0:T(8,128)S(1)} %get-tuple-element.121), channel_id=1, source_target_pairs={{0,2},{1,3},{2,0},{3,1},{4,6},{5,7},{6,4},{7,5},{8,10},{9,11},{10,... | collective-permute-start | bytes 98312 | tf_op jit(solution)/shard_map/z_train/ppermute | solution.py:211
  70.9 4.8 %collective-permute-start.16 = (f32[8,8,128]{2,1,0:T(8,128)S(1)}, f32[8,8,128]{2,1,0:T(8,128)S(1)}, u32[]{:S(2)}, u32[]{:S(2)}) collective-permute-start(f32[8,8,128]{2,1,0:T(8,128)S(1)} %get-tuple-element.122), channel_id=1, source_target_pairs={{0,4},{1,5},{2,6},{3,7},{4,0},{5,1},{6,2},{7,3},{8,12},{9,13},{10,... | collective-permute-start | bytes 98312 | tf_op jit(solution)/shard_map/z_train/ppermute | solution.py:211
  73.4 5.7 %collective-permute-start.17 = (f32[8,8,128]{2,1,0:T(8,128)S(1)}, f32[8,8,128]{2,1,0:T(8,128)S(1)}, u32[]{:S(2)}, u32[]{:S(2)}) collective-permute-start(f32[8,8,128]{2,1,0:T(8,128)S(1)} %get-tuple-element.123), channel_id=1, source_target_pairs={{0,6},{1,7},{2,4},{3,5},{4,2},{5,3},{6,0},{7,1},{8,14},{9,15},{10,... | collective-permute-start | bytes 98312 | tf_op jit(solution)/shard_map/z_train/ppermute | solution.py:211
  80.0 4.9 %collective-permute-start.20 = (f32[64,128]{1,0:T(8,128)S(1)}, f32[64,128]{1,0:T(8,128)S(1)}, u32[]{:S(2)}, u32[]{:S(2)}) collective-permute-start(f32[64,128]{1,0:T(8,128)S(1)} %partial_scores.1), channel_id=1, source_target_pairs={{0,4},{1,5},{2,6},{3,7},{4,0},{5,1},{6,2},{7,3},{8,12},{9,13},{10,... | collective-permute-start | bytes 98312 | tf_op jit(solution)/shard_map/scores/ppermute | solution.py:211
  84.9 3.9 %collective-permute-start.21 = (f32[64,128]{1,0:T(8,128)S(1)}, f32[64,128]{1,0:T(8,128)S(1)}, u32[]{:S(2)}, u32[]{:S(2)}) collective-permute-start(f32[64,128]{1,0:T(8,128)S(1)} %add.95), channel_id=1, source_target_pairs={{0,2},{1,3},{2,0},{3,1},{4,6},{5,7},{6,4},{7,5},{8,10},{9,11},{10,... | collective-permute-start | bytes 98312 | tf_op jit(solution)/shard_map/scores/ppermute | solution.py:211
  88.8 3.9 %collective-permute-start.22 = (f32[64,128]{1,0:T(8,128)S(1)}, f32[64,128]{1,0:T(8,128)S(1)}, u32[]{:S(2)}, u32[]{:S(2)}) collective-permute-start(f32[64,128]{1,0:T(8,128)S(1)} %add.96), channel_id=1, source_target_pairs={{0,1},{1,0},{2,3},{3,2},{4,5},{5,4},{6,7},{7,6},{8,9},{9,8},{10,11... | collective-permute-start | bytes 98312 | tf_op jit(solution)/shard_map/scores/ppermute | solution.py:211

commit v6 on v5

--- a/solution.py
+++ b/solution.py
@@ -12,9 +12,9 @@
 X, Z1, Z2 = 1, 2, 4
 X_FIRST = (0, Z2, Z1, Z1 | Z2, X, X | Z2, X | Z1, X | Z1 | Z2)
 Z_FIRST = (0, Z2, X, X | Z2, Z1, Z1 | Z2, Z1 | X, X | Z1 | Z2)
-AHEAD = 7 * 1024 * 1024
+AHEAD = 8 * 1024 * 1024
 LIGHT = 1
-VMEM = 26 * 1024 * 1024
+VMEM = 3 * 1024 * 1024
 
 
 def example_grads(proj_out, proj_in, slot_ids):
@@ -63,7 +63,13 @@
     count, made_count = len(sources), len(jobs)
     steps = [(n, i, source, mask) for n, (source, masks) in enumerate(jobs) for i, mask in enumerate(masks)]
 
-    ahead = AHEAD // max(data.shape[0] * BLK * 2 for _, data in sources) + 1
+    sizes = [sources[source][1].shape[0] * BLK * 2 for _, _, source, _ in steps]
+    started = []
+    for step in range(len(steps) + 1):
+        upto = started[-1] if started else 0
+        while upto < len(steps) and (upto <= step or sum(sizes[step : upto + 1]) <= AHEAD):
+            upto += 1
+        started.append(upto)
 
     def kernel(me_ref, *refs):
         bases, datas = refs[:count], refs[count : 2 * count]
@@ -73,8 +79,6 @@
         basis_sem, in_sem = refs[2 * count :]
         here = me_ref[0]
         firsts = [pltpu.make_async_copy(bases[n], held[n], basis_sem.at[n]) for n in range(count)]
-        for first in firsts:
-            first.start()
         used = [0] * count
         copies = []
         for step, (n, i, source, mask) in enumerate(steps):
@@ -84,15 +88,18 @@
             )
             copies.append((copy, used[source]))
             used[source] += 1
-            if step < ahead:
+            if step < started[0]:
                 copy.start()
+            if step == 0:
+                for first in firsts:
+                    first.start()
         for step, (n, i, source, mask) in enumerate(steps):
             copy, slot = copies[step]
             if slot == 0:
                 firsts[source].wait()
             copy.wait()
-            if step + ahead < len(steps):
-                copies[step + ahead][0].start()
+            for later in range(started[step], started[step + 1]):
+                copies[later][0].start()
             outs[n][i] = jnp.dot(
                 held[source][...], slots[source][slot], preferred_element_type=jnp.float32
             )
@@ -110,7 +117,7 @@
             pltpu.SemaphoreType.DMA((count,)),
             pltpu.SemaphoreType.DMA((len(steps),)),
         ],
-        compiler_params=pltpu.CompilerParams(vmem_limit_bytes=VMEM),
+        compiler_params=pltpu.CompilerParams(vmem_limit_bytes=sum(sizes) + VMEM),
         cost_estimate=pl.CostEstimate(
             flops=moved * RANK // LIGHT, bytes_accessed=moved // LIGHT, transcendentals=0
         ),
@@ -233,19 +240,19 @@
     (qo_send,) = project(me, [outs], [(0, Z_FIRST[4:])], "first_query_out")
     qo1 = swap(qo_send, Z1, "z1_qo")
     me = after(me, qo_send)
-    to_send, qi_send = project(
-        me, [train_outs, ins], [(0, Z_FIRST[4:]), (1, X_FIRST[4:])], "first_query_in"
+    qi_send, to_send = project(
+        me, [ins, train_outs], [(0, X_FIRST[4:]), (1, Z_FIRST[4:])], "first_query_in"
     )
     qi1 = swap(qi_send, X, "x_qi")
     to1 = swap(to_send, Z1, "z1_to")
     me = after(me, qi_send)
-    qo, ti_send = project(me, [outs, train_ins], [(0, Z_FIRST[:4]), (1, X_FIRST[4:])], "middle_a")
+    ti_send, qo = project(me, [train_ins, outs], [(0, X_FIRST[4:]), (1, Z_FIRST[:4])], "middle_a")
     qo_send = qo[2:] + qo1[2:]
     ti_send = after(ti_send, qo_send)
     qo2 = swap(qo_send, X, "x_qo")
     ti1 = swap(ti_send, X, "x_ti")
     me = after(me, qo_send, ti_send)
-    to, qi = project(me, [train_outs, ins], [(0, Z_FIRST[:4]), (1, X_FIRST[:4])], "middle_b")
+    qi, to = project(me, [ins, train_outs], [(0, X_FIRST[:4]), (1, Z_FIRST[:4])], "middle_b")
     qi_send = qi[2:] + qi1[2:]
     qi2 = swap(qi_send, Z1, "z1_qi")
     qo, qo1, qo2, _ = lax.optimization_barrier((qo, qo1, qo2, qi_send))

time: 93.5 us -> 92.9 us (level)
  starting transfers between devices: 32.7 us -> 34.5 us
  waiting for transfers between devices: 21 us -> 19.4 us
    ppermute x22, starting transfers between devices: 32.6 us -> 34.4 us  [swap(): return lax.ppermute(value, 'tensor', [(i, i ^ mask) for i in range(8)])]
    ppermute x22, waiting for transfers between devices: 20.9 us -> 19.2 us  [swap(): return lax.ppermute(value, 'tensor', [(i, i ^ mask) for i in range(8)])]
  transfers between devices with their start and end apart: 23 -> 23, of which waited for: 10 -> 9; matrix products, arithmetic and copies ran while one was open for 1% -> 1% of each run, Pallas kernels for 37% -> 36%
where the time goes in v6:
time: 92.9 us; the launch traced here: 92.7 us
  Pallas kernels  37.5 us (40%)
  starting transfers between devices  34.5 us (37%)
  waiting for transfers between devices  19.4 us (21%)
  other arithmetic  1.13 us (1%)
    ppermute x22, starting transfers between devices, swap(): return lax.ppermute(value, 'tensor', [(i, i ^ mask) for i in range(8)])  34.4 us
    pallas_call x6, Pallas kernels, project(): pl.pallas_call(kernel, out_shape=[pltpu.VMEM((len(masks), RANK, BLK), jnp...  34.3 us
    ppermute x22, waiting for transfers between devices, swap(): return lax.ppermute(value, 'tensor', [(i, i ^ mask) for i in range(8)])  19.2 us
    pallas_call x2, Pallas kernels, examples(): pl.pallas_call(kernel, out_shape=[pltpu.VMEM((HALF // 4, SEGS, 2 * RANK),...  2.29 us
  transfers between devices with their start and end apart: 23, of which 9 were waited for; matrix products, arithmetic and copies ran while one was open for 1% of the time, Pallas kernels for 36%

profile of v6, /device:TPU:0, one launch (start us, length us, event | category | flops | bytes accessed | tf_op | source)
XLA Modules:
  0.0 92.7 jit_solution(9135506646837280565)
XLA Ops:
  0.0 3.1 %first_query_out.1 = f32[4,64,512]{2,1,0:T(8,128)S(1)} custom-call(s32[1]{0:T(128)} %bitcast.1.me_ref, bf16[64,1024]{1,0:T(8,128)(2,1)} %refs_1_.9, bf16[1024,4096]{1,0:T(8,128)(2,1)} %refs_3_.4), custom_call_target="tpu_custom_call" | custom-call | flops 268435456 | bytes 4194304 | tf_op jit(solution)/shard_map/first_query_out/pallas_call | solution.py:109
  3.1 3.1 %collective-permute-start = (f32[4,64,512]{2,1,0:T(8,128)S(1)}, f32[4,64,512]{2,1,0:T(8,128)S(1)}, u32[]{:S(2)}, u32[]{:S(2)}) collective-permute-start(f32[4,64,512]{2,1,0:T(8,128)S(1)} %first_query_out.1), channel_id=1, source_target_pairs={{0,2},{1,3},{2,0},{3,1},{4,6},{5,7},{6,4},{7,5},{8,10},{9,11},{10,... | collective-permute-start | bytes 1572872 | tf_op jit(solution)/shard_map/z1_qo/ppermute | solution.py:218
  6.2 7.7 %first_query_in.1 = (f32[4,64,512]{2,1,0:T(8,128)S(1)}, f32[4,64,512]{2,1,0:T(8,128)S(1)}) custom-call(s32[1]{0:T(128)} %bitcast.1.me_ref, bf16[64,3584]{1,0:T(8,128)(2,1)} %refs_0_.11, bf16[64,1024]{1,0:T(8,128)(2,1)} %refs_1_.9, bf16[3584,4096]{1,0:T(8,128)(2,1)} %refs_2_.5, bf16[1024,4096]{1,0:T(8,128)(2,1)} %refs_3_.5), custom_call_target="tpu_custom_call" | custom-call | flops 1207959552 | bytes 18874368 | tf_op jit(solution)/shard_map/first_query_in/pallas_call | solution.py:109
  13.9 0.1 collective-permute-start.1
  14.0 1.9 %collective-permute-start.3 = (f32[4,64,512]{2,1,0:T(8,128)S(1)}, f32[4,64,512]{2,1,0:T(8,128)S(1)}, u32[]{:S(2)}, u32[]{:S(2)}) collective-permute-start(f32[4,64,512]{2,1,0:T(8,128)S(1)} %get-tuple-element.68), channel_id=1, source_target_pairs={{0,1},{1,0},{2,3},{3,2},{4,5},{5,4},{6,7},{7,6},{8,9},{9,8},{10,11... | collective-permute-start | bytes 1572872 | tf_op jit(solution)/shard_map/x_qi/ppermute | solution.py:218
  15.9 0.1 pad_add_fusion.place_ref
  16.0 7.7 %middle_a.1 = (f32[4,64,512]{2,1,0:T(8,128)S(1)}, f32[4,64,512]{2,1,0:T(8,128)S(1)}) custom-call(s32[1]{0:T(128)} %bitcast.1.me_ref, bf16[64,3584]{1,0:T(8,128)(2,1)} %refs_0_.11, bf16[64,1024]{1,0:T(8,128)(2,1)} %refs_1_.9, bf16[3584,4096]{1,0:T(8,128)(2,1)} %refs_1_.11, bf16[1024,4096]{1,0:T(8,128)(2,1)} %refs_3_.4), custom_call_target="tpu_custom_call" | custom-call | flops 1207959552 | bytes 18874368 | tf_op jit(solution)/shard_map/middle_a/pallas_call | solution.py:109
  23.7 0.0 collective-permute-done
  23.7 0.2 collective-permute-start.2
  23.9 1.9 %collective-permute-start.6 = (f32[4,64,512]{2,1,0:T(8,128)S(1)}, f32[4,64,512]{2,1,0:T(8,128)S(1)}, u32[]{:S(2)}, u32[]{:S(2)}) collective-permute-start(f32[4,64,512]{2,1,0:T(8,128)S(1)} %get-tuple-element.72), channel_id=1, source_target_pairs={{0,1},{1,0},{2,3},{3,2},{4,5},{5,4},{6,7},{7,6},{8,9},{9,8},{10,11... | collective-permute-start | bytes 1572872 | tf_op jit(solution)/shard_map/x_ti/ppermute | solution.py:218
  25.8 7.7 %middle_b.1 = (f32[4,64,512]{2,1,0:T(8,128)S(1)}, f32[4,64,512]{2,1,0:T(8,128)S(1)}) custom-call(s32[1]{0:T(128)} %bitcast.1.me_ref, bf16[64,3584]{1,0:T(8,128)(2,1)} %refs_0_.11, bf16[64,1024]{1,0:T(8,128)(2,1)} %refs_1_.9, bf16[3584,4096]{1,0:T(8,128)(2,1)} %refs_2_.5, bf16[1024,4096]{1,0:T(8,128)(2,1)} %refs_3_.5), custom_call_target="tpu_custom_call" | custom-call | flops 1207959552 | bytes 18874368 | tf_op jit(solution)/shard_map/middle_b/pallas_call | solution.py:109
  33.5 0.0 collective-permute-done.3
  33.5 1.6 %collective-permute-start.5 = (f32[2,64,512]{2,1,0:T(8,128)S(1)}, f32[2,64,512]{2,1,0:T(8,128)S(1)}, u32[]{:S(2)}, u32[]{:S(2)}) collective-permute-start(f32[2,64,512]{2,1,0:T(8,128)S(1)} %slice_add_fusion), channel_id=1, source_target_pairs={{0,2},{1,3},{2,0},{3,1},{4,6},{5,7},{6,4},{7,5},{8,10},{9,11},{10,... | collective-permute-start | bytes 786440 | tf_op jit(solution)/shard_map/z1_qi/ppermute | solution.py:218
  35.2 0.0 collective-permute-done.2
  35.2 0.1 slice_add_fusion.10
  35.3 2.7 %collective-permute-start.7 = (f32[1,64,512]{2,1,0:T(8,128)S(1)}, f32[1,64,512]{2,1,0:T(8,128)S(1)}, u32[]{:S(2)}, u32[]{:S(2)}) collective-permute-start(f32[1,64,512]{2,1,0:T(8,128)S(1)} %get-tuple-element.130), channel_id=1, source_target_pairs={{0,4},{1,5},{2,6},{3,7},{4,0},{5,1},{6,2},{7,3},{8,12},{9,13},{10,... | collective-permute-start | bytes 393224 | tf_op jit(solution)/shard_map/z2_qo/ppermute | solution.py:218
  37.9 0.0 collective-permute-done.1
  38.0 1.2 %collective-permute-start.4 = (f32[2,64,512]{2,1,0:T(8,128)S(1)}, f32[2,64,512]{2,1,0:T(8,128)S(1)}, u32[]{:S(2)}, u32[]{:S(2)}) collective-permute-start(f32[2,64,512]{2,1,0:T(8,128)S(1)} %slice_add_fusion.3), channel_id=1, source_target_pairs={{0,1},{1,0},{2,3},{3,2},{4,5},{5,4},{6,7},{7,6},{8,9},{9,8},{10,11... | collective-permute-start | bytes 786440 | tf_op jit(solution)/shard_map/x_to/ppermute | solution.py:218
  39.2 4.1 %last_train_in_a.1 = f32[2,64,512]{2,1,0:T(8,128)S(1)} custom-call(s32[1]{0:T(128)} %bitcast.1.me_ref, bf16[64,3584]{1,0:T(8,128)(2,1)} %refs_0_.11, bf16[3584,4096]{1,0:T(8,128)(2,1)} %refs_1_.11), custom_call_target="tpu_custom_call" | custom-call | flops 469762048 | bytes 7340032 | tf_op jit(solution)/shard_map/last_train_in_a/pallas_call | solution.py:109
  43.3 0.0 collective-permute-done.5
  43.4 1.5 %collective-permute-start.9 = (f32[1,64,512]{2,1,0:T(8,128)S(1)}, f32[1,64,512]{2,1,0:T(8,128)S(1)}, u32[]{:S(2)}, u32[]{:S(2)}) collective-permute-start(f32[1,64,512]{2,1,0:T(8,128)S(1)} %fusion), channel_id=1, source_target_pairs={{0,4},{1,5},{2,6},{3,7},{4,0},{5,1},{6,2},{7,3},{8,12},{9,13},{10,... | collective-permute-start | bytes 393224 | tf_op jit(solution)/shard_map/z2_qi/ppermute | solution.py:218
  44.8 0.9 collective-permute-done.6
  45.8 2.0 %collective-permute-start.8 = (f32[2,64,512]{2,1,0:T(8,128)S(1)}, f32[2,64,512]{2,1,0:T(8,128)S(1)}, u32[]{:S(2)}, u32[]{:S(2)}) collective-permute-start(f32[2,64,512]{2,1,0:T(8,128)S(1)} %slice_add_fusion.2), channel_id=1, source_target_pairs={{0,2},{1,3},{2,0},{3,1},{4,6},{5,7},{6,4},{7,5},{8,10},{9,11},{10,... | collective-permute-start | bytes 786440 | tf_op jit(solution)/shard_map/z1_ti/ppermute | solution.py:218
  47.8 4.1 %last_train_in_b.1 = f32[2,64,512]{2,1,0:T(8,128)S(1)} custom-call(s32[1]{0:T(128)} %bitcast.1.me_ref, bf16[64,3584]{1,0:T(8,128)(2,1)} %refs_0_.11, bf16[3584,4096]{1,0:T(8,128)(2,1)} %refs_1_.11), custom_call_target="tpu_custom_call" | custom-call | flops 469762048 | bytes 7340032 | tf_op jit(solution)/shard_map/last_train_in_b/pallas_call | solution.py:109
  52.0 2.7 %collective-permute-start.11 = (f32[1,64,512]{2,1,0:T(8,128)S(1)}, f32[1,64,512]{2,1,0:T(8,128)S(1)}, u32[]{:S(2)}, u32[]{:S(2)}) collective-permute-start(f32[1,64,512]{2,1,0:T(8,128)S(1)} %slice_add_fusion.8), channel_id=1, source_target_pairs={{0,4},{1,5},{2,6},{3,7},{4,0},{5,1},{6,2},{7,3},{8,12},{9,13},{10,... | collective-permute-start | bytes 393224 | tf_op jit(solution)/shard_map/z2_to/ppermute | solution.py:218
  54.7 1.1 %examples.2 = (f32[8,8,128]{2,1,0:T(8,128)S(1)}, f32[8,8,128]{2,1,0:T(8,128)S(1)}, f32[8,8,128]{2,1,0:T(8,128)S(1)}, f32[8,8,128]{2,1,0:T(8,128)S(1)}) custom-call(s32[4]{0:T(128)S(1)} %pad_add_fusion.place_ref, f32[1,64,512]{2,1,0:T(8,128)S(1)} %get-tuple-element.129.refs_0_, f32[1,64,512]{2,1,0:T(8,128)S(1)} %collective-permute-done.7.refs_1_, ...), custom_call_target="tpu_custom_call" | custom-call | flops 1 | bytes 1 | tf_op jit(solution)/shard_map/examples/pallas_call | solution.py:172
  55.9 2.4 %collective-permute-start.10 = (f32[1,64,512]{2,1,0:T(8,128)S(1)}, f32[1,64,512]{2,1,0:T(8,128)S(1)}, u32[]{:S(2)}, u32[]{:S(2)}) collective-permute-start(f32[1,64,512]{2,1,0:T(8,128)S(1)} %slice_add_fusion.6), channel_id=1, source_target_pairs={{0,4},{1,5},{2,6},{3,7},{4,0},{5,1},{6,2},{7,3},{8,12},{9,13},{10,... | collective-permute-start | bytes 393224 | tf_op jit(solution)/shard_map/z2_ti/ppermute | solution.py:218
  58.3 2.4 %collective-permute-start.12 = (f32[8,8,128]{2,1,0:T(8,128)S(1)}, f32[8,8,128]{2,1,0:T(8,128)S(1)}, u32[]{:S(2)}, u32[]{:S(2)}) collective-permute-start(f32[8,8,128]{2,1,0:T(8,128)S(1)} %get-tuple-element.111), channel_id=1, source_target_pairs={{0,2},{1,3},{2,0},{3,1},{4,6},{5,7},{6,4},{7,5},{8,10},{9,11},{10,... | collective-permute-start | bytes 98312 | tf_op jit(solution)/shard_map/z_query/ppermute | solution.py:218
  60.7 0.4 collective-permute-start.13
  61.1 2.0 %collective-permute-start.14 = (f32[8,8,128]{2,1,0:T(8,128)S(1)}, f32[8,8,128]{2,1,0:T(8,128)S(1)}, u32[]{:S(2)}, u32[]{:S(2)}) collective-permute-start(f32[8,8,128]{2,1,0:T(8,128)S(1)} %get-tuple-element.113), channel_id=1, source_target_pairs={{0,6},{1,7},{2,4},{3,5},{4,2},{5,3},{6,0},{7,1},{8,14},{9,15},{10,... | collective-permute-start | bytes 98312 | tf_op jit(solution)/shard_map/z_query/ppermute | solution.py:218
  63.1 0.8 collective-permute-done.11.refs_1_
  63.9 3.2 %collective-permute-done.13 = f32[8,8,128]{2,1,0:T(8,128)S(1)} collective-permute-done((f32[8,8,128]{2,1,0:T(8,128)S(1)}, f32[8,8,128]{2,1,0:T(8,128)S(1)}, u32[]{:S(2)}, u32[]{:S(2)}) %collective-permute-start.13) | collective-permute-done | bytes 32800 | tf_op jit(solution)/shard_map/z_query/ppermute | solution.py:218
  67.2 0.1 collective-permute-start.18
  67.3 1.1 %examples.3 = (f32[8,8,128]{2,1,0:T(8,128)S(1)}, f32[8,8,128]{2,1,0:T(8,128)S(1)}, f32[8,8,128]{2,1,0:T(8,128)S(1)}, f32[8,8,128]{2,1,0:T(8,128)S(1)}) custom-call(s32[4]{0:T(128)S(1)} %pad_add_fusion.place_ref, f32[1,64,512]{2,1,0:T(8,128)S(1)} %slice_add_fusion.7.refs_0_, f32[1,64,512]{2,1,0:T(8,128)S(1)} %collective-permute-done.11.refs_1_, ...), custom_call_target="tpu_custom_call" | custom-call | flops 1 | bytes 1 | tf_op jit(solution)/shard_map/examples/pallas_call | solution.py:172
  68.4 0.1 collective-permute-done.18
  68.6 1.7 %collective-permute-start.19 = (f32[8,8,8,128]{3,2,1,0:T(8,128)S(1)}, f32[8,8,8,128]{3,2,1,0:T(8,128)S(1)}, u32[]{:S(2)}, u32[]{:S(2)}) collective-permute-start(f32[8,8,8,128]{3,2,1,0:T(8,128)S(1)} %constant_dynamic-update-slice_fusion.refs_4_), channel_id=1, source_target_pairs={{0,1},{1,0},{2,3},{3,2},{4,5},{5,4},{6,7},{7,6},{8,9},{9,8},{10,11... | collective-permute-start | bytes 786440 | tf_op jit(solution)/shard_map/x_query/ppermute | solution.py:218
  70.3 0.9 collective-permute-start.15
  71.2 1.6 %collective-permute-start.16 = (f32[8,8,128]{2,1,0:T(8,128)S(1)}, f32[8,8,128]{2,1,0:T(8,128)S(1)}, u32[]{:S(2)}, u32[]{:S(2)}) collective-permute-start(f32[8,8,128]{2,1,0:T(8,128)S(1)} %get-tuple-element.122), channel_id=1, source_target_pairs={{0,4},{1,5},{2,6},{3,7},{4,0},{5,1},{6,2},{7,3},{8,12},{9,13},{10,... | collective-permute-start | bytes 98312 | tf_op jit(solution)/shard_map/z_train/ppermute | solution.py:218
  72.8 1.9 %collective-permute-start.17 = (f32[8,8,128]{2,1,0:T(8,128)S(1)}, f32[8,8,128]{2,1,0:T(8,128)S(1)}, u32[]{:S(2)}, u32[]{:S(2)}) collective-permute-start(f32[8,8,128]{2,1,0:T(8,128)S(1)} %get-tuple-element.123), channel_id=1, source_target_pairs={{0,6},{1,7},{2,4},{3,5},{4,2},{5,3},{6,0},{7,1},{8,14},{9,15},{10,... | collective-permute-start | bytes 98312 | tf_op jit(solution)/shard_map/z_train/ppermute | solution.py:218
  74.7 1.4 %collective-permute-done.16.refs_2_ = f32[8,8,128]{2,1,0:T(8,128)S(1)} collective-permute-done((f32[8,8,128]{2,1,0:T(8,128)S(1)}, f32[8,8,128]{2,1,0:T(8,128)S(1)}, u32[]{:S(2)}, u32[]{:S(2)}) %collective-permute-start.16) | collective-permute-done | bytes 32800 | tf_op jit(solution)/shard_map/z_train/ppermute | solution.py:218
  76.1 2.4 %collective-permute-done.17.refs_3_ = f32[8,8,128]{2,1,0:T(8,128)S(1)} collective-permute-done((f32[8,8,128]{2,1,0:T(8,128)S(1)}, f32[8,8,128]{2,1,0:T(8,128)S(1)}, u32[]{:S(2)}, u32[]{:S(2)}) %collective-permute-start.17) | collective-permute-done | bytes 32800 | tf_op jit(solution)/shard_map/z_train/ppermute | solution.py:218
  78.5 0.9 partial_scores.1
  79.4 1.0 %collective-permute-start.20 = (f32[64,128]{1,0:T(8,128)S(1)}, f32[64,128]{1,0:T(8,128)S(1)}, u32[]{:S(2)}, u32[]{:S(2)}) collective-permute-start(f32[64,128]{1,0:T(8,128)S(1)} %partial_scores.1), channel_id=1, source_target_pairs={{0,4},{1,5},{2,6},{3,7},{4,0},{5,1},{6,2},{7,3},{8,12},{9,13},{10,... | collective-permute-start | bytes 98312 | tf_op jit(solution)/shard_map/scores/ppermute | solution.py:218
  80.4 3.9 %collective-permute-done.20 = f32[64,128]{1,0:T(8,128)S(1)} collective-permute-done((f32[64,128]{1,0:T(8,128)S(1)}, f32[64,128]{1,0:T(8,128)S(1)}, u32[]{:S(2)}, u32[]{:S(2)}) %collective-permute-start.20) | collective-permute-done | bytes 32800 | tf_op jit(solution)/shard_map/scores/ppermute | solution.py:218
  84.3 3.9 %collective-permute-done.21 = f32[64,128]{1,0:T(8,128)S(1)} collective-permute-done((f32[64,128]{1,0:T(8,128)S(1)}, f32[64,128]{1,0:T(8,128)S(1)}, u32[]{:S(2)}, u32[]{:S(2)}) %collective-permute-start.21) | collective-permute-done | bytes 32800 | tf_op jit(solution)/shard_map/scores/ppermute | solution.py:218
  88.2 1.2 %collective-permute-start.22 = (f32[64,128]{1,0:T(8,128)S(1)}, f32[64,128]{1,0:T(8,128)S(1)}, u32[]{:S(2)}, u32[]{:S(2)}) collective-permute-start(f32[64,128]{1,0:T(8,128)S(1)} %add.96), channel_id=1, source_target_pairs={{0,1},{1,0},{2,3},{3,2},{4,5},{5,4},{6,7},{7,6},{8,9},{9,8},{10,11... | collective-permute-start | bytes 98312 | tf_op jit(solution)/shard_map/scores/ppermute | solution.py:218
  89.4 2.7 %collective-permute-done.22 = f32[64,128]{1,0:T(8,128)S(1)} collective-permute-done((f32[64,128]{1,0:T(8,128)S(1)}, f32[64,128]{1,0:T(8,128)S(1)}, u32[]{:S(2)}, u32[]{:S(2)}) %collective-permute-start.22) | collective-permute-done | bytes 32800 | tf_op jit(solution)/shard_map/scores/ppermute | solution.py:218
  92.1 0.6 add.97
  (32 shorter events, 0.4 us)
Async XLA Ops:
  3.1 20.5 %collective-permute-start = (f32[4,64,512]{2,1,0:T(8,128)S(1)}, f32[4,64,512]{2,1,0:T(8,128)S(1)}, u32[]{:S(2)}, u32[]{:S(2)}) collective-permute-start(f32[4,64,512]{2,1,0:T(8,128)S(1)} %first_query_out.1), channel_id=1, source_target_pairs={{0,2},{1,3},{2,0},{3,1},{4,6},{5,7},{6,4},{7,5},{8,10},{9,11},{10,... | collective-permute-start | bytes 1572872 | tf_op jit(solution)/shard_map/z1_qo/ppermute | solution.py:218
  13.9 24.0 %collective-permute-start.1 = (f32[4,64,512]{2,1,0:T(8,128)S(1)}, f32[4,64,512]{2,1,0:T(8,128)S(1)}, u32[]{:S(2)}, u32[]{:S(2)}) collective-permute-start(f32[4,64,512]{2,1,0:T(8,128)S(1)} %get-tuple-element.75), channel_id=1, source_target_pairs={{0,2},{1,3},{2,0},{3,1},{4,6},{5,7},{6,4},{7,5},{8,10},{9,11},{10,... | collective-permute-start | bytes 1572872 | tf_op jit(solution)/shard_map/z1_to/ppermute | solution.py:218
  14.0 19.5 %collective-permute-start.3 = (f32[4,64,512]{2,1,0:T(8,128)S(1)}, f32[4,64,512]{2,1,0:T(8,128)S(1)}, u32[]{:S(2)}, u32[]{:S(2)}) collective-permute-start(f32[4,64,512]{2,1,0:T(8,128)S(1)} %get-tuple-element.68), channel_id=1, source_target_pairs={{0,1},{1,0},{2,3},{3,2},{4,5},{5,4},{6,7},{7,6},{8,9},{9,8},{10,11... | collective-permute-start | bytes 1572872 | tf_op jit(solution)/shard_map/x_qi/ppermute | solution.py:218
  23.7 11.5 %collective-permute-start.2 = (f32[2,64,512]{2,1,0:T(8,128)S(1)}, f32[2,64,512]{2,1,0:T(8,128)S(1)}, u32[]{:S(2)}, u32[]{:S(2)}) collective-permute-start(f32[2,64,512]{2,1,0:T(8,128)S(1)} %slice_add_fusion.1), channel_id=1, source_target_pairs={{0,1},{1,0},{2,3},{3,2},{4,5},{5,4},{6,7},{7,6},{8,9},{9,8},{10,11... | collective-permute-start | bytes 786440 | tf_op jit(solution)/shard_map/x_qo/ppermute | solution.py:218
  23.9 21.8 %collective-permute-start.6 = (f32[4,64,512]{2,1,0:T(8,128)S(1)}, f32[4,64,512]{2,1,0:T(8,128)S(1)}, u32[]{:S(2)}, u32[]{:S(2)}) collective-permute-start(f32[4,64,512]{2,1,0:T(8,128)S(1)} %get-tuple-element.72), channel_id=1, source_target_pairs={{0,1},{1,0},{2,3},{3,2},{4,5},{5,4},{6,7},{7,6},{8,9},{9,8},{10,11... | collective-permute-start | bytes 1572872 | tf_op jit(solution)/shard_map/x_ti/ppermute | solution.py:218
  33.5 9.8 %collective-permute-start.5 = (f32[2,64,512]{2,1,0:T(8,128)S(1)}, f32[2,64,512]{2,1,0:T(8,128)S(1)}, u32[]{:S(2)}, u32[]{:S(2)}) collective-permute-start(f32[2,64,512]{2,1,0:T(8,128)S(1)} %slice_add_fusion), channel_id=1, source_target_pairs={{0,2},{1,3},{2,0},{3,1},{4,6},{5,7},{6,4},{7,5},{8,10},{9,11},{10,... | collective-permute-start | bytes 786440 | tf_op jit(solution)/shard_map/z1_qi/ppermute | solution.py:218
  35.3 16.6 %collective-permute-start.7 = (f32[1,64,512]{2,1,0:T(8,128)S(1)}, f32[1,64,512]{2,1,0:T(8,128)S(1)}, u32[]{:S(2)}, u32[]{:S(2)}) collective-permute-start(f32[1,64,512]{2,1,0:T(8,128)S(1)} %get-tuple-element.130), channel_id=1, source_target_pairs={{0,4},{1,5},{2,6},{3,7},{4,0},{5,1},{6,2},{7,3},{8,12},{9,13},{10,... | collective-permute-start | bytes 393224 | tf_op jit(solution)/shard_map/z2_qo/ppermute | solution.py:218
  38.0 14.0 %collective-permute-start.4 = (f32[2,64,512]{2,1,0:T(8,128)S(1)}, f32[2,64,512]{2,1,0:T(8,128)S(1)}, u32[]{:S(2)}, u32[]{:S(2)}) collective-permute-start(f32[2,64,512]{2,1,0:T(8,128)S(1)} %slice_add_fusion.3), channel_id=1, source_target_pairs={{0,1},{1,0},{2,3},{3,2},{4,5},{5,4},{6,7},{7,6},{8,9},{9,8},{10,11... | collective-permute-start | bytes 786440 | tf_op jit(solution)/shard_map/x_to/ppermute | solution.py:218
  39.2 15.5 %copy-start = (s32[4096]{0:T(1024)S(1)}, s32[4096]{0:T(1024)}, u32[]{:S(2)}) copy-start(s32[4096]{0:T(1024)} %param.15) | copy-start | bytes 49156
  39.2 28.0 %copy-start.1 = (s32[4096]{0:T(1024)S(1)}, s32[4096]{0:T(1024)}, u32[]{:S(2)}) copy-start(s32[4096]{0:T(1024)} %param.14) | copy-start | bytes 49156
  43.4 11.3 %collective-permute-start.9 = (f32[1,64,512]{2,1,0:T(8,128)S(1)}, f32[1,64,512]{2,1,0:T(8,128)S(1)}, u32[]{:S(2)}, u32[]{:S(2)}) collective-permute-start(f32[1,64,512]{2,1,0:T(8,128)S(1)} %fusion), channel_id=1, source_target_pairs={{0,4},{1,5},{2,6},{3,7},{4,0},{5,1},{6,2},{7,3},{8,12},{9,13},{10,... | collective-permute-start | bytes 393224 | tf_op jit(solution)/shard_map/z2_qi/ppermute | solution.py:218
  45.8 8.9 %collective-permute-start.8 = (f32[2,64,512]{2,1,0:T(8,128)S(1)}, f32[2,64,512]{2,1,0:T(8,128)S(1)}, u32[]{:S(2)}, u32[]{:S(2)}) collective-permute-start(f32[2,64,512]{2,1,0:T(8,128)S(1)} %slice_add_fusion.2), channel_id=1, source_target_pairs={{0,2},{1,3},{2,0},{3,1},{4,6},{5,7},{6,4},{7,5},{8,10},{9,11},{10,... | collective-permute-start | bytes 786440 | tf_op jit(solution)/shard_map/z1_ti/ppermute | solution.py:218
  52.0 11.9 %collective-permute-start.11 = (f32[1,64,512]{2,1,0:T(8,128)S(1)}, f32[1,64,512]{2,1,0:T(8,128)S(1)}, u32[]{:S(2)}, u32[]{:S(2)}) collective-permute-start(f32[1,64,512]{2,1,0:T(8,128)S(1)} %slice_add_fusion.8), channel_id=1, source_target_pairs={{0,4},{1,5},{2,6},{3,7},{4,0},{5,1},{6,2},{7,3},{8,12},{9,13},{10,... | collective-permute-start | bytes 393224 | tf_op jit(solution)/shard_map/z2_to/ppermute | solution.py:218
  55.9 11.2 %collective-permute-start.10 = (f32[1,64,512]{2,1,0:T(8,128)S(1)}, f32[1,64,512]{2,1,0:T(8,128)S(1)}, u32[]{:S(2)}, u32[]{:S(2)}) collective-permute-start(f32[1,64,512]{2,1,0:T(8,128)S(1)} %slice_add_fusion.6), channel_id=1, source_target_pairs={{0,4},{1,5},{2,6},{3,7},{4,0},{5,1},{6,2},{7,3},{8,12},{9,13},{10,... | collective-permute-start | bytes 393224 | tf_op jit(solution)/shard_map/z2_ti/ppermute | solution.py:218
  58.3 5.6 %collective-permute-start.12 = (f32[8,8,128]{2,1,0:T(8,128)S(1)}, f32[8,8,128]{2,1,0:T(8,128)S(1)}, u32[]{:S(2)}, u32[]{:S(2)}) collective-permute-start(f32[8,8,128]{2,1,0:T(8,128)S(1)} %get-tuple-element.111), channel_id=1, source_target_pairs={{0,2},{1,3},{2,0},{3,1},{4,6},{5,7},{6,4},{7,5},{8,10},{9,11},{10,... | collective-permute-start | bytes 98312 | tf_op jit(solution)/shard_map/z_query/ppermute | solution.py:218
  60.7 6.4 %collective-permute-start.13 = (f32[8,8,128]{2,1,0:T(8,128)S(1)}, f32[8,8,128]{2,1,0:T(8,128)S(1)}, u32[]{:S(2)}, u32[]{:S(2)}) collective-permute-start(f32[8,8,128]{2,1,0:T(8,128)S(1)} %get-tuple-element.112), channel_id=1, source_target_pairs={{0,4},{1,5},{2,6},{3,7},{4,0},{5,1},{6,2},{7,3},{8,12},{9,13},{10,... | collective-permute-start | bytes 98312 | tf_op jit(solution)/shard_map/z_query/ppermute | solution.py:218
  61.1 6.0 %collective-permute-start.14 = (f32[8,8,128]{2,1,0:T(8,128)S(1)}, f32[8,8,128]{2,1,0:T(8,128)S(1)}, u32[]{:S(2)}, u32[]{:S(2)}) collective-permute-start(f32[8,8,128]{2,1,0:T(8,128)S(1)} %get-tuple-element.113), channel_id=1, source_target_pairs={{0,6},{1,7},{2,4},{3,5},{4,2},{5,3},{6,0},{7,1},{8,14},{9,15},{10,... | collective-permute-start | bytes 98312 | tf_op jit(solution)/shard_map/z_query/ppermute | solution.py:218
  67.2 1.4 %collective-permute-start.18 = (f32[4,8,8,128]{3,2,1,0:T(8,128)S(1)}, f32[4,8,8,128]{3,2,1,0:T(8,128)S(1)}, u32[]{:S(2)}, u32[]{:S(2)}) collective-permute-start(f32[4,8,8,128]{3,2,1,0:T(8,128)S(1)} %pad_maximum_fusion), channel_id=1, source_target_pairs={{0,8},{8,0},{1,9},{9,1},{2,10},{10,2},{3,11},{11,3},{4,12},{12,4},... | collective-permute-start | bytes 393224 | tf_op jit(solution)/shard_map/dp_query/ppermute | solution.py:223
  68.6 9.9 %collective-permute-start.19 = (f32[8,8,8,128]{3,2,1,0:T(8,128)S(1)}, f32[8,8,8,128]{3,2,1,0:T(8,128)S(1)}, u32[]{:S(2)}, u32[]{:S(2)}) collective-permute-start(f32[8,8,8,128]{3,2,1,0:T(8,128)S(1)} %constant_dynamic-update-slice_fusion.refs_4_), channel_id=1, source_target_pairs={{0,1},{1,0},{2,3},{3,2},{4,5},{5,4},{6,7},{7,6},{8,9},{9,8},{10,11... | collective-permute-start | bytes 786440 | tf_op jit(solution)/shard_map/x_query/ppermute | solution.py:218
  70.3 4.4 %collective-permute-start.15 = (f32[8,8,128]{2,1,0:T(8,128)S(1)}, f32[8,8,128]{2,1,0:T(8,128)S(1)}, u32[]{:S(2)}, u32[]{:S(2)}) collective-permute-start(f32[8,8,128]{2,1,0:T(8,128)S(1)} %get-tuple-element.121), channel_id=1, source_target_pairs={{0,2},{1,3},{2,0},{3,1},{4,6},{5,7},{6,4},{7,5},{8,10},{9,11},{10,... | collective-permute-start | bytes 98312 | tf_op jit(solution)/shard_map/z_train/ppermute | solution.py:218
  71.2 4.9 %collective-permute-start.16 = (f32[8,8,128]{2,1,0:T(8,128)S(1)}, f32[8,8,128]{2,1,0:T(8,128)S(1)}, u32[]{:S(2)}, u32[]{:S(2)}) collective-permute-start(f32[8,8,128]{2,1,0:T(8,128)S(1)} %get-tuple-element.122), channel_id=1, source_target_pairs={{0,4},{1,5},{2,6},{3,7},{4,0},{5,1},{6,2},{7,3},{8,12},{9,13},{10,... | collective-permute-start | bytes 98312 | tf_op jit(solution)/shard_map/z_train/ppermute | solution.py:218
  72.8 5.7 %collective-permute-start.17 = (f32[8,8,128]{2,1,0:T(8,128)S(1)}, f32[8,8,128]{2,1,0:T(8,128)S(1)}, u32[]{:S(2)}, u32[]{:S(2)}) collective-permute-start(f32[8,8,128]{2,1,0:T(8,128)S(1)} %get-tuple-element.123), channel_id=1, source_target_pairs={{0,6},{1,7},{2,4},{3,5},{4,2},{5,3},{6,0},{7,1},{8,14},{9,15},{10,... | collective-permute-start | bytes 98312 | tf_op jit(solution)/shard_map/z_train/ppermute | solution.py:218
  79.4 4.9 %collective-permute-start.20 = (f32[64,128]{1,0:T(8,128)S(1)}, f32[64,128]{1,0:T(8,128)S(1)}, u32[]{:S(2)}, u32[]{:S(2)}) collective-permute-start(f32[64,128]{1,0:T(8,128)S(1)} %partial_scores.1), channel_id=1, source_target_pairs={{0,4},{1,5},{2,6},{3,7},{4,0},{5,1},{6,2},{7,3},{8,12},{9,13},{10,... | collective-permute-start | bytes 98312 | tf_op jit(solution)/shard_map/scores/ppermute | solution.py:218
  84.3 3.9 %collective-permute-start.21 = (f32[64,128]{1,0:T(8,128)S(1)}, f32[64,128]{1,0:T(8,128)S(1)}, u32[]{:S(2)}, u32[]{:S(2)}) collective-permute-start(f32[64,128]{1,0:T(8,128)S(1)} %add.95), channel_id=1, source_target_pairs={{0,2},{1,3},{2,0},{3,1},{4,6},{5,7},{6,4},{7,5},{8,10},{9,11},{10,... | collective-permute-start | bytes 98312 | tf_op jit(solution)/shard_map/scores/ppermute | solution.py:218
  88.2 3.9 %collective-permute-start.22 = (f32[64,128]{1,0:T(8,128)S(1)}, f32[64,128]{1,0:T(8,128)S(1)}, u32[]{:S(2)}, u32[]{:S(2)}) collective-permute-start(f32[64,128]{1,0:T(8,128)S(1)} %add.96), channel_id=1, source_target_pairs={{0,1},{1,0},{2,3},{3,2},{4,5},{5,4},{6,7},{7,6},{8,9},{9,8},{10,11... | collective-permute-start | bytes 98312 | tf_op jit(solution)/shard_map/scores/ppermute | solution.py:218

commit v7 on v6

--- a/solution.py
+++ b/solution.py
@@ -297,7 +297,7 @@
     trains = [train[0]] + [swap(train[k], 2 * k, "z_train") for k in (3, 2, 1)][::-1]
     queries = [query, other]
     scores = partial_scores(place, trains, queries)
-    for mask in (Z2, Z1, X):
+    for mask in (X, Z1, Z2):
         scores = scores + swap(scores, mask, "scores")
     return scores
 

time: 92.9 us -> 93.1 us (level)
  no operation moved by 1% of the time
where the time goes in v7:
time: 93.1 us; the launch traced here: 93 us
  Pallas kernels  37.5 us (40%)
  starting transfers between devices  34.4 us (37%)
  waiting for transfers between devices  19.6 us (21%)
  other arithmetic  1.13 us (1%)
    ppermute x22, starting transfers between devices, swap(): return lax.ppermute(value, 'tensor', [(i, i ^ mask) for i in range(8)])  34.3 us
    pallas_call x6, Pallas kernels, project(): pl.pallas_call(kernel, out_shape=[pltpu.VMEM((len(masks), RANK, BLK), jnp...  34.3 us
    ppermute x22, waiting for transfers between devices, swap(): return lax.ppermute(value, 'tensor', [(i, i ^ mask) for i in range(8)])  19.5 us
    pallas_call x2, Pallas kernels, examples(): pl.pallas_call(kernel, out_shape=[pltpu.VMEM((HALF // 4, SEGS, 2 * RANK),...  2.29 us
  transfers between devices with their start and end apart: 23, of which 9 were waited for; matrix products, arithmetic and copies ran while one was open for 1% of the time, Pallas kernels for 36%

profile of v7, /device:TPU:0, one launch (start us, length us, event | category | flops | bytes accessed | tf_op | source)
XLA Modules:
  0.0 93.0 jit_solution(10484078125451777739)
XLA Ops:
  0.0 3.1 %first_query_out.1 = f32[4,64,512]{2,1,0:T(8,128)S(1)} custom-call(s32[1]{0:T(128)} %bitcast.1.me_ref, bf16[64,1024]{1,0:T(8,128)(2,1)} %refs_1_.9, bf16[1024,4096]{1,0:T(8,128)(2,1)} %refs_3_.4), custom_call_target="tpu_custom_call" | custom-call | flops 268435456 | bytes 4194304 | tf_op jit(solution)/shard_map/first_query_out/pallas_call | solution.py:109
  3.1 3.1 %collective-permute-start = (f32[4,64,512]{2,1,0:T(8,128)S(1)}, f32[4,64,512]{2,1,0:T(8,128)S(1)}, u32[]{:S(2)}, u32[]{:S(2)}) collective-permute-start(f32[4,64,512]{2,1,0:T(8,128)S(1)} %first_query_out.1), channel_id=1, source_target_pairs={{0,2},{1,3},{2,0},{3,1},{4,6},{5,7},{6,4},{7,5},{8,10},{9,11},{10,... | collective-permute-start | bytes 1572872 | tf_op jit(solution)/shard_map/z1_qo/ppermute | solution.py:218
  6.2 7.7 %first_query_in.1 = (f32[4,64,512]{2,1,0:T(8,128)S(1)}, f32[4,64,512]{2,1,0:T(8,128)S(1)}) custom-call(s32[1]{0:T(128)} %bitcast.1.me_ref, bf16[64,3584]{1,0:T(8,128)(2,1)} %refs_0_.11, bf16[64,1024]{1,0:T(8,128)(2,1)} %refs_1_.9, bf16[3584,4096]{1,0:T(8,128)(2,1)} %refs_2_.5, bf16[1024,4096]{1,0:T(8,128)(2,1)} %refs_3_.5), custom_call_target="tpu_custom_call" | custom-call | flops 1207959552 | bytes 18874368 | tf_op jit(solution)/shard_map/first_query_in/pallas_call | solution.py:109
  13.9 0.1 collective-permute-start.1
  14.0 1.9 %collective-permute-start.3 = (f32[4,64,512]{2,1,0:T(8,128)S(1)}, f32[4,64,512]{2,1,0:T(8,128)S(1)}, u32[]{:S(2)}, u32[]{:S(2)}) collective-permute-start(f32[4,64,512]{2,1,0:T(8,128)S(1)} %get-tuple-element.68), channel_id=1, source_target_pairs={{0,1},{1,0},{2,3},{3,2},{4,5},{5,4},{6,7},{7,6},{8,9},{9,8},{10,11... | collective-permute-start | bytes 1572872 | tf_op jit(solution)/shard_map/x_qi/ppermute | solution.py:218
  15.9 0.1 pad_add_fusion.place_ref
  16.0 7.7 %middle_a.1 = (f32[4,64,512]{2,1,0:T(8,128)S(1)}, f32[4,64,512]{2,1,0:T(8,128)S(1)}) custom-call(s32[1]{0:T(128)} %bitcast.1.me_ref, bf16[64,3584]{1,0:T(8,128)(2,1)} %refs_0_.11, bf16[64,1024]{1,0:T(8,128)(2,1)} %refs_1_.9, bf16[3584,4096]{1,0:T(8,128)(2,1)} %refs_1_.11, bf16[1024,4096]{1,0:T(8,128)(2,1)} %refs_3_.4), custom_call_target="tpu_custom_call" | custom-call | flops 1207959552 | bytes 18874368 | tf_op jit(solution)/shard_map/middle_a/pallas_call | solution.py:109
  23.7 0.0 collective-permute-done
  23.7 0.2 collective-permute-start.2
  23.9 1.9 %collective-permute-start.6 = (f32[4,64,512]{2,1,0:T(8,128)S(1)}, f32[4,64,512]{2,1,0:T(8,128)S(1)}, u32[]{:S(2)}, u32[]{:S(2)}) collective-permute-start(f32[4,64,512]{2,1,0:T(8,128)S(1)} %get-tuple-element.72), channel_id=1, source_target_pairs={{0,1},{1,0},{2,3},{3,2},{4,5},{5,4},{6,7},{7,6},{8,9},{9,8},{10,11... | collective-permute-start | bytes 1572872 | tf_op jit(solution)/shard_map/x_ti/ppermute | solution.py:218
  25.8 7.7 %middle_b.1 = (f32[4,64,512]{2,1,0:T(8,128)S(1)}, f32[4,64,512]{2,1,0:T(8,128)S(1)}) custom-call(s32[1]{0:T(128)} %bitcast.1.me_ref, bf16[64,3584]{1,0:T(8,128)(2,1)} %refs_0_.11, bf16[64,1024]{1,0:T(8,128)(2,1)} %refs_1_.9, bf16[3584,4096]{1,0:T(8,128)(2,1)} %refs_2_.5, bf16[1024,4096]{1,0:T(8,128)(2,1)} %refs_3_.5), custom_call_target="tpu_custom_call" | custom-call | flops 1207959552 | bytes 18874368 | tf_op jit(solution)/shard_map/middle_b/pallas_call | solution.py:109
  33.5 1.6 %collective-permute-start.5 = (f32[2,64,512]{2,1,0:T(8,128)S(1)}, f32[2,64,512]{2,1,0:T(8,128)S(1)}, u32[]{:S(2)}, u32[]{:S(2)}) collective-permute-start(f32[2,64,512]{2,1,0:T(8,128)S(1)} %slice_add_fusion), channel_id=1, source_target_pairs={{0,2},{1,3},{2,0},{3,1},{4,6},{5,7},{6,4},{7,5},{8,10},{9,11},{10,... | collective-permute-start | bytes 786440 | tf_op jit(solution)/shard_map/z1_qi/ppermute | solution.py:218
  35.2 0.1 slice_add_fusion.10
  35.3 2.7 %collective-permute-start.7 = (f32[1,64,512]{2,1,0:T(8,128)S(1)}, f32[1,64,512]{2,1,0:T(8,128)S(1)}, u32[]{:S(2)}, u32[]{:S(2)}) collective-permute-start(f32[1,64,512]{2,1,0:T(8,128)S(1)} %get-tuple-element.130), channel_id=1, source_target_pairs={{0,4},{1,5},{2,6},{3,7},{4,0},{5,1},{6,2},{7,3},{8,12},{9,13},{10,... | collective-permute-start | bytes 393224 | tf_op jit(solution)/shard_map/z2_qo/ppermute | solution.py:218
  38.0 1.2 %collective-permute-start.4 = (f32[2,64,512]{2,1,0:T(8,128)S(1)}, f32[2,64,512]{2,1,0:T(8,128)S(1)}, u32[]{:S(2)}, u32[]{:S(2)}) collective-permute-start(f32[2,64,512]{2,1,0:T(8,128)S(1)} %slice_add_fusion.3), channel_id=1, source_target_pairs={{0,1},{1,0},{2,3},{3,2},{4,5},{5,4},{6,7},{7,6},{8,9},{9,8},{10,11... | collective-permute-start | bytes 786440 | tf_op jit(solution)/shard_map/x_to/ppermute | solution.py:218
  39.2 4.1 %last_train_in_a.1 = f32[2,64,512]{2,1,0:T(8,128)S(1)} custom-call(s32[1]{0:T(128)} %bitcast.1.me_ref, bf16[64,3584]{1,0:T(8,128)(2,1)} %refs_0_.11, bf16[3584,4096]{1,0:T(8,128)(2,1)} %refs_1_.11), custom_call_target="tpu_custom_call" | custom-call | flops 469762048 | bytes 7340032 | tf_op jit(solution)/shard_map/last_train_in_a/pallas_call | solution.py:109
  43.4 1.5 %collective-permute-start.9 = (f32[1,64,512]{2,1,0:T(8,128)S(1)}, f32[1,64,512]{2,1,0:T(8,128)S(1)}, u32[]{:S(2)}, u32[]{:S(2)}) collective-permute-start(f32[1,64,512]{2,1,0:T(8,128)S(1)} %fusion), channel_id=1, source_target_pairs={{0,4},{1,5},{2,6},{3,7},{4,0},{5,1},{6,2},{7,3},{8,12},{9,13},{10,... | collective-permute-start | bytes 393224 | tf_op jit(solution)/shard_map/z2_qi/ppermute | solution.py:218
  44.8 0.9 collective-permute-done.6
  45.8 2.0 %collective-permute-start.8 = (f32[2,64,512]{2,1,0:T(8,128)S(1)}, f32[2,64,512]{2,1,0:T(8,128)S(1)}, u32[]{:S(2)}, u32[]{:S(2)}) collective-permute-start(f32[2,64,512]{2,1,0:T(8,128)S(1)} %slice_add_fusion.2), channel_id=1, source_target_pairs={{0,2},{1,3},{2,0},{3,1},{4,6},{5,7},{6,4},{7,5},{8,10},{9,11},{10,... | collective-permute-start | bytes 786440 | tf_op jit(solution)/shard_map/z1_ti/ppermute | solution.py:218
  47.8 4.1 %last_train_in_b.1 = f32[2,64,512]{2,1,0:T(8,128)S(1)} custom-call(s32[1]{0:T(128)} %bitcast.1.me_ref, bf16[64,3584]{1,0:T(8,128)(2,1)} %refs_0_.11, bf16[3584,4096]{1,0:T(8,128)(2,1)} %refs_1_.11), custom_call_target="tpu_custom_call" | custom-call | flops 469762048 | bytes 7340032 | tf_op jit(solution)/shard_map/last_train_in_b/pallas_call | solution.py:109
  51.9 0.0 collective-permute-done.7.refs_1_
  52.0 2.7 %collective-permute-start.11 = (f32[1,64,512]{2,1,0:T(8,128)S(1)}, f32[1,64,512]{2,1,0:T(8,128)S(1)}, u32[]{:S(2)}, u32[]{:S(2)}) collective-permute-start(f32[1,64,512]{2,1,0:T(8,128)S(1)} %slice_add_fusion.8), channel_id=1, source_target_pairs={{0,4},{1,5},{2,6},{3,7},{4,0},{5,1},{6,2},{7,3},{8,12},{9,13},{10,... | collective-permute-start | bytes 393224 | tf_op jit(solution)/shard_map/z2_to/ppermute | solution.py:218
  54.6 0.0 collective-permute-done.8
  54.7 0.0 collective-permute-done.9.refs_3_
  54.7 1.1 %examples.2 = (f32[8,8,128]{2,1,0:T(8,128)S(1)}, f32[8,8,128]{2,1,0:T(8,128)S(1)}, f32[8,8,128]{2,1,0:T(8,128)S(1)}, f32[8,8,128]{2,1,0:T(8,128)S(1)}) custom-call(s32[4]{0:T(128)S(1)} %pad_add_fusion.place_ref, f32[1,64,512]{2,1,0:T(8,128)S(1)} %get-tuple-element.129.refs_0_, f32[1,64,512]{2,1,0:T(8,128)S(1)} %collective-permute-done.7.refs_1_, ...), custom_call_target="tpu_custom_call" | custom-call | flops 1 | bytes 1 | tf_op jit(solution)/shard_map/examples/pallas_call | solution.py:172
  55.9 2.4 %collective-permute-start.10 = (f32[1,64,512]{2,1,0:T(8,128)S(1)}, f32[1,64,512]{2,1,0:T(8,128)S(1)}, u32[]{:S(2)}, u32[]{:S(2)}) collective-permute-start(f32[1,64,512]{2,1,0:T(8,128)S(1)} %slice_add_fusion.6), channel_id=1, source_target_pairs={{0,4},{1,5},{2,6},{3,7},{4,0},{5,1},{6,2},{7,3},{8,12},{9,13},{10,... | collective-permute-start | bytes 393224 | tf_op jit(solution)/shard_map/z2_ti/ppermute | solution.py:218
  58.3 2.4 %collective-permute-start.12 = (f32[8,8,128]{2,1,0:T(8,128)S(1)}, f32[8,8,128]{2,1,0:T(8,128)S(1)}, u32[]{:S(2)}, u32[]{:S(2)}) collective-permute-start(f32[8,8,128]{2,1,0:T(8,128)S(1)} %get-tuple-element.111), channel_id=1, source_target_pairs={{0,2},{1,3},{2,0},{3,1},{4,6},{5,7},{6,4},{7,5},{8,10},{9,11},{10,... | collective-permute-start | bytes 98312 | tf_op jit(solution)/shard_map/z_query/ppermute | solution.py:218
  60.7 0.4 collective-permute-start.13
  61.1 2.0 %collective-permute-start.14 = (f32[8,8,128]{2,1,0:T(8,128)S(1)}, f32[8,8,128]{2,1,0:T(8,128)S(1)}, u32[]{:S(2)}, u32[]{:S(2)}) collective-permute-start(f32[8,8,128]{2,1,0:T(8,128)S(1)} %get-tuple-element.113), channel_id=1, source_target_pairs={{0,6},{1,7},{2,4},{3,5},{4,2},{5,3},{6,0},{7,1},{8,14},{9,15},{10,... | collective-permute-start | bytes 98312 | tf_op jit(solution)/shard_map/z_query/ppermute | solution.py:218
  63.1 0.8 collective-permute-done.11.refs_1_
  63.9 3.2 %collective-permute-done.13 = f32[8,8,128]{2,1,0:T(8,128)S(1)} collective-permute-done((f32[8,8,128]{2,1,0:T(8,128)S(1)}, f32[8,8,128]{2,1,0:T(8,128)S(1)}, u32[]{:S(2)}, u32[]{:S(2)}) %collective-permute-start.13) | collective-permute-done | bytes 32800 | tf_op jit(solution)/shard_map/z_query/ppermute | solution.py:218
  67.1 0.0 collective-permute-done.14
  67.2 0.1 collective-permute-start.18
  67.3 1.1 %examples.3 = (f32[8,8,128]{2,1,0:T(8,128)S(1)}, f32[8,8,128]{2,1,0:T(8,128)S(1)}, f32[8,8,128]{2,1,0:T(8,128)S(1)}, f32[8,8,128]{2,1,0:T(8,128)S(1)}) custom-call(s32[4]{0:T(128)S(1)} %pad_add_fusion.place_ref, f32[1,64,512]{2,1,0:T(8,128)S(1)} %slice_add_fusion.7.refs_0_, f32[1,64,512]{2,1,0:T(8,128)S(1)} %collective-permute-done.11.refs_1_, ...), custom_call_target="tpu_custom_call" | custom-call | flops 1 | bytes 1 | tf_op jit(solution)/shard_map/examples/pallas_call | solution.py:172
  68.4 0.1 collective-permute-done.18
  68.6 1.7 %collective-permute-start.19 = (f32[8,8,8,128]{3,2,1,0:T(8,128)S(1)}, f32[8,8,8,128]{3,2,1,0:T(8,128)S(1)}, u32[]{:S(2)}, u32[]{:S(2)}) collective-permute-start(f32[8,8,8,128]{3,2,1,0:T(8,128)S(1)} %constant_dynamic-update-slice_fusion.refs_4_), channel_id=1, source_target_pairs={{0,1},{1,0},{2,3},{3,2},{4,5},{5,4},{6,7},{7,6},{8,9},{9,8},{10,11... | collective-permute-start | bytes 786440 | tf_op jit(solution)/shard_map/x_query/ppermute | solution.py:218
  70.3 0.9 collective-permute-start.15
  71.2 1.6 %collective-permute-start.16 = (f32[8,8,128]{2,1,0:T(8,128)S(1)}, f32[8,8,128]{2,1,0:T(8,128)S(1)}, u32[]{:S(2)}, u32[]{:S(2)}) collective-permute-start(f32[8,8,128]{2,1,0:T(8,128)S(1)} %get-tuple-element.122), channel_id=1, source_target_pairs={{0,4},{1,5},{2,6},{3,7},{4,0},{5,1},{6,2},{7,3},{8,12},{9,13},{10,... | collective-permute-start | bytes 98312 | tf_op jit(solution)/shard_map/z_train/ppermute | solution.py:218
  72.8 1.9 %collective-permute-start.17 = (f32[8,8,128]{2,1,0:T(8,128)S(1)}, f32[8,8,128]{2,1,0:T(8,128)S(1)}, u32[]{:S(2)}, u32[]{:S(2)}) collective-permute-start(f32[8,8,128]{2,1,0:T(8,128)S(1)} %get-tuple-element.123), channel_id=1, source_target_pairs={{0,6},{1,7},{2,4},{3,5},{4,2},{5,3},{6,0},{7,1},{8,14},{9,15},{10,... | collective-permute-start | bytes 98312 | tf_op jit(solution)/shard_map/z_train/ppermute | solution.py:218
  74.7 1.4 %collective-permute-done.16.refs_2_ = f32[8,8,128]{2,1,0:T(8,128)S(1)} collective-permute-done((f32[8,8,128]{2,1,0:T(8,128)S(1)}, f32[8,8,128]{2,1,0:T(8,128)S(1)}, u32[]{:S(2)}, u32[]{:S(2)}) %collective-permute-start.16) | collective-permute-done | bytes 32800 | tf_op jit(solution)/shard_map/z_train/ppermute | solution.py:218
  76.1 2.4 %collective-permute-done.17.refs_3_ = f32[8,8,128]{2,1,0:T(8,128)S(1)} collective-permute-done((f32[8,8,128]{2,1,0:T(8,128)S(1)}, f32[8,8,128]{2,1,0:T(8,128)S(1)}, u32[]{:S(2)}, u32[]{:S(2)}) %collective-permute-start.17) | collective-permute-done | bytes 32800 | tf_op jit(solution)/shard_map/z_train/ppermute | solution.py:218
  78.5 0.9 partial_scores.1
  79.4 1.3 %collective-permute-start.20 = (f32[64,128]{1,0:T(8,128)S(1)}, f32[64,128]{1,0:T(8,128)S(1)}, u32[]{:S(2)}, u32[]{:S(2)}) collective-permute-start(f32[64,128]{1,0:T(8,128)S(1)} %partial_scores.1), channel_id=1, source_target_pairs={{0,1},{1,0},{2,3},{3,2},{4,5},{5,4},{6,7},{7,6},{8,9},{9,8},{10,11... | collective-permute-start | bytes 98312 | tf_op jit(solution)/shard_map/scores/ppermute | solution.py:218
  80.7 2.7 %collective-permute-done.20 = f32[64,128]{1,0:T(8,128)S(1)} collective-permute-done((f32[64,128]{1,0:T(8,128)S(1)}, f32[64,128]{1,0:T(8,128)S(1)}, u32[]{:S(2)}, u32[]{:S(2)}) %collective-permute-start.20) | collective-permute-done | bytes 32800 | tf_op jit(solution)/shard_map/scores/ppermute | solution.py:218
  83.4 4.1 %collective-permute-done.21 = f32[64,128]{1,0:T(8,128)S(1)} collective-permute-done((f32[64,128]{1,0:T(8,128)S(1)}, f32[64,128]{1,0:T(8,128)S(1)}, u32[]{:S(2)}, u32[]{:S(2)}) %collective-permute-start.21) | collective-permute-done | bytes 32800 | tf_op jit(solution)/shard_map/scores/ppermute | solution.py:218
  87.5 0.9 collective-permute-start.22
  88.4 4.0 %collective-permute-done.22 = f32[64,128]{1,0:T(8,128)S(1)} collective-permute-done((f32[64,128]{1,0:T(8,128)S(1)}, f32[64,128]{1,0:T(8,128)S(1)}, u32[]{:S(2)}, u32[]{:S(2)}) %collective-permute-start.22) | collective-permute-done | bytes 32800 | tf_op jit(solution)/shard_map/scores/ppermute | solution.py:218
  92.3 0.6 add.97
  (32 shorter events, 0.4 us)
Async XLA Ops:
  3.1 20.5 %collective-permute-start = (f32[4,64,512]{2,1,0:T(8,128)S(1)}, f32[4,64,512]{2,1,0:T(8,128)S(1)}, u32[]{:S(2)}, u32[]{:S(2)}) collective-permute-start(f32[4,64,512]{2,1,0:T(8,128)S(1)} %first_query_out.1), channel_id=1, source_target_pairs={{0,2},{1,3},{2,0},{3,1},{4,6},{5,7},{6,4},{7,5},{8,10},{9,11},{10,... | collective-permute-start | bytes 1572872 | tf_op jit(solution)/shard_map/z1_qo/ppermute | solution.py:218
  13.9 24.0 %collective-permute-start.1 = (f32[4,64,512]{2,1,0:T(8,128)S(1)}, f32[4,64,512]{2,1,0:T(8,128)S(1)}, u32[]{:S(2)}, u32[]{:S(2)}) collective-permute-start(f32[4,64,512]{2,1,0:T(8,128)S(1)} %get-tuple-element.75), channel_id=1, source_target_pairs={{0,2},{1,3},{2,0},{3,1},{4,6},{5,7},{6,4},{7,5},{8,10},{9,11},{10,... | collective-permute-start | bytes 1572872 | tf_op jit(solution)/shard_map/z1_to/ppermute | solution.py:218
  14.0 19.5 %collective-permute-start.3 = (f32[4,64,512]{2,1,0:T(8,128)S(1)}, f32[4,64,512]{2,1,0:T(8,128)S(1)}, u32[]{:S(2)}, u32[]{:S(2)}) collective-permute-start(f32[4,64,512]{2,1,0:T(8,128)S(1)} %get-tuple-element.68), channel_id=1, source_target_pairs={{0,1},{1,0},{2,3},{3,2},{4,5},{5,4},{6,7},{7,6},{8,9},{9,8},{10,11... | collective-permute-start | bytes 1572872 | tf_op jit(solution)/shard_map/x_qi/ppermute | solution.py:218
  23.7 11.5 %collective-permute-start.2 = (f32[2,64,512]{2,1,0:T(8,128)S(1)}, f32[2,64,512]{2,1,0:T(8,128)S(1)}, u32[]{:S(2)}, u32[]{:S(2)}) collective-permute-start(f32[2,64,512]{2,1,0:T(8,128)S(1)} %slice_add_fusion.1), channel_id=1, source_target_pairs={{0,1},{1,0},{2,3},{3,2},{4,5},{5,4},{6,7},{7,6},{8,9},{9,8},{10,11... | collective-permute-start | bytes 786440 | tf_op jit(solution)/shard_map/x_qo/ppermute | solution.py:218
  23.9 21.8 %collective-permute-start.6 = (f32[4,64,512]{2,1,0:T(8,128)S(1)}, f32[4,64,512]{2,1,0:T(8,128)S(1)}, u32[]{:S(2)}, u32[]{:S(2)}) collective-permute-start(f32[4,64,512]{2,1,0:T(8,128)S(1)} %get-tuple-element.72), channel_id=1, source_target_pairs={{0,1},{1,0},{2,3},{3,2},{4,5},{5,4},{6,7},{7,6},{8,9},{9,8},{10,11... | collective-permute-start | bytes 1572872 | tf_op jit(solution)/shard_map/x_ti/ppermute | solution.py:218
  33.5 9.8 %collective-permute-start.5 = (f32[2,64,512]{2,1,0:T(8,128)S(1)}, f32[2,64,512]{2,1,0:T(8,128)S(1)}, u32[]{:S(2)}, u32[]{:S(2)}) collective-permute-start(f32[2,64,512]{2,1,0:T(8,128)S(1)} %slice_add_fusion), channel_id=1, source_target_pairs={{0,2},{1,3},{2,0},{3,1},{4,6},{5,7},{6,4},{7,5},{8,10},{9,11},{10,... | collective-permute-start | bytes 786440 | tf_op jit(solution)/shard_map/z1_qi/ppermute | solution.py:218
  35.3 16.6 %collective-permute-start.7 = (f32[1,64,512]{2,1,0:T(8,128)S(1)}, f32[1,64,512]{2,1,0:T(8,128)S(1)}, u32[]{:S(2)}, u32[]{:S(2)}) collective-permute-start(f32[1,64,512]{2,1,0:T(8,128)S(1)} %get-tuple-element.130), channel_id=1, source_target_pairs={{0,4},{1,5},{2,6},{3,7},{4,0},{5,1},{6,2},{7,3},{8,12},{9,13},{10,... | collective-permute-start | bytes 393224 | tf_op jit(solution)/shard_map/z2_qo/ppermute | solution.py:218
  38.0 14.0 %collective-permute-start.4 = (f32[2,64,512]{2,1,0:T(8,128)S(1)}, f32[2,64,512]{2,1,0:T(8,128)S(1)}, u32[]{:S(2)}, u32[]{:S(2)}) collective-permute-start(f32[2,64,512]{2,1,0:T(8,128)S(1)} %slice_add_fusion.3), channel_id=1, source_target_pairs={{0,1},{1,0},{2,3},{3,2},{4,5},{5,4},{6,7},{7,6},{8,9},{9,8},{10,11... | collective-permute-start | bytes 786440 | tf_op jit(solution)/shard_map/x_to/ppermute | solution.py:218
  39.2 15.5 %copy-start = (s32[4096]{0:T(1024)S(1)}, s32[4096]{0:T(1024)}, u32[]{:S(2)}) copy-start(s32[4096]{0:T(1024)} %param.15) | copy-start | bytes 49156
  39.2 28.0 %copy-start.1 = (s32[4096]{0:T(1024)S(1)}, s32[4096]{0:T(1024)}, u32[]{:S(2)}) copy-start(s32[4096]{0:T(1024)} %param.14) | copy-start | bytes 49156
  43.4 11.3 %collective-permute-start.9 = (f32[1,64,512]{2,1,0:T(8,128)S(1)}, f32[1,64,512]{2,1,0:T(8,128)S(1)}, u32[]{:S(2)}, u32[]{:S(2)}) collective-permute-start(f32[1,64,512]{2,1,0:T(8,128)S(1)} %fusion), channel_id=1, source_target_pairs={{0,4},{1,5},{2,6},{3,7},{4,0},{5,1},{6,2},{7,3},{8,12},{9,13},{10,... | collective-permute-start | bytes 393224 | tf_op jit(solution)/shard_map/z2_qi/ppermute | solution.py:218
  45.8 8.9 %collective-permute-start.8 = (f32[2,64,512]{2,1,0:T(8,128)S(1)}, f32[2,64,512]{2,1,0:T(8,128)S(1)}, u32[]{:S(2)}, u32[]{:S(2)}) collective-permute-start(f32[2,64,512]{2,1,0:T(8,128)S(1)} %slice_add_fusion.2), channel_id=1, source_target_pairs={{0,2},{1,3},{2,0},{3,1},{4,6},{5,7},{6,4},{7,5},{8,10},{9,11},{10,... | collective-permute-start | bytes 786440 | tf_op jit(solution)/shard_map/z1_ti/ppermute | solution.py:218
  52.0 11.9 %collective-permute-start.11 = (f32[1,64,512]{2,1,0:T(8,128)S(1)}, f32[1,64,512]{2,1,0:T(8,128)S(1)}, u32[]{:S(2)}, u32[]{:S(2)}) collective-permute-start(f32[1,64,512]{2,1,0:T(8,128)S(1)} %slice_add_fusion.8), channel_id=1, source_target_pairs={{0,4},{1,5},{2,6},{3,7},{4,0},{5,1},{6,2},{7,3},{8,12},{9,13},{10,... | collective-permute-start | bytes 393224 | tf_op jit(solution)/shard_map/z2_to/ppermute | solution.py:218
  55.9 11.2 %collective-permute-start.10 = (f32[1,64,512]{2,1,0:T(8,128)S(1)}, f32[1,64,512]{2,1,0:T(8,128)S(1)}, u32[]{:S(2)}, u32[]{:S(2)}) collective-permute-start(f32[1,64,512]{2,1,0:T(8,128)S(1)} %slice_add_fusion.6), channel_id=1, source_target_pairs={{0,4},{1,5},{2,6},{3,7},{4,0},{5,1},{6,2},{7,3},{8,12},{9,13},{10,... | collective-permute-start | bytes 393224 | tf_op jit(solution)/shard_map/z2_ti/ppermute | solution.py:218
  58.3 5.6 %collective-permute-start.12 = (f32[8,8,128]{2,1,0:T(8,128)S(1)}, f32[8,8,128]{2,1,0:T(8,128)S(1)}, u32[]{:S(2)}, u32[]{:S(2)}) collective-permute-start(f32[8,8,128]{2,1,0:T(8,128)S(1)} %get-tuple-element.111), channel_id=1, source_target_pairs={{0,2},{1,3},{2,0},{3,1},{4,6},{5,7},{6,4},{7,5},{8,10},{9,11},{10,... | collective-permute-start | bytes 98312 | tf_op jit(solution)/shard_map/z_query/ppermute | solution.py:218
  60.7 6.4 %collective-permute-start.13 = (f32[8,8,128]{2,1,0:T(8,128)S(1)}, f32[8,8,128]{2,1,0:T(8,128)S(1)}, u32[]{:S(2)}, u32[]{:S(2)}) collective-permute-start(f32[8,8,128]{2,1,0:T(8,128)S(1)} %get-tuple-element.112), channel_id=1, source_target_pairs={{0,4},{1,5},{2,6},{3,7},{4,0},{5,1},{6,2},{7,3},{8,12},{9,13},{10,... | collective-permute-start | bytes 98312 | tf_op jit(solution)/shard_map/z_query/ppermute | solution.py:218
  61.1 6.0 %collective-permute-start.14 = (f32[8,8,128]{2,1,0:T(8,128)S(1)}, f32[8,8,128]{2,1,0:T(8,128)S(1)}, u32[]{:S(2)}, u32[]{:S(2)}) collective-permute-start(f32[8,8,128]{2,1,0:T(8,128)S(1)} %get-tuple-element.113), channel_id=1, source_target_pairs={{0,6},{1,7},{2,4},{3,5},{4,2},{5,3},{6,0},{7,1},{8,14},{9,15},{10,... | collective-permute-start | bytes 98312 | tf_op jit(solution)/shard_map/z_query/ppermute | solution.py:218
  67.2 1.4 %collective-permute-start.18 = (f32[4,8,8,128]{3,2,1,0:T(8,128)S(1)}, f32[4,8,8,128]{3,2,1,0:T(8,128)S(1)}, u32[]{:S(2)}, u32[]{:S(2)}) collective-permute-start(f32[4,8,8,128]{3,2,1,0:T(8,128)S(1)} %pad_maximum_fusion), channel_id=1, source_target_pairs={{0,8},{8,0},{1,9},{9,1},{2,10},{10,2},{3,11},{11,3},{4,12},{12,4},... | collective-permute-start | bytes 393224 | tf_op jit(solution)/shard_map/dp_query/ppermute | solution.py:223
  68.6 9.9 %collective-permute-start.19 = (f32[8,8,8,128]{3,2,1,0:T(8,128)S(1)}, f32[8,8,8,128]{3,2,1,0:T(8,128)S(1)}, u32[]{:S(2)}, u32[]{:S(2)}) collective-permute-start(f32[8,8,8,128]{3,2,1,0:T(8,128)S(1)} %constant_dynamic-update-slice_fusion.refs_4_), channel_id=1, source_target_pairs={{0,1},{1,0},{2,3},{3,2},{4,5},{5,4},{6,7},{7,6},{8,9},{9,8},{10,11... | collective-permute-start | bytes 786440 | tf_op jit(solution)/shard_map/x_query/ppermute | solution.py:218
  70.3 4.4 %collective-permute-start.15 = (f32[8,8,128]{2,1,0:T(8,128)S(1)}, f32[8,8,128]{2,1,0:T(8,128)S(1)}, u32[]{:S(2)}, u32[]{:S(2)}) collective-permute-start(f32[8,8,128]{2,1,0:T(8,128)S(1)} %get-tuple-element.121), channel_id=1, source_target_pairs={{0,2},{1,3},{2,0},{3,1},{4,6},{5,7},{6,4},{7,5},{8,10},{9,11},{10,... | collective-permute-start | bytes 98312 | tf_op jit(solution)/shard_map/z_train/ppermute | solution.py:218
  71.2 4.9 %collective-permute-start.16 = (f32[8,8,128]{2,1,0:T(8,128)S(1)}, f32[8,8,128]{2,1,0:T(8,128)S(1)}, u32[]{:S(2)}, u32[]{:S(2)}) collective-permute-start(f32[8,8,128]{2,1,0:T(8,128)S(1)} %get-tuple-element.122), channel_id=1, source_target_pairs={{0,4},{1,5},{2,6},{3,7},{4,0},{5,1},{6,2},{7,3},{8,12},{9,13},{10,... | collective-permute-start | bytes 98312 | tf_op jit(solution)/shard_map/z_train/ppermute | solution.py:218
  72.8 5.7 %collective-permute-start.17 = (f32[8,8,128]{2,1,0:T(8,128)S(1)}, f32[8,8,128]{2,1,0:T(8,128)S(1)}, u32[]{:S(2)}, u32[]{:S(2)}) collective-permute-start(f32[8,8,128]{2,1,0:T(8,128)S(1)} %get-tuple-element.123), channel_id=1, source_target_pairs={{0,6},{1,7},{2,4},{3,5},{4,2},{5,3},{6,0},{7,1},{8,14},{9,15},{10,... | collective-permute-start | bytes 98312 | tf_op jit(solution)/shard_map/z_train/ppermute | solution.py:218
  79.4 4.0 %collective-permute-start.20 = (f32[64,128]{1,0:T(8,128)S(1)}, f32[64,128]{1,0:T(8,128)S(1)}, u32[]{:S(2)}, u32[]{:S(2)}) collective-permute-start(f32[64,128]{1,0:T(8,128)S(1)} %partial_scores.1), channel_id=1, source_target_pairs={{0,1},{1,0},{2,3},{3,2},{4,5},{5,4},{6,7},{7,6},{8,9},{9,8},{10,11... | collective-permute-start | bytes 98312 | tf_op jit(solution)/shard_map/scores/ppermute | solution.py:218
  83.4 4.1 %collective-permute-start.21 = (f32[64,128]{1,0:T(8,128)S(1)}, f32[64,128]{1,0:T(8,128)S(1)}, u32[]{:S(2)}, u32[]{:S(2)}) collective-permute-start(f32[64,128]{1,0:T(8,128)S(1)} %add.95), channel_id=1, source_target_pairs={{0,2},{1,3},{2,0},{3,1},{4,6},{5,7},{6,4},{7,5},{8,10},{9,11},{10,... | collective-permute-start | bytes 98312 | tf_op jit(solution)/shard_map/scores/ppermute | solution.py:218
  87.5 4.8 %collective-permute-start.22 = (f32[64,128]{1,0:T(8,128)S(1)}, f32[64,128]{1,0:T(8,128)S(1)}, u32[]{:S(2)}, u32[]{:S(2)}) collective-permute-start(f32[64,128]{1,0:T(8,128)S(1)} %add.96), channel_id=1, source_target_pairs={{0,4},{1,5},{2,6},{3,7},{4,0},{5,1},{6,2},{7,3},{8,12},{9,13},{10,... | collective-permute-start | bytes 98312 | tf_op jit(solution)/shard_map/scores/ppermute | solution.py:218
